TPU v7x, 32 devices: a whole 2x2x4 slice. The times are simulated.
32 devices in a mesh: head: 4 (over y, x), dp: 8 (over z, core).
Axes of the slice: x: 2, y: 2, z: 4, core: 2. Of those that a mesh axis runs over, the one named last changes fastest.
Arguments:
- tokens: bfloat16 [8, 1024, 1024], P('dp', 'head'), may hold values from -6 to 6
- cotangent: bfloat16 [8, 1024, 1024], P('dp', 'head'), may hold values from -6 to 6
- segments: int32 [8, 1024], P('dp'), may hold values from 0 to 15, never falling along the last dimension, each value on 1 to 512 neighbouring positions
- value_expert_route: int32 [8, 1024, 4, 2], P('dp', None, 'head'), may hold values from 0 to 4, all different within a row
- output_expert_route: int32 [8, 1024, 4, 2], P('dp', None, 'head'), may hold values from 0 to 4, all different within a row
- feedforward_route: int32 [8, 1024, 16], P('dp', 'head'), may hold values from 0 to 31, all different within a row; in each aligned block of 256 rows (0 to 255, 256 to 511, ..., all dimensions but the last counted through in order) at most 160 rows name the same one
- attention_norm_gain: float32 [1024], replicated, may hold values from 0.5 to 1.5
- attention_norm_bias: float32 [1024], replicated, may hold values from -2 to 2
- feedforward_norm_gain: float32 [1024], replicated, may hold values from 0.5 to 1.5
- feedforward_norm_bias: float32 [1024], replicated, may hold values from -2 to 2
- query_projection: bfloat16 [1024, 512], P('dp', 'head'), may hold values from -0.1875 to 0.1875
- key_projection: bfloat16 [1024, 512], P('dp', 'head'), may hold values from -0.1875 to 0.1875
- value_selector: bfloat16 [1024, 20], P('dp', 'head'), may hold values from -0.125 to 0.125
- output_selector: bfloat16 [1024, 20], P('dp', 'head'), may hold values from -0.125 to 0.125
- value_experts: bfloat16 [4, 1024, 640], P('head', 'dp'), may hold values from -0.1875 to 0.1875
- output_experts: bfloat16 [4, 640, 1024], P('head', None, 'dp'), may hold values from -1 to 1
- feedforward_selector: bfloat16 [32, 1024], P(('head', 'dp')), may hold values from -0.09375 to 0.09375
- expert_up_weight: bfloat16 [32, 1024, 128], P(('head', 'dp')), may hold values from -0.1875 to 0.1875
- expert_down_weight: bfloat16 [32, 128, 1024], P(('head', 'dp')), may hold values from -0.5 to 0.5
Outputs:
- output: bfloat16 [8, 1024, 1024], P('dp', 'head')
- grad_tokens: bfloat16 [8, 1024, 1024], P('dp', 'head')
- grad_norms: float32 [4, 1024], P(None, ('head', 'dp'))
- grad_query: float32 [1024, 512], P('dp', 'head')
- grad_key: float32 [1024, 512], P('dp', 'head')
- value_selector_grads: float32 [1024, 20], P('dp', 'head')
- grad_osel: float32 [1024, 20], P('dp', 'head')
- grad_value: float32 [4, 1024, 640], P('head', 'dp')
- grad_out: float32 [4, 640, 1024], P('head', None, 'dp')
- grad_router: float32 [32, 1024], P(('head', 'dp'))
- grad_up: float32 [32, 1024, 128], P(('head', 'dp'))
- grad_down: float32 [32, 128, 1024], P(('head', 'dp'))
Inputs may be any that keep to these rules, and one draw needn't show every extreme that they name: `segments`: segment numbers never fall along a pack; 16 documents of 1 to 512 tokens, one of exactly 512. `value_expert_route`: A token's 2 value experts of one head differ. `output_expert_route`: A token's 2 output experts of one head differ. `feedforward_route`: A token's 16 experts differ; in the rows of one device (aligned blocks of 256 rows) no expert is named more than 160 times, a bound that some block reaches.
All inputs are finite; a program needn't handle non-finite values.
Results may differ from a plain program's by a relative error of at most 0.02.
Values may be sent and summed in bfloat16 or wider, within the bound.
No kernel may reach another device: no remote copies, remote signals or barrier semaphores. Data moves between devices by JAX's collectives and lax.ppermute only.
A program may use at most 256 MiB of HBM per device.

v0:
```python
import functools

import jax
import jax.numpy as jnp
from jax import lax
from jax.experimental import pallas as pl
from jax.experimental.pallas import tpu as pltpu
from jax.sharding import PartitionSpec as P

EPS = 1e-05
F32 = jnp.float32
BF16 = jnp.bfloat16
CHUNK = 8
LANES = 128
WIDE = 256
PAD = 16
MEAN, SPREAD = 16, 17
VMEM_BYTES = 56 * 2**20
ROOT_HALF = 0.7071067811865476
INV_ROOT_2PI = 0.3989422804014327
ANY = pl.BlockSpec(memory_space=pl.ANY)
SMEM = pl.BlockSpec(memory_space=pltpu.SMEM)


def dot(a, b, dims):
    return lax.dot_general(a, b, (dims, ((), ())), preferred_element_type=F32)


def nn(a, b):
    return dot(a, b, ((1,), (0,)))


def nt(a, b):
    return dot(a, b, ((1,), (1,)))


def tn(a, b):
    return dot(a, b, ((0,), (0,)))


def shape(dims, kind):
    return jax.ShapeDtypeStruct(dims, kind)


def cost(micros):
    return pl.CostEstimate(flops=int(micros * 1e9), bytes_accessed=0, transcendentals=0)


class Rows:
    def __init__(self, arrays, most=1 << 20):
        self.arrays = list(arrays)
        most = most if isinstance(most, list) else [most] * len(self.arrays)
        self.counts = [min(a.shape[0], m) for a, m in zip(arrays, most)]
        self.dims = (sum(self.counts),) + tuple(arrays[0].shape[1:])


class Part:
    def __init__(self, array, first, count):
        self.arrays, self.first, self.count = [array], first, count
        self.dims = (array.shape[0], count) + tuple(array.shape[2:])


class In:
    def __init__(self, ref, copies, spans):
        self.ref, self.copies, self.spans, self.waited = ref, copies, spans, set()

    def ready(self, first=0, count=1 << 20):
        for i, (copy, (start, size)) in enumerate(zip(self.copies, self.spans)):
            if i not in self.waited and start < first + count and first < start + size:
                copy.wait()
                self.waited.add(i)
        return self.ref

    def rows(self, first, count):
        return self.ready(first, count)[pl.ds(first, count), :]

    def __getitem__(self, at):
        return self.ready()[at]


class Split:
    def __init__(self, n, dims, kind):
        self.n, self.block, self.kind = n, dims, kind
        self.shape, self.dtype = (n * dims[0], dims[1]), kind


class Out:
    def __init__(self, ref, dest, sems):
        self.ref, self.dest, self.sems, self.copies = ref, dest, sems, []

    def block(self, i, count):
        at = pl.ds(i * count if isinstance(i, int) else pl.multiple_of(i * count, count), count)
        return pltpu.make_async_copy(self.ref.at[at], self.dest.at[at], self.sems.at[i])

    def blocks_sent(self, n, count):
        self.copies += [self.block(i, count) for i in range(n)]

    def __setitem__(self, at, value):
        self.ref[at] = value

    def __getitem__(self, at):
        return self.ref[at]

    def send(self, first=None, count=None):
        if isinstance(self.dest, list):
            n = self.dest[0].shape[0]
            for i, dest in enumerate(self.dest):
                source = self.ref.at[pl.ds(i * n, n)]
                self.copies.append(pltpu.make_async_copy(source, dest, self.sems.at[i]))
                self.copies[-1].start()
            return
        source, dest = self.ref, self.dest
        if first is not None:
            source, dest = source.at[pl.ds(first, count)], dest.at[pl.ds(first, count)]
        copy = pltpu.make_async_copy(source, dest, self.sems.at[len(self.copies)])
        copy.start()
        self.copies.append(copy)


def call(name, micros, body, outs, args, after=()):
    entries = [a if isinstance(a, (Rows, Part)) else Rows([a]) for a in args]
    arrays = [a for e in entries for a in e.arrays]
    single = not isinstance(outs, (list, tuple))
    out_list = [outs] if single else list(outs)

    def kernel(*refs):
        refs = list(refs)
        sources, refs = refs[: len(arrays)], refs[len(arrays) + len(after) :]
        dests = []
        for out in out_list:
            if isinstance(out, Split):
                dests.append(refs[: out.n])
                refs = refs[out.n :]
            else:
                dests.append(refs.pop(0))
        bufs, refs = refs[: len(entries)], refs[len(entries) :]
        in_sems, refs = refs[: len(entries)], refs[len(entries) :]
        out_bufs, out_sems = refs[: len(out_list)], refs[len(out_list) :]
        ins = []
        for entry, buf, sems in zip(entries, bufs, in_sems):
            pairs, spans, at = [], [], 0
            for i, array in enumerate(entry.arrays):
                source, n = sources.pop(0), array.shape[0]
                if isinstance(entry, Rows) and entry.counts[i] < n:
                    n = entry.counts[i]
                    source = source.at[pl.ds(0, n)]
                spans.append((at, n))
                if isinstance(entry, Part):
                    pairs.append((source.at[:, pl.ds(entry.first, entry.count)], buf))
                elif len(entry.arrays) == 1:
                    pairs.append((source, buf))
                else:
                    pairs.append((source, buf.at[pl.ds(at, n)]))
                at += n
            copies = [
                pltpu.make_async_copy(source, dest, sems.at[i])
                for i, (source, dest) in enumerate(pairs)
            ]
            for copy in copies:
                copy.start()
            ins.append(In(buf, copies, spans))
        results = [Out(b, d, s) for b, d, s in zip(out_bufs, dests, out_sems)]
        body(*ins, *results)
        for entry in ins:
            entry.ready()
        for result in results:
            if not result.copies:
                result.send()
        for result in results:
            for copy in result.copies:
                copy.wait()

    shapes = []
    for out in out_list:
        shapes += [shape(out.block, out.kind)] * out.n if isinstance(out, Split) else [out]
    return pl.pallas_call(
        kernel,
        name=name,
        out_shape=shapes[0] if single else shapes,
        in_specs=[ANY] * (len(arrays) + len(after)),
        out_specs=ANY if single else [ANY] * len(shapes),
        scratch_shapes=[pltpu.VMEM(e.dims, e.arrays[0].dtype) for e in entries]
        + [pltpu.SemaphoreType.DMA((len(e.arrays),)) for e in entries]
        + [pltpu.VMEM(o.shape, o.dtype) for o in out_list]
        + [pltpu.SemaphoreType.DMA((8,)) for o in out_list],
        compiler_params=pltpu.CompilerParams(vmem_limit_bytes=VMEM_BYTES),
        cost_estimate=cost(micros),
    )(*arrays, *after)


def repeat(n, body):
    if n == 1:
        body(0)
    else:
        lax.fori_loop(0, n, lambda i, carry: (body(i), carry)[1], 0)


def block_at(i, count):
    return pl.ds(i * count if isinstance(i, int) else pl.multiple_of(i * count, count), count)


def pack_in_kernel(kinds, q, k, v, vsel, osel, o, out):
    size = q.ref.shape[1]
    out[:, 3 * LANES + kinds * size :] = o[...].T
    out[:, 2 * size : 3 * LANES] = jnp.zeros((q.ref.shape[0], LANES), BF16)
    out[:, :size] = q[...]
    out[:, size : 2 * size] = k[...]
    out[:, 2 * size : 2 * size + kinds] = vsel[...]
    out[:, 2 * size + kinds : 2 * size + 2 * kinds] = osel[...]
    out[:, 3 * LANES : 3 * LANES + kinds * size] = v[...]


def pack_experts_kernel(up, down, router, out):
    hidden = up.ref.shape[1]
    out[:hidden, :] = up[...].T
    out[hidden : 2 * hidden, :] = down[...]
    out[2 * hidden :, :] = jnp.broadcast_to(router[...], (PAD, router.ref.shape[1]))


def stack_kernel(pieces, out):
    out[...] = pieces[...]


def split_copy_kernel(a, b, top, bottom):
    top[...] = a[...]
    bottom[...] = b[...]


def split_kernel(rows, top, bottom):
    half = top.ref.shape[0]
    top[...] = rows[:half, :]
    bottom[...] = rows[half:, :]


def residual_kernel(*refs):
    parts, (total, top, bottom) = refs[:-3], refs[-3:]
    half = top.ref.shape[0]
    for first, low in ((0, top), (half, bottom)):
        at = pl.ds(first, half)
        found = parts[0][at, :].astype(F32)
        for part in parts[1:]:
            found = found + part[at, :].astype(F32)
        low[...] = found.astype(BF16)
        low.send()
        total[at, :] = found
        total.send(first, half)


def finish_kernel(*refs):
    parts, out = refs[:-1], refs[-1]
    found = parts[0][...].astype(F32)
    for part in parts[1:]:
        found = found + part[...].astype(F32)
    out[...] = found.astype(BF16)


def finish_experts_kernel(found, up, down, router):
    hidden = up.ref.shape[1]
    up[...] = found[:hidden, :].astype(F32).T
    down[...] = found[hidden : 2 * hidden, :].astype(F32)
    router[...] = found[2 * hidden : 2 * hidden + 1, :].astype(F32)


def finish_weights_kernel(scale, kinds, found, q, k, vsel, osel, v, o):
    size = q.ref.shape[1]
    at = 3 * LANES
    q[...] = found[:, :size].astype(F32) * scale
    k[...] = found[:, size : 2 * size].astype(F32)
    both = found[:, 2 * size : at].astype(F32)
    vsel[...] = both[:, :kinds]
    osel[...] = both[:, kinds : 2 * kinds]
    v[...] = found[:, at : at + kinds * size].astype(F32)
    o[...] = found[:, at + kinds * size :].astype(F32).T


def layer_stats(values):
    mean = jnp.mean(values, -1, keepdims=True)
    center = values - mean
    return mean, lax.rsqrt(jnp.mean(center * center, -1, keepdims=True) + EPS)


def norm_back(scaled, unit, spread):
    return spread * (
        scaled
        - jnp.mean(scaled, -1, keepdims=True)
        - unit * jnp.mean(scaled * unit, -1, keepdims=True)
    )


def project_kernel(own, scale, kinds, size, x, gain, bias, info, w, q, k, v, ev, gate):
    for value in (x, gain, bias, info, w):
        value.ready()

    def block(b):
        at = block_at(b, own)
        rows = x.ref[at, :]
        mean, spread = layer_stats(rows.astype(F32))
        normed = ((rows.astype(F32) - mean) * spread * gain.ref[...] + bias.ref[...]).astype(BF16)
        first = nn(normed, w.ref[:, : 3 * LANES])
        q[at, :] = (first[:, :size] * scale).astype(BF16)
        k[at, :] = first[:, size : 2 * size].astype(BF16)
        lane = lax.broadcasted_iota(jnp.int32, (own, LANES), 1)
        chosen = lane < 0
        for c in range(2, 6):
            chosen = chosen | (lane == info.ref[at, c : c + 1])
        found = jnp.where(chosen, jax.nn.sigmoid(first[:, 2 * size :]), 0.0)
        gate[at, :] = jnp.where(lane == MEAN, mean, jnp.where(lane == SPREAD, spread, found))
        experts = nn(rows, w.ref[:, 3 * LANES :])
        ev[at, :] = experts.astype(BF16)
        ev.block(b, own).start()
        value = found[:, :1] * experts[:, :size]
        for e in range(1, kinds):
            value = value + found[:, e : e + 1] * experts[:, e * size : (e + 1) * size]
        v[at, :] = value.astype(BF16)

    repeat(4, block)
    ev.blocks_sent(4, own)


def visible(info, code):
    return (code >= info[:, 0:1]) & (code <= info[:, 1:2])


def attend_kernel(own, kinds, size, q, k, v, info, code, gate, w, parts, att, lse, mixed):
    for value in (q, k, v, info, code, gate, w):
        value.ready()

    def block(b):
        at = block_at(b, own)
        scores = jnp.where(
            visible(info.ref[at, :], code.ref[...]), nt(q.ref[at, :], k.ref[...]), -jnp.inf
        )
        top = jnp.max(scores, -1, keepdims=True)
        weights = jnp.exp(scores - top)
        total = jnp.sum(weights, -1, keepdims=True)
        probs = (weights / total).astype(BF16)
        found = nn(probs, v.ref[...])
        att[at, :] = found
        lse[at, :] = jnp.broadcast_to(top + jnp.log(total), (own, LANES))
        opened = gate.ref[at, :]
        for e in range(kinds):
            mixed[at, e * size : (e + 1) * size] = (
                opened[:, kinds + e : kinds + e + 1] * found
            ).astype(BF16)
        parts[at, :] = nt(mixed[at, :], w.ref[...]).astype(BF16)

    repeat(4, block)
    parts.send()


def expert_kernel(n_blocks, count, hidden, rows_in, gain, bias, router, hits, up_in, grad_in, down_in, backs, dpre, gated, norm, route):
    width = rows_in.ref.shape[1]
    own = rows_in.ref.shape[0] // n_blocks
    for value in (rows_in, gain, bias, router, hits, up_in):
        value.ready()
    norm[...] = jnp.zeros(norm.ref.shape, F32)
    route[...] = jnp.zeros(route.ref.shape, F32)
    if n_blocks > 1:
        grad_in.ready()
        down_in.ready()

    def block(i):
        at = block_at(i, own)
        rows = rows_in.ref[at, :]
        mean, spread = layer_stats(rows.astype(F32))
        unit = (rows.astype(F32) - mean) * spread
        normed = (unit * gain.ref[...] + bias.ref[...]).astype(BF16)
        gate = jax.nn.sigmoid(nt(normed, router.ref[...])) * hits.ref[at, :]
        pre = nt(rows, up_in.ref[...].reshape(count * hidden, width))
        if n_blocks == 1:
            grad_in.ready()
            down_in.ready()
        back = nt(grad_in.ref[at, :], down_in.ref[...].reshape(count * hidden, width))
        d_gate = []
        for e in range(count):
            col = slice(e * hidden, (e + 1) * hidden)
            p, b, g = pre[:, col], back[:, col], gate[:, e : e + 1]
            bell = 0.5 * (1.0 + lax.erf(p * ROOT_HALF))
            active = p * bell
            slope = bell + p * jnp.exp(-0.5 * p * p) * INV_ROOT_2PI
            gated[at, col] = (g * active).astype(BF16)
            dpre[at, col] = (g * b * slope).astype(BF16)
            d_gate.append(jnp.sum(active * b, -1, keepdims=True))
        gated.block(i, own).start()
        dpre.block(i, own).start()
        d_logit = (jnp.concatenate(d_gate, 1) * gate * (1.0 - gate)).astype(BF16)
        d_n2 = nn(d_logit, router.ref[...])
        backs[at, :] = (
            nn(dpre[at, :], up_in.ref[...].reshape(count * hidden, width))
            + norm_back(d_n2 * gain.ref[...], unit, spread)
        ).astype(BF16)
        norm[...] += jnp.concatenate(
            [jnp.sum(d_n2 * unit, 0, keepdims=True), jnp.sum(d_n2, 0, keepdims=True)], 0
        )
        route[...] += tn(d_logit, normed)

    repeat(n_blocks, block)
    gated.blocks_sent(n_blocks, own)
    dpre.blocks_sent(n_blocks, own)
    backs.send()


def expert_out_kernel(count, hidden, gated, down, outs):
    own, width = gated.ref.shape[0] // 4, outs.ref.shape[1]
    gated.ready()
    down.ready()

    def block(i):
        at = block_at(i, own)
        rows = gated.ref[at, :]
        outs[at, :] = nn(rows, down.ref[...].reshape(count * hidden, width)).astype(BF16)

    repeat(4, block)
    outs.send()


def expert_grad_kernel(count, hidden, gated, grad, dpre, rows, *refs):
    routes, out = refs[:-1], refs[-1]
    pair = WIDE // hidden
    for value in (gated, grad, dpre, rows, *routes):
        value.ready()
    for e in range(count):
        route = sum(r.ref[e : e + 1, :] for r in routes)
        out[e, 2 * hidden :, :] = jnp.broadcast_to(route, (PAD, route.shape[1])).astype(BF16)

    def block(c):
        col = block_at(c, WIDE)
        down = tn(gated.ref[:, col], grad.ref[...]).astype(BF16)
        up = tn(dpre.ref[:, col], rows.ref[...]).astype(BF16)
        for j in range(pair):
            out[c * pair + j, :hidden, :] = up[j * hidden : (j + 1) * hidden]
            out[c * pair + j, hidden : 2 * hidden, :] = down[j * hidden : (j + 1) * hidden]
        out.block(c, pair).start()

    repeat(count // pair, block)
    out.blocks_sent(count // pair, pair)


def attend_back_rows(own, b, d_rows, kinds, size, w, q, k, v, info, code, gate, att, lse):
    at = block_at(b, own)
    lane = lax.broadcasted_iota(jnp.int32, (own, LANES), 1)
    found, opened, queries = att.ref[at, :], gate.ref[at, :], q.ref[at, :]
    scores = jnp.where(visible(info.ref[at, :], code.ref[...]), nt(queries, k.ref[...]), -jnp.inf)
    probs = jnp.exp(scores - lse.ref[at, 0:1])
    d_mixed = nn(d_rows, w.ref[...])
    d_att = jnp.zeros((own, size), F32)
    d_sel = jnp.zeros((own, LANES), F32)
    for e in range(kinds):
        part = d_mixed[:, e * size : (e + 1) * size]
        d_att = d_att + opened[:, kinds + e : kinds + e + 1] * part
        d_sel = jnp.where(lane == kinds + e, jnp.sum(part * found, -1, keepdims=True), d_sel)
    d_att = d_att.astype(BF16)
    d_probs = nt(d_att, v.ref[...])
    centered = jnp.sum(probs * d_probs, -1, keepdims=True)
    d_scores = (probs * (d_probs - centered)).astype(BF16)
    return (
        nn(d_scores, k.ref[...]).astype(BF16),
        d_sel * opened * (1.0 - opened),
        tn(d_scores, queries),
        tn(probs.astype(BF16), d_att),
    )


def attend_back_kernel(own, n, kinds, size, q, k, info, code, lse, w, d_rows, v, gate, att, dq, dsel, dk, dv):
    for value in (q, k, info, code, lse, w, d_rows, v, gate, att):
        value.ready()
    dk[...] = jnp.zeros(dk.ref.shape, F32)
    dv[...] = jnp.zeros(dv.ref.shape, F32)

    def block(b):
        at = block_at(b, own)
        query, selector, key, value = attend_back_rows(
            own, b, d_rows.ref[at, :], kinds, size, w, q, k, v, info, code, gate, att, lse
        )
        dq[at, :] = query
        dsel[at, :] = selector
        dk[...] += key
        dv[...] += value

    repeat(n, block)


def attend_last_kernel(own, kinds, size, q, k, info, code, lse, w, d_rows, v, gate, att, dq, dsel, dk, dv, ev, din, dexp):
    last = 3 * own
    for value in (q, k, info, code, lse, w, d_rows, v, gate, att):
        value.ready()
    query, selector, more_k, more_v = attend_back_rows(
        own, 3, d_rows.ref[...], kinds, size, w, q, k, v, info, code, gate, att, lse
    )
    for value in (dq, dsel, dk, dv, ev):
        value.ready()
    din[last:, :size] = query
    din[:last, :size] = dq.ref[...]
    dk.ref[...] += more_k
    dv.ref[...] += more_v
    dsel.ref[last:, :] = selector
    lane = lax.broadcasted_iota(jnp.int32, (own, LANES), 1)

    def block(b):
        at = block_at(b, own)
        opened, value = gate.ref[at, :], dv.ref[at, :]
        factor = opened * (1.0 - opened)
        din[at, size : 2 * size] = dk.ref[at, :].astype(BF16)
        d_sel = dsel.ref[at, :]
        for e in range(kinds):
            col = slice(e * size, (e + 1) * size)
            moved = jnp.sum(ev.ref[at, col].astype(F32) * value, -1, keepdims=True)
            d_sel = jnp.where(lane == e, moved * factor, d_sel)
            dexp[at, col] = (opened[:, e : e + 1] * value).astype(BF16)
        din[at, 2 * size :] = d_sel.astype(BF16)

    repeat(4, block)


def weight_kernel(din, dexp, x, gate, gain, bias, d_rows, mixed, out):
    width = x.ref.shape[1]
    for value in (din, dexp, x, gate, gain, bias, d_rows, mixed):
        value.ready()
    mean, spread = gate.ref[:, MEAN : MEAN + 1], gate.ref[:, SPREAD : SPREAD + 1]
    first_end = din.ref.shape[1]
    second_end = first_end + dexp.ref.shape[1]

    for first in range(0, width, WIDE):
        at = slice(first, first + WIDE)
        rows = x.ref[:, at]
        normed = (rows.astype(F32) - mean) * spread * gain.ref[:, at] + bias.ref[:, at]
        out[at, :first_end] = tn(normed.astype(BF16), din.ref[...]).astype(BF16)
        out[at, first_end:second_end] = tn(rows, dexp.ref[...]).astype(BF16)
        out[at, second_end:] = tn(d_rows.ref[:, at], mixed.ref[...]).astype(BF16)
        out.send(first, WIDE)


def input_grad_kernel(own, scale, size, x, din, gate, gain, w, dexp, outs, norm):
    for value in (x, din, gate, gain, w, dexp):
        value.ready()
    norm[...] = jnp.zeros(norm.ref.shape, F32)

    def block(b):
        at = block_at(b, own)
        spread = gate.ref[at, SPREAD : SPREAD + 1]
        unit = (x.ref[at, :].astype(F32) - gate.ref[at, MEAN : MEAN + 1]) * spread
        d_normed = nt(din.ref[at, :size], w.ref[:, :size]) * scale + nt(
            din.ref[at, size:], w.ref[:, size : 3 * LANES]
        )
        outs[at, :] = (
            norm_back(d_normed * gain.ref[...], unit, spread)
            + nt(dexp.ref[at, :], w.ref[:, 3 * LANES :])
        ).astype(BF16)
        norm[...] += jnp.concatenate(
            [jnp.sum(d_normed * unit, 0, keepdims=True), jnp.sum(d_normed, 0, keepdims=True)], 0
        )

    repeat(4, block)
    outs.send()


def to_head(value, flip):
    n = lax.axis_size("head")
    return lax.ppermute(value, "head", [(i, i ^ flip) for i in range(n)])


def near_rows(top, bottom):
    y_top, x_bottom = to_head(top, 2), to_head(bottom, 1)
    y_bottom, x_top = to_head(bottom, 2), to_head(top, 1)
    return [[x_top, x_bottom], [y_top, y_bottom]]


def far_rows(near):
    return [to_head(near[1][0], 1), to_head(near[0][1], 2)]


def spread_rows(top, bottom):
    near = near_rows(top, bottom)
    return [[top, bottom], *near, far_rows(near)]


def far_rows_after(near, after):
    half = shape(near[0][0].shape, BF16)
    passed = call(
        "relay", 1, split_copy_kernel, [half, half], [near[1][0], near[0][1]], after
    )
    return [to_head(passed[0], 1), to_head(passed[1], 2)]


def flat(blocks):
    return [piece for block in blocks for piece in block]


def expert_blocks(name, rows, grads, hits, weights, router, gain, bias, after=()):
    count, hidden = weights.shape[0], (weights.shape[1] - PAD) // 2
    n, own, width = len(hits), hits[0].shape[0], weights.shape[2]
    wide = shape((n * own, count * hidden), BF16)
    got = call(
        name,
        3 * n + 2,
        functools.partial(expert_kernel, n, count, hidden),
        [
            Split(n, (own, width), BF16),
            wide,
            wide,
            shape((2, width), F32),
            shape((count, width), F32),
        ],
        [
            Rows(flat(rows)),
            gain,
            bias,
            router,
            Rows(hits),
            Part(weights, 0, hidden),
            Rows(flat(grads), most=[own // min(2, len(g)) for g in grads for _ in g]),
            Part(weights, hidden, hidden),
        ],
        after,
    )
    return [list(got[:n]), [got[n]], [got[n + 1]], got[-2], got[-1]]


def expert_chunk(rows, spread, grads, hits, weights, router, gain, bias, moves=()):
    count, hidden = weights.shape[0], (weights.shape[1] - PAD) // 2
    width, own = weights.shape[2], hits[0].shape[0]
    shared = (weights, router, gain, bias)
    first = expert_blocks("experts_own", rows[:1], grads[:1], hits[:1], *shared)
    rows = [rows[0], *spread(first[0])]
    near = expert_blocks(
        "experts_near", rows[1:3], grads[1:3], hits[1:3], *shared, (first[0][0], *rows[3])
    )
    far = expert_blocks("experts_far", rows[3:], grads[3:], hits[3:], *shared, near[0])
    back, dpre, gated = (first[i] + near[i] + far[i] for i in range(3))
    norm = first[3] + near[3] + far[3]
    moved = [to_head(back[flip], flip) for flip in moves]
    slabs = call(
        "experts_weights",
        8,
        functools.partial(expert_grad_kernel, count, hidden),
        shape((count, 2 * hidden + PAD, width), BF16),
        [
            Rows(gated),
            Rows(flat(grads), most=[own] * 3 + [own // 2] * 2),
            Rows(dpre),
            Rows(flat(rows)),
            first[4],
            near[4],
            far[4],
        ],
        moved[:2],
    )
    return back, moved, gated, norm, slabs


def expert_out(gated, weights, after):
    count, hidden = weights.shape[0], (weights.shape[1] - PAD) // 2
    return call(
        "experts_out",
        12,
        functools.partial(expert_out_kernel, count, hidden),
        [Split(4, (sum(g.shape[0] for g in gated) // 4, weights.shape[2]), BF16)],
        [Rows(gated), Part(weights, hidden, hidden)],
        after,
    )


def shards(
    tokens,
    cotangent,
    segments,
    value_expert_route,
    output_expert_route,
    feedforward_route,
    attention_norm_gain,
    attention_norm_bias,
    feedforward_norm_gain,
    feedforward_norm_bias,
    query_projection,
    key_projection,
    value_selector,
    output_selector,
    value_experts,
    output_experts,
    feedforward_selector,
    expert_up_weight,
    expert_down_weight,
):
    n_data = lax.axis_size("dp")
    head = lax.axis_index("head")
    own, width = tokens.shape[1:]
    half = own // 2
    length = segments.shape[1]
    size = query_projection.shape[1]
    kinds = value_selector.shape[1]
    hidden = expert_up_weight.shape[2]
    scale = size ** (-0.5)
    mixed_width = kinds * size

    def arranged(value):
        return jnp.concatenate(
            [lax.dynamic_slice_in_dim(value, (head ^ k) * own, own, 0) for k in range(4)]
        )

    x_own, grad_own = tokens[0], cotangent[0]
    last = 3 * LANES + mixed_width
    all_own = call(
        "pack_weights",
        1,
        functools.partial(pack_in_kernel, kinds),
        shape((query_projection.shape[0], last + mixed_width), BF16),
        [
            query_projection,
            key_projection,
            value_experts[0],
            value_selector,
            output_selector,
            output_experts[0],
        ],
    )
    all_in = lax.all_gather(all_own, "dp", axis=0, tiled=True)
    in_all, out_all = Part(all_in, 0, last), Part(all_in, last, mixed_width)
    x = spread_rows(
        *call("split_rows", 1, split_kernel, [shape((half, width), BF16)] * 2, [x_own])
    )
    experts = 4 * n_data
    hot = jnp.sum(jax.nn.one_hot(feedforward_route[0], experts, dtype=BF16), 1)
    hot_rows = own * experts // width
    hot = hot.reshape(hot_rows, width)
    hot = jnp.concatenate([hot, jnp.zeros((-hot_rows % PAD, width), BF16)])
    grad_sent = call(
        "pack_grad",
        1,
        stack_kernel,
        shape((own + hot.shape[0], width), BF16),
        [Rows([grad_own, hot])],
    )
    near_x, near_y = to_head(grad_sent, 1), to_head(grad_sent, 2)
    far_top, far_bottom = to_head(near_y[:half], 1), to_head(near_x[half:], 2)
    grad = [[grad_own], [near_x], [near_y], [far_top, far_bottom]]

    def hits_of(rows):
        found = rows[:hot_rows].reshape(own, experts)
        return lax.dynamic_slice_in_dim(found, head * n_data, n_data, 1).astype(F32)

    hits = [hits_of(v) for v in (hot, near_x[own:], near_y[own:], far_bottom[half:])]
    ffn_own = call(
        "pack_experts",
        2,
        pack_experts_kernel,
        shape((2 * hidden + PAD, width), BF16),
        [expert_up_weight[0], expert_down_weight[0], feedforward_selector],
        flat(x[1:3]),
    )
    ffn_all = lax.all_gather(ffn_own, "dp", axis=0, tiled=False)
    router = ffn_all[:, 2 * hidden]

    spots = jnp.arange(length, dtype=jnp.int32)
    first_code = segments[0] * length
    info = arranged(
        jnp.concatenate(
            [
                first_code[:, None],
                (first_code + spots)[:, None],
                value_expert_route[0, :, 0],
                output_expert_route[0, :, 0] + kinds,
                jnp.zeros((length, 2), jnp.int32),
            ],
            1,
        )
    )
    code = arranged(first_code + spots)[None]
    gain1, bias1 = attention_norm_gain[None], attention_norm_bias[None]
    gain2, bias2 = feedforward_norm_gain[None], feedforward_norm_bias[None]
    query, key, value, experts_v, gate = call(
        "project",
        7,
        functools.partial(project_kernel, own, scale, kinds, size),
        [shape((length, size), BF16)] * 3
        + [shape((length, mixed_width), BF16), shape((length, LANES), F32)],
        [Rows(flat(x)), gain1, bias1, info, in_all],
    )

    part_own, part_x, part_y, part_far, att, lse, mixed = call(
        "attend",
        8,
        functools.partial(attend_kernel, own, kinds, size),
        [
            Split(4, (own, width), BF16),
            shape((length, size), F32),
            shape((length, LANES), F32),
            shape((length, mixed_width), BF16),
        ],
        [query, key, value, info, code, gate, out_all],
        flat(grad[1:]),
    )

    def residual(name, parts, after=()):
        return call(
            name,
            2,
            residual_kernel,
            [shape((own, width), F32)] + [shape((half, width), BF16)] * 2,
            parts,
            after,
        )

    parts = [to_head(part, flip) for part, flip in ((part_far, 3), (part_x, 1), (part_y, 2))]
    resid, top, bottom = residual("residual", [x_own, part_own, *parts])
    near = near_rows(top, bottom)

    if n_data <= CHUNK:
        back, moved, gated, norm2, slabs = expert_chunk(
            [[top, bottom]],
            lambda after: [*near, far_rows_after(near, after)],
            grad,
            hits,
            ffn_all,
            router,
            gain2,
            bias2,
            (1, 2, 3),
        )
    else:
        cut = lambda a: a.reshape((n_data // CHUNK, CHUNK) + a.shape[1:])
        others = [*near, far_rows(near)]
        hit_cuts = [
            h.reshape(own, n_data // CHUNK, CHUNK).transpose(1, 0, 2) for h in hits
        ]

        def step(carry, item):
            hit, rt, w = item
            got_back, _, got_gated, got_norm, slab = expert_chunk(
                [[top, bottom]], lambda _: others, grad, hit, w, rt, gain2, bias2
            )
            got_out = expert_out(got_gated, w, ())
            add = lambda old, new: [o + v.astype(F32) for o, v in zip(old, new)]
            new = (add(carry[0], got_out), add(carry[1], got_back), carry[2] + got_norm)
            return new, slab

        zero = [jnp.zeros((own, width), F32)] * 4
        (out, back, norm2), slabs = lax.scan(
            step,
            (zero, zero, jnp.zeros((2, width), F32)),
            (hit_cuts, cut(router), cut(ffn_all)),
        )
        out, back = [v.astype(BF16) for v in out], [v.astype(BF16) for v in back]
        moved = [to_head(back[flip], flip) for flip in (1, 2, 3)]
        slabs = slabs.reshape((n_data,) + slabs.shape[2:])

    ffn_grads = lax.psum_scatter(slabs, "dp", scatter_dimension=0, tiled=True)
    if n_data <= CHUNK:
        out = expert_out(gated, ffn_all, ())
    d_resid, top, bottom = residual("residual_back", [grad_own, back[0], *moved], [slabs, *out])
    d_pack = spread_rows(top, bottom)

    dq, dsel, dk, dv = call(
        "attend_back",
        6,
        functools.partial(attend_back_kernel, own, 3, kinds, size),
        [
            shape((3 * own, size), BF16),
            shape((length, LANES), F32),
            shape((length, size), F32),
            shape((length, size), F32),
        ],
        [query, key, info, code, lse, out_all, Rows(flat(d_pack[:3])), value, gate, att],
        out,
    )
    out_moved = [to_head(out[flip], flip) for flip in (3, 1, 2)]
    d_in, d_exp = call(
        "attend_last",
        5,
        functools.partial(attend_last_kernel, own, kinds, size),
        [shape((length, 3 * LANES), BF16), shape((length, mixed_width), BF16)],
        [
            query,
            key,
            info,
            code,
            lse,
            out_all,
            Rows(d_pack[3]),
            value,
            gate,
            att,
            dq,
            dsel,
            dk,
            dv,
            experts_v,
        ],
    )
    weight_part = call(
        "weights",
        6,
        weight_kernel,
        shape((width, 3 * LANES + 2 * mixed_width), BF16),
        [
            d_in,
            d_exp,
            Rows(flat(x)),
            gate,
            gain1,
            bias1,
            Rows(flat(d_pack)),
            mixed,
        ],
        (ffn_grads, *out_moved[1:]),
    )
    d_own, d_x, d_y, d_far, norm1 = call(
        "input_back",
        6,
        functools.partial(input_grad_kernel, own, scale, size),
        [Split(4, (own, width), BF16), shape((2, width), F32)],
        [Rows(flat(x)), d_in, gate, gain1, in_all, d_exp],
        (weight_part,),
    )
    moved = [to_head(part, flip) for part, flip in ((d_far, 3), (d_x, 1), (d_y, 2))]
    block = shape((own, width), BF16)
    up_grad, down_grad, router_grad = call(
        "finish_experts",
        2,
        finish_experts_kernel,
        [shape((width, hidden), F32), shape((hidden, width), F32), shape((1, width), F32)],
        [ffn_grads[0]],
    )
    output = call(
        "output",
        2,
        finish_kernel,
        block,
        [resid, out[0], *out_moved],
        moved[1:],
    )
    grad_tokens = call(
        "token_grads", 2, finish_kernel, block, [d_resid, d_own, *moved]
    )

    part = width // n_data
    grads = lax.psum_scatter(weight_part, "dp", scatter_dimension=0, tiled=True)
    query_grad, key_grad, value_sel, output_sel, value_grad, output_grad = call(
        "finish_weights",
        2,
        functools.partial(finish_weights_kernel, scale, kinds),
        [
            shape((part, size), F32),
            shape((part, size), F32),
            shape((part, kinds), F32),
            shape((part, kinds), F32),
            shape((part, mixed_width), F32),
            shape((mixed_width, part), F32),
        ],
        [grads],
    )
    norms = jnp.concatenate([norm1, norm2]).reshape(4, 4 * n_data, -1).transpose(1, 0, 2)
    norms = lax.all_to_all(norms, ("head", "dp"), split_axis=0, concat_axis=0, tiled=True)
    norms = jnp.sum(norms, 0)
    return (
        output[None],
        grad_tokens[None],
        norms,
        query_grad,
        key_grad,
        value_sel,
        output_sel,
        value_grad[None],
        output_grad[None],
        router_grad,
        up_grad[None],
        down_grad[None],
    )


def solution(mesh):
    placed = (
        P("dp", "head", None),
        P("dp", "head", None),
        P("dp", None),
        P("dp", None, "head", None),
        P("dp", None, "head", None),
        P("dp", "head", None),
        P(),
        P(),
        P(),
        P(),
        P("dp", "head"),
        P("dp", "head"),
        P("dp", "head"),
        P("dp", "head"),
        P("head", "dp", None),
        P("head", None, "dp"),
        P(("head", "dp"), None),
        P(("head", "dp"), None, None),
        P(("head", "dp"), None, None),
    )
    return jax.shard_map(
        shards,
        mesh=mesh,
        in_specs=placed,
        out_specs=(
            P("dp", "head", None),
            P("dp", "head", None),
            P(None, ("head", "dp")),
            P("dp", "head"),
            P("dp", "head"),
            P("dp", "head"),
            P("dp", "head"),
            P("head", "dp", None),
            P("head", None, "dp"),
            P(("head", "dp"), None),
            P(("head", "dp"), None, None),
            P(("head", "dp"), None, None),
        ),
        check_vma=False,
    )
```

profile of v0, /device:TPU:0, one launch (start us, length us, event | category | flops | bytes accessed | tf_op | source)
XLA Modules:
  0.0 286.5 jit_solution(14229564256720249209)
XLA Ops:
  14.3 3.0 %collective-permute-start.2 = (bf16[128,1024]{1,0:T(8,128)(2,1)}, bf16[128,1024]{1,0:T(8,128)(2,1)S(1)}, u32[]{:S(2)}, u32[]{:S(2)}) collective-permute-start(bf16[128,1024]{1,0:T(8,128)(2,1)} %get-tuple-element.74.refs_0_.refs_2_), channel_id=1, source_target_pairs={{0,16},{8,24},{16,0},{24,8},{1,17},{9,25},{17,1},{25,9},{2,18},{10... | collective-permute-start | bytes 786440 | tf_op jit(solution)/shard_map/ppermute | solution.py:559
  19.5 5.2 %collective-permute-done.2.refs_4_.refs_5_.refs_6_ = bf16[128,1024]{1,0:T(8,128)(2,1)S(1)} collective-permute-done((bf16[128,1024]{1,0:T(8,128)(2,1)}, bf16[128,1024]{1,0:T(8,128)(2,1)S(1)}, u32[]{:S(2)}, u32[]{:S(2)}) %collective-permute-start.2) | collective-permute-done | bytes 262176 | tf_op jit(solution)/shard_map/ppermute | solution.py:559
  26.8 2.7 collective-permute-done.3.refs_5_.refs_6_.refs_7_
  42.8 9.8 %collective-permute-done.7.refs_8_.refs_11_.refs_5_ = bf16[272,1024]{1,0:T(8,128)(2,1)S(1)} collective-permute-done((bf16[272,1024]{1,0:T(8,128)(2,1)}, bf16[272,1024]{1,0:T(8,128)(2,1)S(1)}, u32[]{:S(2)}, u32[]{:S(2)}) %collective-permute-start.7) | collective-permute-done | bytes 557088 | tf_op jit(solution)/shard_map/ppermute | solution.py:559
  54.8 3.8 %collective-permute-done.4.refs_6_.refs_8_ = bf16[128,1024]{1,0:T(8,128)(2,1)S(1)} collective-permute-done((bf16[128,1024]{1,0:T(8,128)(2,1)S(1)}, bf16[128,1024]{1,0:T(8,128)(2,1)S(1)}, u32[]{:S(2)}, u32[]{:S(2)}) %collective-permute-start.4) | collective-permute-done | bytes 262176 | tf_op jit(solution)/shard_map/ppermute | solution.py:559
  59.4 8.4 %project.1 = (bf16[1024,128]{1,0:T(8,128)(2,1)}, bf16[1024,128]{1,0:T(8,128)(2,1)}, bf16[1024,128]{1,0:T(8,128)(2,1)}, bf16[1024,640]{1,0:T(8,128)(2,1)}, f32[1024,128]{1,0:T(8,128)}) custom-call(bf16[128,1024]{1,0:T(8,128)(2,1)} %get-tuple-element.74.refs_0_.refs_2_, bf16[128,1024]{1,0:T(8,128)(2,1)} %get-tuple-element.75.refs_1_.refs_3_, ...), custom_call_target="tpu_custom_call" | custom-call | flops 7000000000 | tf_op jit(solution)/shard_map/project/pallas_call | solution.py:176
  68.6 10.2 %attend.1 = (bf16[256,1024]{1,0:T(8,128)(2,1)}, bf16[256,1024]{1,0:T(8,128)(2,1)}, bf16[256,1024]{1,0:T(8,128)(2,1)}, bf16[256,1024]{1,0:T(8,128)(2,1)}, f32[102...) custom-call(bf16[1024,128]{1,0:T(8,128)(2,1)} %get-tuple-element.76.refs_0_, ...), custom_call_target="tpu_custom_call" | custom-call | flops 8000000000 | tf_op jit(solution)/shard_map/attend/pallas_call | solution.py:176
  78.8 2.7 collective-permute-start.10
  83.1 11.7 %collective-permute-done.10.refs_2_ = bf16[256,1024]{1,0:T(8,128)(2,1)S(1)} collective-permute-done((bf16[256,1024]{1,0:T(8,128)(2,1)}, bf16[256,1024]{1,0:T(8,128)(2,1)S(1)}, u32[]{:S(2)}, u32[]{:S(2)}) %collective-permute-start.10) | collective-permute-done | bytes 524320 | tf_op jit(solution)/shard_map/ppermute | solution.py:559
  94.8 6.7 %collective-permute-done.11.refs_3_ = bf16[256,1024]{1,0:T(8,128)(2,1)S(1)} collective-permute-done((bf16[256,1024]{1,0:T(8,128)(2,1)}, bf16[256,1024]{1,0:T(8,128)(2,1)S(1)}, u32[]{:S(2)}, u32[]{:S(2)}) %collective-permute-start.11) | collective-permute-done | bytes 524320 | tf_op jit(solution)/shard_map/ppermute | solution.py:559
  102.4 3.2 %residual.1 = (f32[256,1024]{1,0:T(8,128)}, bf16[128,1024]{1,0:T(8,128)(2,1)}, bf16[128,1024]{1,0:T(8,128)(2,1)}) custom-call(bf16[256,1024]{1,0:T(8,128)(2,1)} %bitcast.57, bf16[256,1024]{1,0:T(8,128)(2,1)} %get-tuple-element.80.refs_1_, bf16[256,1024]{1,0:T(8,128)(2,1)} %copy-done.23, bf16[256,1024]{1,0:T(8,128)(2,1)} %copy-done.24, ...), custom_call_target="tpu_custom_call" | custom-call | flops 2000000000 | tf_op jit(solution)/shard_map/residual/pallas_call | solution.py:176
  111.3 6.5 %experts_own.1 = (bf16[256,1024]{1,0:T(8,128)(2,1)}, bf16[256,1024]{1,0:T(8,128)(2,1)}, bf16[256,1024]{1,0:T(8,128)(2,1)}, f32[2,1024]{1,0:T(2,128)}, f32[8,1024]{1,0:T(8,128)}) custom-call(bf16[128,1024]{1,0:T(8,128)(2,1)} %get-tuple-element.85.refs_0_.refs_11_, bf16[128,1024]{1,0:T(8,128)(2,1)} %get-tuple-element.86.refs_1_.refs_12_, f32[1,1024]{1,0:T(1,128)} %bitcast.62, ...), custom_call_target="tpu_custom_call" | custom-call | flops 5000000000 | tf_op jit(solution)/shard_map/experts_own/pallas_call | solution.py:176
  117.8 3.0 %collective-permute-done.14.refs_1_.refs_14_ = bf16[128,1024]{1,0:T(8,128)(2,1)S(1)} collective-permute-done((bf16[128,1024]{1,0:T(8,128)(2,1)}, bf16[128,1024]{1,0:T(8,128)(2,1)S(1)}, u32[]{:S(2)}, u32[]{:S(2)}) %collective-permute-start.14) | collective-permute-done | bytes 262176 | tf_op jit(solution)/shard_map/ppermute | solution.py:559
  127.4 3.6 %collective-permute-done.17.refs_14_.refs_0_.refs_17_ = bf16[128,1024]{1,0:T(8,128)(2,1)S(1)} collective-permute-done((bf16[128,1024]{1,0:T(8,128)(2,1)}, bf16[128,1024]{1,0:T(8,128)(2,1)S(1)}, u32[]{:S(2)}, u32[]{:S(2)}) %collective-permute-start.17) | collective-permute-done | bytes 262176 | tf_op jit(solution)/shard_map/ppermute | solution.py:559
  132.9 10.5 %experts_near.1 = (bf16[256,1024]{1,0:T(8,128)(2,1)}, bf16[256,1024]{1,0:T(8,128)(2,1)}, bf16[512,1024]{1,0:T(8,128)(2,1)}, bf16[512,1024]{1,0:T(8,128)(2,1)}, f32[2,1024]{1,0:T(2,128)}, /*index=5*/f32[8,1024]{1,0:T(8,128)}) custom-call(bf16[128,1024]{1,0:T(8,128)(2,1)} %copy-done.35, bf16[128,1024]{1,0:T(8,128)(2,1)} %copy-done.37, ...), custom_call_target="tpu_custom_call" | custom-call | flops 8000000000 | tf_op jit(solution)/shard_map/experts_near/pallas_call | solution.py:176
  145.3 6.6 %experts_far.1 = (bf16[256,1024]{1,0:T(8,128)(2,1)}, bf16[256,1024]{1,0:T(8,128)(2,1)}, bf16[256,1024]{1,0:T(8,128)(2,1)}, f32[2,1024]{1,0:T(2,128)}, f32[8,1024]{1,0:T(8,128)}) custom-call(bf16[128,1024]{1,0:T(8,128)(2,1)} %copy-done.40, bf16[128,1024]{1,0:T(8,128)(2,1)} %copy-done.42, f32[1,1024]{1,0:T(1,128)} %bitcast.64, f32[1,1024]{1,0:T(1,128)} %bitcast.67, ...), custom_call_target="tpu_custom_call" | custom-call | flops 5000000000 | tf_op jit(solution)/shard_map/experts_far/pallas_call | solution.py:176
  151.9 3.4 %collective-permute-done.22.refs_22_.refs_2_ = bf16[256,1024]{1,0:T(8,128)(2,1)S(1)} collective-permute-done((bf16[256,1024]{1,0:T(8,128)(2,1)}, bf16[256,1024]{1,0:T(8,128)(2,1)S(1)}, u32[]{:S(2)}, u32[]{:S(2)}) %collective-permute-start.22) | collective-permute-done | bytes 524320 | tf_op jit(solution)/shard_map/ppermute | solution.py:559
  157.1 9.9 %experts_weights.1.refs_5_ = bf16[8,272,1024]{2,1,0:T(8,128)(2,1)} custom-call(bf16[256,1024]{1,0:T(8,128)(2,1)} %get-tuple-element.87.refs_0_, bf16[512,1024]{1,0:T(8,128)(2,1)} %get-tuple-element.91.refs_1_, bf16[256,1024]{1,0:T(8,128)(2,1)} %get-tuple-element.94.refs_2_, bf16[256,1024]{1,0:T(8,128)(2,1)} %bitcast.35, bf16[272,1024]{1,0:T(8,128)(2,1)} %copy-done.6, ...), custom_call_target="tpu_custom_call" | custom-call | flops 8000000000 | tf_op jit(solution)/shard_map/experts_weights/pallas_call | solution.py:176
  168.5 6.9 %experts_out.1 = (bf16[256,1024]{1,0:T(8,128)(2,1)}, bf16[256,1024]{1,0:T(8,128)(2,1)}, bf16[256,1024]{1,0:T(8,128)(2,1)}, bf16[256,1024]{1,0:T(8,128)(2,1)}) custom-call(bf16[256,1024]{1,0:T(8,128)(2,1)} %get-tuple-element.87.refs_0_, bf16[512,1024]{1,0:T(8,128)(2,1)} %get-tuple-element.91.refs_1_, bf16[256,1024]{1,0:T(8,128)(2,1)} %get-tuple-element.94.refs_2_, ...), custom_call_target="tpu_custom_call" | custom-call | flops 12000000000 | tf_op jit(solution)/shard_map/experts_out/pallas_call | solution.py:176
  175.4 4.2 %collective-permute-done.24.refs_4_ = bf16[256,1024]{1,0:T(8,128)(2,1)S(1)} collective-permute-done((bf16[256,1024]{1,0:T(8,128)(2,1)S(1)}, bf16[256,1024]{1,0:T(8,128)(2,1)S(1)}, u32[]{:S(2)}, u32[]{:S(2)}) %collective-permute-start.24) | collective-permute-done | bytes 524320 | tf_op jit(solution)/shard_map/ppermute | solution.py:559
  180.4 3.2 %residual_back.1 = (f32[256,1024]{1,0:T(8,128)}, bf16[128,1024]{1,0:T(8,128)(2,1)}, bf16[128,1024]{1,0:T(8,128)(2,1)}) custom-call(bf16[256,1024]{1,0:T(8,128)(2,1)} %bitcast.36, bf16[256,1024]{1,0:T(8,128)(2,1)} %get-tuple-element.88.refs_2_.refs_13_.refs_1_, bf16[256,1024]{1,0:T(8,128)(2,1)} %copy-done.3, bf16[256,1024]{1,0:T(8,128)(2,1)} %copy-done.4, ...), custom_call_target="tpu_custom_call" | custom-call | flops 2000000000 | tf_op jit(solution)/shard_map/residual_back/pallas_call | solution.py:176
  188.5 4.6 %collective-permute-done.29.refs_8_.refs_15_ = bf16[128,1024]{1,0:T(8,128)(2,1)S(1)} collective-permute-done((bf16[128,1024]{1,0:T(8,128)(2,1)}, bf16[128,1024]{1,0:T(8,128)(2,1)S(1)}, u32[]{:S(2)}, u32[]{:S(2)}) %collective-permute-start.29) | collective-permute-done | bytes 262176 | tf_op jit(solution)/shard_map/ppermute | solution.py:559
  195.2 3.6 %collective-permute-done.27.refs_9_.refs_16_ = bf16[128,1024]{1,0:T(8,128)(2,1)S(1)} collective-permute-done((bf16[128,1024]{1,0:T(8,128)(2,1)}, bf16[128,1024]{1,0:T(8,128)(2,1)S(1)}, u32[]{:S(2)}, u32[]{:S(2)}) %collective-permute-start.27) | collective-permute-done | bytes 262176 | tf_op jit(solution)/shard_map/ppermute | solution.py:559
  200.2 9.3 %attend_back.1 = (bf16[768,128]{1,0:T(8,128)(2,1)}, f32[1024,128]{1,0:T(8,128)}, f32[1024,128]{1,0:T(8,128)}, f32[1024,128]{1,0:T(8,128)}) custom-call(bf16[1024,128]{1,0:T(8,128)(2,1)} %get-tuple-element.76.refs_0_, bf16[1024,128]{1,0:T(8,128)(2,1)} %get-tuple-element.77.refs_1_, s32[1024,8]{1,0:T(8,128)} %copy.59.refs_10_.refs_3_.refs_2_, ...), custom_call_target="tpu_custom_call" | custom-call | flops 6000000000 | tf_op jit(solution)/shard_map/attend_back/pallas_call | solution.py:176
  211.8 8.1 %attend_last.1 = (bf16[1024,384]{1,0:T(8,128)(2,1)}, bf16[1024,640]{1,0:T(8,128)(2,1)}) custom-call(bf16[1024,128]{1,0:T(8,128)(2,1)} %get-tuple-element.76.refs_0_, bf16[1024,128]{1,0:T(8,128)(2,1)} %get-tuple-element.77.refs_1_, s32[1024,8]{1,0:T(8,128)} %copy.59.refs_10_.refs_3_.refs_2_, s32[1,1024]{1,0:T(1,128)} %bitcast.46, ...), custom_call_target="tpu_custom_call" | custom-call | flops 5000000000 | tf_op jit(solution)/shard_map/attend_last/pallas_call | solution.py:176
  220.9 10.1 %weights.1.refs_13_ = bf16[1024,1664]{1,0:T(8,128)(2,1)} custom-call(bf16[1024,384]{1,0:T(8,128)(2,1)} %get-tuple-element.115.refs_0_.refs_8_, bf16[1024,640]{1,0:T(8,128)(2,1)} %get-tuple-element.116.refs_1_.refs_12_, bf16[128,1024]{1,0:T(8,128)(2,1)} %get-tuple-element.74.refs_0_.refs_2_, bf16[128,1024]{1,0:T(8,128)(2,1)} %get-tuple-element.75.refs_1_.refs_3_, ...), custom_call_target="tpu_custom_call" | custom-call | flops 6000000000 | tf_op jit(solution)/shard_map/weights/pallas_call | solution.py:176
  233.5 10.0 %input_back.1 = (bf16[256,1024]{1,0:T(8,128)(2,1)}, bf16[256,1024]{1,0:T(8,128)(2,1)}, bf16[256,1024]{1,0:T(8,128)(2,1)}, bf16[256,1024]{1,0:T(8,128)(2,1)}, f32[2,1024]{1,0:T(2,128)}) custom-call(bf16[128,1024]{1,0:T(8,128)(2,1)} %get-tuple-element.74.refs_0_.refs_2_, bf16[128,1024]{1,0:T(8,128)(2,1)} %get-tuple-element.75.refs_1_.refs_3_, ...), custom_call_target="tpu_custom_call" | custom-call | flops 6000000000 | tf_op jit(solution)/shard_map/input_back/pallas_call | solution.py:176
  248.6 2.5 all-to-all-start
  253.5 11.4 %all-to-all-done = f32[32,1,128]{2,1,0:T(1,128)S(1)} async-done(((f32[32,1,128]{2,1,0:T(1,128)}), f32[32,1,128]{2,1,0:T(1,128)S(1)}, u32[]{:S(2)}, u32[]{:S(2)}) %all-to-all-start) | async-done | bytes 16416 | tf_op jit(solution)/shard_map/all_to_all | solution.py:952
  268.0 2.9 output.1
  271.7 2.8 token_grads.1
  274.5 2.4 finish_weights.1
  (209 shorter events, 79.1 us)
Async XLA Ops:
  7.2 51.5 %all-gather.4.cloned.1.call-start = ((), (), s32[]{:S(2)}) async-start(), calls=%async_computation.3 | async-start | bytes 3833856 | tf_op jit(solution)/shard_map/all_gather | solution.py:716
  12.2 97.5 %all-gather.6.cloned.1.call-start = ((), (), s32[]{:S(2)}) async-start(), calls=%async_computation.6 | async-start | bytes 5013504 | tf_op jit(solution)/shard_map/all_gather | solution.py:750
  19.4 11.6 %collective-permute-start.1 = (bf16[128,1024]{1,0:T(8,128)(2,1)}, bf16[128,1024]{1,0:T(8,128)(2,1)S(1)}, u32[]{:S(2)}, u32[]{:S(2)}) collective-permute-start(bf16[128,1024]{1,0:T(8,128)(2,1)} %get-tuple-element.75.refs_1_.refs_3_), channel_id=1, source_target_pairs={{0,8},{8,0},{16,24},{24,16},{1,9},{9,1},{17,25},{25,17},{2,10},{10... | collective-permute-start | bytes 786440 | tf_op jit(solution)/shard_map/ppermute | solution.py:559
  33.8 186.2 %reduce-scatter.3.cloned.1.call-start = ((), (), s32[]{:S(2)}) async-start(), calls=%async_computation.4 | async-start | bytes 5013504 | tf_op jit(solution)/shard_map/reduce_scatter | solution.py:846
  36.8 15.8 %collective-permute-start.7 = (bf16[272,1024]{1,0:T(8,128)(2,1)}, bf16[272,1024]{1,0:T(8,128)(2,1)S(1)}, u32[]{:S(2)}, u32[]{:S(2)}) collective-permute-start(bf16[272,1024]{1,0:T(8,128)(2,1)} %pack_grad.1), channel_id=1, source_target_pairs={{0,16},{8,24},{16,0},{24,8},{1,17},{9,25},{17,1},{25,9},{2,18},{10... | collective-permute-start | bytes 1671176 | tf_op jit(solution)/shard_map/ppermute | solution.py:559
  37.2 17.0 %collective-permute-start.6 = (bf16[272,1024]{1,0:T(8,128)(2,1)}, bf16[272,1024]{1,0:T(8,128)(2,1)S(1)}, u32[]{:S(2)}, u32[]{:S(2)}) collective-permute-start(bf16[272,1024]{1,0:T(8,128)(2,1)} %pack_grad.1), channel_id=1, source_target_pairs={{0,8},{8,0},{16,24},{24,16},{1,9},{9,1},{17,25},{25,17},{2,10},{10... | collective-permute-start | bytes 1671176 | tf_op jit(solution)/shard_map/ppermute | solution.py:559
  39.0 19.6 %collective-permute-start.4 = (bf16[128,1024]{1,0:T(8,128)(2,1)S(1)}, bf16[128,1024]{1,0:T(8,128)(2,1)S(1)}, u32[]{:S(2)}, u32[]{:S(2)}) collective-permute-start(bf16[128,1024]{1,0:T(8,128)(2,1)S(1)} %copy-done.27), channel_id=1, source_target_pairs={{0,8},{8,0},{16,24},{24,16},{1,9},{9,1},{17,25},{25,17},{2,10},{10... | collective-permute-start | bytes 786440 | tf_op jit(solution)/shard_map/ppermute | solution.py:559
  39.5 19.1 %collective-permute-start.5 = (bf16[128,1024]{1,0:T(8,128)(2,1)S(1)}, bf16[128,1024]{1,0:T(8,128)(2,1)S(1)}, u32[]{:S(2)}, u32[]{:S(2)}) collective-permute-start(bf16[128,1024]{1,0:T(8,128)(2,1)S(1)} %copy-done.31), channel_id=1, source_target_pairs={{0,16},{8,24},{16,0},{24,8},{1,17},{9,25},{17,1},{25,9},{2,18},{10... | collective-permute-start | bytes 786440 | tf_op jit(solution)/shard_map/ppermute | solution.py:559
  52.6 15.2 %collective-permute-start.8 = (bf16[128,1024]{1,0:T(8,128)(2,1)S(1)}, bf16[128,1024]{1,0:T(8,128)(2,1)}, u32[]{:S(2)}, u32[]{:S(2)}) collective-permute-start(bf16[128,1024]{1,0:T(8,128)(2,1)S(1)} %slice.30), channel_id=1, source_target_pairs={{0,8},{8,0},{16,24},{24,16},{1,9},{9,1},{17,25},{25,17},{2,10},{10... | collective-permute-start | bytes 786440 | tf_op jit(solution)/shard_map/ppermute | solution.py:559
  54.2 13.6 %collective-permute-start.9 = (bf16[144,1024]{1,0:T(8,128)(2,1)S(1)}, bf16[144,1024]{1,0:T(8,128)(2,1)S(1)}, u32[]{:S(2)}, u32[]{:S(2)}) collective-permute-start(bf16[144,1024]{1,0:T(8,128)(2,1)S(1)} %slice.31), channel_id=1, source_target_pairs={{0,16},{8,24},{16,0},{24,8},{1,17},{9,25},{17,1},{25,9},{2,18},{10... | collective-permute-start | bytes 884744 | tf_op jit(solution)/shard_map/ppermute | solution.py:559
  78.8 16.0 %collective-permute-start.10 = (bf16[256,1024]{1,0:T(8,128)(2,1)}, bf16[256,1024]{1,0:T(8,128)(2,1)S(1)}, u32[]{:S(2)}, u32[]{:S(2)}) collective-permute-start(bf16[256,1024]{1,0:T(8,128)(2,1)} %get-tuple-element.81), channel_id=1, source_target_pairs={{0,24},{8,16},{16,8},{24,0},{1,25},{9,17},{17,9},{25,1},{2,26},{10... | collective-permute-start | bytes 1572872 | tf_op jit(solution)/shard_map/ppermute | solution.py:559
  81.4 20.0 %collective-permute-start.11 = (bf16[256,1024]{1,0:T(8,128)(2,1)}, bf16[256,1024]{1,0:T(8,128)(2,1)S(1)}, u32[]{:S(2)}, u32[]{:S(2)}) collective-permute-start(bf16[256,1024]{1,0:T(8,128)(2,1)} %get-tuple-element.82), channel_id=1, source_target_pairs={{0,8},{8,0},{16,24},{24,16},{1,9},{9,1},{17,25},{25,17},{2,10},{10... | collective-permute-start | bytes 1572872 | tf_op jit(solution)/shard_map/ppermute | solution.py:559
  82.0 19.5 %collective-permute-start.12 = (bf16[256,1024]{1,0:T(8,128)(2,1)}, bf16[256,1024]{1,0:T(8,128)(2,1)S(1)}, u32[]{:S(2)}, u32[]{:S(2)}) collective-permute-start(bf16[256,1024]{1,0:T(8,128)(2,1)} %get-tuple-element.83), channel_id=1, source_target_pairs={{0,16},{8,24},{16,0},{24,8},{1,17},{9,25},{17,1},{25,9},{2,18},{10... | collective-permute-start | bytes 1572872 | tf_op jit(solution)/shard_map/ppermute | solution.py:559
  105.6 12.2 %collective-permute-start.15 = (bf16[128,1024]{1,0:T(8,128)(2,1)}, bf16[128,1024]{1,0:T(8,128)(2,1)S(1)}, u32[]{:S(2)}, u32[]{:S(2)}) collective-permute-start(bf16[128,1024]{1,0:T(8,128)(2,1)} %get-tuple-element.85.refs_0_.refs_11_), channel_id=1, source_target_pairs={{0,16},{8,24},{16,0},{24,8},{1,17},{9,25},{17,1},{25,9},{2,18},{10... | collective-permute-start | bytes 786440 | tf_op jit(solution)/shard_map/ppermute | solution.py:559
  106.9 20.4 %collective-permute-start.13 = (bf16[128,1024]{1,0:T(8,128)(2,1)}, bf16[128,1024]{1,0:T(8,128)(2,1)S(1)}, u32[]{:S(2)}, u32[]{:S(2)}) collective-permute-start(bf16[128,1024]{1,0:T(8,128)(2,1)} %get-tuple-element.85.refs_0_.refs_11_), channel_id=1, source_target_pairs={{0,8},{8,0},{16,24},{24,16},{1,9},{9,1},{17,25},{25,17},{2,10},{10... | collective-permute-start | bytes 786440 | tf_op jit(solution)/shard_map/ppermute | solution.py:559
  108.4 19.0 %collective-permute-start.16 = (bf16[128,1024]{1,0:T(8,128)(2,1)}, bf16[128,1024]{1,0:T(8,128)(2,1)S(1)}, u32[]{:S(2)}, u32[]{:S(2)}) collective-permute-start(bf16[128,1024]{1,0:T(8,128)(2,1)} %get-tuple-element.86.refs_1_.refs_12_), channel_id=1, source_target_pairs={{0,16},{8,24},{16,0},{24,8},{1,17},{9,25},{17,1},{25,9},{2,18},{10... | collective-permute-start | bytes 786440 | tf_op jit(solution)/shard_map/ppermute | solution.py:559
  109.2 11.6 %collective-permute-start.14 = (bf16[128,1024]{1,0:T(8,128)(2,1)}, bf16[128,1024]{1,0:T(8,128)(2,1)S(1)}, u32[]{:S(2)}, u32[]{:S(2)}) collective-permute-start(bf16[128,1024]{1,0:T(8,128)(2,1)} %get-tuple-element.86.refs_1_.refs_12_), channel_id=1, source_target_pairs={{0,8},{8,0},{16,24},{24,16},{1,9},{9,1},{17,25},{25,17},{2,10},{10... | collective-permute-start | bytes 786440 | tf_op jit(solution)/shard_map/ppermute | solution.py:559
  143.4 11.9 %collective-permute-start.22 = (bf16[256,1024]{1,0:T(8,128)(2,1)}, bf16[256,1024]{1,0:T(8,128)(2,1)S(1)}, u32[]{:S(2)}, u32[]{:S(2)}) collective-permute-start(bf16[256,1024]{1,0:T(8,128)(2,1)} %get-tuple-element.92.refs_10_), channel_id=1, source_target_pairs={{0,8},{8,0},{16,24},{24,16},{1,9},{9,1},{17,25},{25,17},{2,10},{10... | collective-permute-start | bytes 1572872 | tf_op jit(solution)/shard_map/ppermute | solution.py:559
  144.5 11.8 %collective-permute-start.23 = (bf16[256,1024]{1,0:T(8,128)(2,1)}, bf16[256,1024]{1,0:T(8,128)(2,1)S(1)}, u32[]{:S(2)}, u32[]{:S(2)}) collective-permute-start(bf16[256,1024]{1,0:T(8,128)(2,1)} %get-tuple-element.93.refs_11_), channel_id=1, source_target_pairs={{0,16},{8,24},{16,0},{24,8},{1,17},{9,25},{17,1},{25,9},{2,18},{10... | collective-permute-start | bytes 1572872 | tf_op jit(solution)/shard_map/ppermute | solution.py:559
  167.0 107.5 %reduce-scatter.5.cloned.1.call-start = ((), (), s32[]{:S(2)}) async-start(), calls=%async_computation.5 | async-start | bytes 3833856 | tf_op jit(solution)/shard_map/reduce_scatter | solution.py:936
  168.0 11.6 %collective-permute-start.24 = (bf16[256,1024]{1,0:T(8,128)(2,1)S(1)}, bf16[256,1024]{1,0:T(8,128)(2,1)S(1)}, u32[]{:S(2)}, u32[]{:S(2)}) collective-permute-start(bf16[256,1024]{1,0:T(8,128)(2,1)S(1)} %copy-done.22), channel_id=1, source_target_pairs={{0,24},{8,16},{16,8},{24,0},{1,25},{9,17},{17,9},{25,1},{2,26},{10... | collective-permute-start | bytes 1572872 | tf_op jit(solution)/shard_map/ppermute | solution.py:559
  184.5 14.2 %collective-permute-start.27 = (bf16[128,1024]{1,0:T(8,128)(2,1)}, bf16[128,1024]{1,0:T(8,128)(2,1)S(1)}, u32[]{:S(2)}, u32[]{:S(2)}) collective-permute-start(bf16[128,1024]{1,0:T(8,128)(2,1)} %get-tuple-element.108.refs_7_.refs_14_), channel_id=1, source_target_pairs={{0,8},{8,0},{16,24},{24,16},{1,9},{9,1},{17,25},{25,17},{2,10},{10... | collective-permute-start | bytes 786440 | tf_op jit(solution)/shard_map/ppermute | solution.py:559
  186.2 13.4 %collective-permute-start.30 = (bf16[128,1024]{1,0:T(8,128)(2,1)}, bf16[128,1024]{1,0:T(8,128)(2,1)S(1)}, u32[]{:S(2)}, u32[]{:S(2)}) collective-permute-start(bf16[128,1024]{1,0:T(8,128)(2,1)} %get-tuple-element.108.refs_7_.refs_14_), channel_id=1, source_target_pairs={{0,16},{8,24},{16,0},{24,8},{1,17},{9,25},{17,1},{25,9},{2,18},{10... | collective-permute-start | bytes 786440 | tf_op jit(solution)/shard_map/ppermute | solution.py:559
  187.7 32.2 %collective-permute-start.20 = (bf16[256,1024]{1,0:T(8,128)(2,1)S(1)}, bf16[256,1024]{1,0:T(8,128)(2,1)S(1)}, u32[]{:S(2)}, u32[]{:S(2)}) collective-permute-start(bf16[256,1024]{1,0:T(8,128)(2,1)S(1)} %copy-done.2), channel_id=1, source_target_pairs={{0,8},{8,0},{16,24},{24,16},{1,9},{9,1},{17,25},{25,17},{2,10},{10... | collective-permute-start | bytes 1572872 | tf_op jit(solution)/shard_map/ppermute | solution.py:559
  193.1 26.8 %collective-permute-start.21 = (bf16[256,1024]{1,0:T(8,128)(2,1)S(1)}, bf16[256,1024]{1,0:T(8,128)(2,1)S(1)}, u32[]{:S(2)}, u32[]{:S(2)}) collective-permute-start(bf16[256,1024]{1,0:T(8,128)(2,1)S(1)} %copy-done.1), channel_id=1, source_target_pairs={{0,16},{8,24},{16,0},{24,8},{1,17},{9,25},{17,1},{25,9},{2,18},{10... | collective-permute-start | bytes 1572872 | tf_op jit(solution)/shard_map/ppermute | solution.py:559
  193.9 16.7 %collective-permute-start.26 = (bf16[128,1024]{1,0:T(8,128)(2,1)S(1)}, bf16[128,1024]{1,0:T(8,128)(2,1)S(1)}, u32[]{:S(2)}, u32[]{:S(2)}) collective-permute-start(bf16[128,1024]{1,0:T(8,128)(2,1)S(1)} %collective-permute-done.25.refs_10_.refs_17_), channel_id=1, source_target_pairs={{0,8},{8,0},{16,24},{24,16},{1,9},{9,1},{17,25},{25,17},{2,10},{10... | collective-permute-start | bytes 786440 | tf_op jit(solution)/shard_map/ppermute | solution.py:559
  198.7 12.3 %collective-permute-start.28 = (bf16[128,1024]{1,0:T(8,128)(2,1)S(1)}, bf16[128,1024]{1,0:T(8,128)(2,1)S(1)}, u32[]{:S(2)}, u32[]{:S(2)}) collective-permute-start(bf16[128,1024]{1,0:T(8,128)(2,1)S(1)} %collective-permute-done.27.refs_9_.refs_16_), channel_id=1, source_target_pairs={{0,16},{8,24},{16,0},{24,8},{1,17},{9,25},{17,1},{25,9},{2,18},{10... | collective-permute-start | bytes 786440 | tf_op jit(solution)/shard_map/ppermute | solution.py:559
  232.1 34.7 %collective-permute-start.19 = (bf16[256,1024]{1,0:T(8,128)(2,1)S(1)}, bf16[256,1024]{1,0:T(8,128)(2,1)S(1)}, u32[]{:S(2)}, u32[]{:S(2)}) collective-permute-start(bf16[256,1024]{1,0:T(8,128)(2,1)S(1)} %copy-done), channel_id=1, source_target_pairs={{0,24},{8,16},{16,8},{24,0},{1,25},{9,17},{17,9},{25,1},{2,26},{10... | collective-permute-start | bytes 1572872 | tf_op jit(solution)/shard_map/ppermute | solution.py:559
  243.4 23.4 %collective-permute-start.31 = (bf16[256,1024]{1,0:T(8,128)(2,1)}, bf16[256,1024]{1,0:T(8,128)(2,1)S(1)}, u32[]{:S(2)}, u32[]{:S(2)}) collective-permute-start(bf16[256,1024]{1,0:T(8,128)(2,1)} %get-tuple-element.118), channel_id=1, source_target_pairs={{0,8},{8,0},{16,24},{24,16},{1,9},{9,1},{17,25},{25,17},{2,10},{10... | collective-permute-start | bytes 1572872 | tf_op jit(solution)/shard_map/ppermute | solution.py:559
  244.0 22.9 %collective-permute-start.32 = (bf16[256,1024]{1,0:T(8,128)(2,1)}, bf16[256,1024]{1,0:T(8,128)(2,1)S(1)}, u32[]{:S(2)}, u32[]{:S(2)}) collective-permute-start(bf16[256,1024]{1,0:T(8,128)(2,1)} %get-tuple-element.119), channel_id=1, source_target_pairs={{0,16},{8,24},{16,0},{24,8},{1,17},{9,25},{17,1},{25,9},{2,18},{10... | collective-permute-start | bytes 1572872 | tf_op jit(solution)/shard_map/ppermute | solution.py:559
  245.7 25.2 %collective-permute-start.33 = (bf16[256,1024]{1,0:T(8,128)(2,1)}, bf16[256,1024]{1,0:T(8,128)(2,1)S(1)}, u32[]{:S(2)}, u32[]{:S(2)}) collective-permute-start(bf16[256,1024]{1,0:T(8,128)(2,1)} %get-tuple-element.122), channel_id=1, source_target_pairs={{0,24},{8,16},{16,8},{24,0},{1,25},{9,17},{17,9},{25,1},{2,26},{10... | collective-permute-start | bytes 1572872 | tf_op jit(solution)/shard_map/ppermute | solution.py:559
  248.6 16.3 %all-to-all-start = ((f32[32,1,128]{2,1,0:T(1,128)}), f32[32,1,128]{2,1,0:T(1,128)S(1)}, u32[]{:S(2)}, u32[]{:S(2)}) async-start(f32[32,1,128]{2,1,0:T(1,128)} %reshape.74), calls=%async_computation.1 | async-start | bytes 32768 | tf_op jit(solution)/shard_map/all_to_all | solution.py:952
  (56 other events, 274.7 us)
Sparse Core Ops, SparseCore 0:
  12.4 43.1 all-gather.3
  57.2 48.3 all-gather.5
  167.1 49.4 reduce-scatter.2
  231.2 39.9 reduce-scatter.4
where the time goes:
time: 287 us
  Pallas kernels  124 us (43%)
  waiting for transfers between devices  81.7 us (28%)
  starting transfers between devices  37.4 us (13%)
  local copies, waits for them, and re-layouts  23.7 us (8%)
  between operations  14.5 us (5%)
  other arithmetic  5.69 us (2%)
    pallas_call x22, Pallas kernels, call(): pl.pallas_call(kernel, name=name, out_shape=shapes[0] if single else shap...  124 us
    ppermute x34, waiting for transfers between devices, to_head(): return lax.ppermute(value, 'head', [(i, i ^ flip) for i in range(n)])  70.2 us
    ppermute x34, starting transfers between devices, to_head(): return lax.ppermute(value, 'head', [(i, i ^ flip) for i in range(n)])  34.7 us
    unnamed x99, local copies, waits for them, and re-layouts  19.7 us
    all_to_all x1, waiting for transfers between devices, shards(): lax.all_to_all(norms, ('head', 'dp'), split_axis=0, concat_axis=0, tiled=...  11.4 us
  transfers between devices with their start and end apart: 39, of which 21 were waited for; matrix products, arithmetic and copies ran while one was open for 4% of the time, Pallas kernels for 31%

commit v1 on v0

--- a/solution.py
+++ b/solution.py
@@ -205,8 +205,8 @@
     out[:, 2 * size : 3 * LANES] = jnp.zeros((q.ref.shape[0], LANES), BF16)
     out[:, :size] = q[...]
     out[:, size : 2 * size] = k[...]
-    out[:, 2 * size : 2 * size + kinds] = vsel[...]
-    out[:, 2 * size + kinds : 2 * size + 2 * kinds] = osel[...]
+    out[:, 2 * size : 2 * size + kinds] = vsel[...].T
+    out[:, 2 * size + kinds : 2 * size + 2 * kinds] = osel[...].T
     out[:, 3 * LANES : 3 * LANES + kinds * size] = v[...]
 
 
@@ -219,17 +219,6 @@
 
 def stack_kernel(pieces, out):
     out[...] = pieces[...]
-
-
-def split_copy_kernel(a, b, top, bottom):
-    top[...] = a[...]
-    bottom[...] = b[...]
-
-
-def split_kernel(rows, top, bottom):
-    half = top.ref.shape[0]
-    top[...] = rows[:half, :]
-    bottom[...] = rows[half:, :]
 
 
 def residual_kernel(*refs):
@@ -266,9 +255,9 @@
     at = 3 * LANES
     q[...] = found[:, :size].astype(F32) * scale
     k[...] = found[:, size : 2 * size].astype(F32)
-    both = found[:, 2 * size : at].astype(F32)
-    vsel[...] = both[:, :kinds]
-    osel[...] = both[:, kinds : 2 * kinds]
+    both = found[:, 2 * size : at].astype(F32).T
+    vsel[...] = both[:kinds, :]
+    osel[...] = both[kinds : 2 * kinds, :]
     v[...] = found[:, at : at + kinds * size].astype(F32)
     o[...] = found[:, at + kinds * size :].astype(F32).T
 
@@ -287,9 +276,7 @@
     )
 
 
-def project_kernel(own, scale, kinds, size, x, gain, bias, info, w, q, k, v, ev, gate):
-    for value in (x, gain, bias, info, w):
-        value.ready()
+def project_block(own, scale, kinds, size, x, gain, bias, info, w, q, k, v, ev, gate):
 
     def block(b):
         at = block_at(b, own)
@@ -313,17 +300,24 @@
             value = value + found[:, e : e + 1] * experts[:, e * size : (e + 1) * size]
         v[at, :] = value.astype(BF16)
 
-    repeat(4, block)
-    ev.blocks_sent(4, own)
+    return block
 
 
 def visible(info, code):
     return (code >= info[:, 0:1]) & (code <= info[:, 1:2])
 
 
-def attend_kernel(own, kinds, size, q, k, v, info, code, gate, w, parts, att, lse, mixed):
-    for value in (q, k, v, info, code, gate, w):
+def forward_kernel(
+    own, scale, kinds, size, x, gain, bias, info, w_in, code, w, parts, q, k, v, ev, gate, att, lse, mixed
+):
+    for value in (x, gain, bias, info, w_in):
         value.ready()
+    repeat(4, project_block(own, scale, kinds, size, x, gain, bias, info, w_in, q, k, v, ev, gate))
+    ev.blocks_sent(4, own)
+    for value in (code, w):
+        value.ready()
+    for value in (q, k, v, gate):
+        value.send()
 
     def block(b):
         at = block_at(b, own)
@@ -417,22 +411,28 @@
 def expert_grad_kernel(count, hidden, gated, grad, dpre, rows, *refs):
     routes, out = refs[:-1], refs[-1]
     pair = WIDE // hidden
-    for value in (gated, grad, dpre, rows, *routes):
+    for value in (gated, grad):
+        value.ready()
+
+    def lower(c):
+        down = tn(gated.ref[:, block_at(c, WIDE)], grad.ref[...]).astype(BF16)
+        for j in range(pair):
+            out[c * pair + j, hidden : 2 * hidden, :] = down[j * hidden : (j + 1) * hidden]
+
+    repeat(count // pair, lower)
+    for value in (dpre, rows, *routes):
         value.ready()
     for e in range(count):
         route = sum(r.ref[e : e + 1, :] for r in routes)
         out[e, 2 * hidden :, :] = jnp.broadcast_to(route, (PAD, route.shape[1])).astype(BF16)
 
-    def block(c):
-        col = block_at(c, WIDE)
-        down = tn(gated.ref[:, col], grad.ref[...]).astype(BF16)
-        up = tn(dpre.ref[:, col], rows.ref[...]).astype(BF16)
+    def upper(c):
+        up = tn(dpre.ref[:, block_at(c, WIDE)], rows.ref[...]).astype(BF16)
         for j in range(pair):
             out[c * pair + j, :hidden, :] = up[j * hidden : (j + 1) * hidden]
-            out[c * pair + j, hidden : 2 * hidden, :] = down[j * hidden : (j + 1) * hidden]
         out.block(c, pair).start()
 
-    repeat(count // pair, block)
+    repeat(count // pair, upper)
     out.blocks_sent(count // pair, pair)
 
 
@@ -512,22 +512,20 @@
     repeat(4, block)
 
 
-def weight_kernel(din, dexp, x, gate, gain, bias, d_rows, mixed, out):
+def weight_kernel(d_rows, mixed, x, gate, gain, bias, din, dexp, out):
     width = x.ref.shape[1]
-    for value in (din, dexp, x, gate, gain, bias, d_rows, mixed):
-        value.ready()
-    mean, spread = gate.ref[:, MEAN : MEAN + 1], gate.ref[:, SPREAD : SPREAD + 1]
     first_end = din.ref.shape[1]
     second_end = first_end + dexp.ref.shape[1]
-
-    for first in range(0, width, WIDE):
-        at = slice(first, first + WIDE)
-        rows = x.ref[:, at]
-        normed = (rows.astype(F32) - mean) * spread * gain.ref[:, at] + bias.ref[:, at]
-        out[at, :first_end] = tn(normed.astype(BF16), din.ref[...]).astype(BF16)
-        out[at, first_end:second_end] = tn(rows, dexp.ref[...]).astype(BF16)
-        out[at, second_end:] = tn(d_rows.ref[:, at], mixed.ref[...]).astype(BF16)
-        out.send(first, WIDE)
+    cuts = [slice(first, first + WIDE) for first in range(0, width, WIDE)]
+    for at in cuts:
+        out[at, second_end:] = tn(d_rows[:, at], mixed[...]).astype(BF16)
+    mean, spread = gate[:, MEAN : MEAN + 1], gate[:, SPREAD : SPREAD + 1]
+    for at in cuts:
+        rows = x[:, at]
+        normed = (rows.astype(F32) - mean) * spread * gain[:, at] + bias[:, at]
+        out[at, :first_end] = tn(normed.astype(BF16), din[...]).astype(BF16)
+        out[at, first_end:second_end] = tn(rows, dexp[...]).astype(BF16)
+        out.send(at.start, WIDE)
 
 
 def input_grad_kernel(own, scale, size, x, din, gate, gain, w, dexp, outs, norm):
@@ -559,27 +557,11 @@
     return lax.ppermute(value, "head", [(i, i ^ flip) for i in range(n)])
 
 
-def near_rows(top, bottom):
+def spread_rows(top, bottom):
     y_top, x_bottom = to_head(top, 2), to_head(bottom, 1)
     y_bottom, x_top = to_head(bottom, 2), to_head(top, 1)
-    return [[x_top, x_bottom], [y_top, y_bottom]]
-
-
-def far_rows(near):
-    return [to_head(near[1][0], 1), to_head(near[0][1], 2)]
-
-
-def spread_rows(top, bottom):
-    near = near_rows(top, bottom)
-    return [[top, bottom], *near, far_rows(near)]
-
-
-def far_rows_after(near, after):
-    half = shape(near[0][0].shape, BF16)
-    passed = call(
-        "relay", 1, split_copy_kernel, [half, half], [near[1][0], near[0][1]], after
-    )
-    return [to_head(passed[0], 1), to_head(passed[1], 2)]
+    far_top, far_bottom = to_head(y_top, 1), to_head(x_bottom, 2)
+    return [[top, bottom], [x_top, x_bottom], [y_top, y_bottom], [far_top, far_bottom]]
 
 
 def flat(blocks):
@@ -616,15 +598,12 @@
     return [list(got[:n]), [got[n]], [got[n + 1]], got[-2], got[-1]]
 
 
-def expert_chunk(rows, spread, grads, hits, weights, router, gain, bias, moves=()):
+def expert_chunk(rows, grads, hits, weights, router, gain, bias, moves=()):
     count, hidden = weights.shape[0], (weights.shape[1] - PAD) // 2
     width, own = weights.shape[2], hits[0].shape[0]
     shared = (weights, router, gain, bias)
     first = expert_blocks("experts_own", rows[:1], grads[:1], hits[:1], *shared)
-    rows = [rows[0], *spread(first[0])]
-    near = expert_blocks(
-        "experts_near", rows[1:3], grads[1:3], hits[1:3], *shared, (first[0][0], *rows[3])
-    )
+    near = expert_blocks("experts_near", rows[1:3], grads[1:3], hits[1:3], *shared, first[0])
     far = expert_blocks("experts_far", rows[3:], grads[3:], hits[3:], *shared, near[0])
     back, dpre, gated = (first[i] + near[i] + far[i] for i in range(3))
     norm = first[3] + near[3] + far[3]
@@ -708,16 +687,13 @@
             query_projection,
             key_projection,
             value_experts[0],
-            value_selector,
-            output_selector,
+            value_selector.T,
+            output_selector.T,
             output_experts[0],
         ],
     )
     all_in = lax.all_gather(all_own, "dp", axis=0, tiled=True)
     in_all, out_all = Part(all_in, 0, last), Part(all_in, last, mixed_width)
-    x = spread_rows(
-        *call("split_rows", 1, split_kernel, [shape((half, width), BF16)] * 2, [x_own])
-    )
     experts = 4 * n_data
     hot = jnp.sum(jax.nn.one_hot(feedforward_route[0], experts, dtype=BF16), 1)
     hot_rows = own * experts // width
@@ -725,14 +701,20 @@
     hot = jnp.concatenate([hot, jnp.zeros((-hot_rows % PAD, width), BF16)])
     grad_sent = call(
         "pack_grad",
-        1,
+        2,
         stack_kernel,
         shape((own + hot.shape[0], width), BF16),
         [Rows([grad_own, hot])],
     )
-    near_x, near_y = to_head(grad_sent, 1), to_head(grad_sent, 2)
-    far_top, far_bottom = to_head(near_y[:half], 1), to_head(near_x[half:], 2)
-    grad = [[grad_own], [near_x], [near_y], [far_top, far_bottom]]
+
+    def spread_whole(value):
+        near_x, near_y = to_head(value, 1), to_head(value, 2)
+        far = [to_head(near_y[:half], 1), to_head(near_x[half:], 2)]
+        return [near_x], [near_y], far
+
+    x = [[x_own], *spread_whole(x_own)]
+    grad = [[grad_own], *spread_whole(grad_sent)]
+    (near_x,), (near_y,), (_, far_bottom) = grad[1:]
 
     def hits_of(rows):
         found = rows[:hot_rows].reshape(own, experts)
@@ -745,7 +727,7 @@
         pack_experts_kernel,
         shape((2 * hidden + PAD, width), BF16),
         [expert_up_weight[0], expert_down_weight[0], feedforward_selector],
-        flat(x[1:3]),
+        [all_own, grad_sent],
     )
     ffn_all = lax.all_gather(ffn_own, "dp", axis=0, tiled=False)
     router = ffn_all[:, 2 * hidden]
@@ -767,26 +749,33 @@
     code = arranged(first_code + spots)[None]
     gain1, bias1 = attention_norm_gain[None], attention_norm_bias[None]
     gain2, bias2 = feedforward_norm_gain[None], feedforward_norm_bias[None]
-    query, key, value, experts_v, gate = call(
-        "project",
-        7,
-        functools.partial(project_kernel, own, scale, kinds, size),
-        [shape((length, size), BF16)] * 3
-        + [shape((length, mixed_width), BF16), shape((length, LANES), F32)],
-        [Rows(flat(x)), gain1, bias1, info, in_all],
-    )
-
-    part_own, part_x, part_y, part_far, att, lse, mixed = call(
-        "attend",
-        8,
-        functools.partial(attend_kernel, own, kinds, size),
-        [
-            Split(4, (own, width), BF16),
+    (
+        part_own,
+        part_x,
+        part_y,
+        part_far,
+        query,
+        key,
+        value,
+        experts_v,
+        gate,
+        att,
+        lse,
+        mixed,
+    ) = call(
+        "forward",
+        14,
+        functools.partial(forward_kernel, own, scale, kinds, size),
+        [Split(4, (own, width), BF16)]
+        + [shape((length, size), BF16)] * 3
+        + [
+            shape((length, mixed_width), BF16),
+            shape((length, LANES), F32),
             shape((length, size), F32),
             shape((length, LANES), F32),
             shape((length, mixed_width), BF16),
         ],
-        [query, key, value, info, code, gate, out_all],
+        [Rows(flat(x)), gain1, bias1, info, in_all, code, out_all],
         flat(grad[1:]),
     )
 
@@ -802,12 +791,11 @@
 
     parts = [to_head(part, flip) for part, flip in ((part_far, 3), (part_x, 1), (part_y, 2))]
     resid, top, bottom = residual("residual", [x_own, part_own, *parts])
-    near = near_rows(top, bottom)
+    rows = spread_rows(top, bottom)
 
     if n_data <= CHUNK:
         back, moved, gated, norm2, slabs = expert_chunk(
-            [[top, bottom]],
-            lambda after: [*near, far_rows_after(near, after)],
+            rows,
             grad,
             hits,
             ffn_all,
@@ -818,7 +806,6 @@
         )
     else:
         cut = lambda a: a.reshape((n_data // CHUNK, CHUNK) + a.shape[1:])
-        others = [*near, far_rows(near)]
         hit_cuts = [
             h.reshape(own, n_data // CHUNK, CHUNK).transpose(1, 0, 2) for h in hits
         ]
@@ -826,7 +813,7 @@
         def step(carry, item):
             hit, rt, w = item
             got_back, _, got_gated, got_norm, slab = expert_chunk(
-                [[top, bottom]], lambda _: others, grad, hit, w, rt, gain2, bias2
+                rows, grad, hit, w, rt, gain2, bias2
             )
             got_out = expert_out(got_gated, w, ())
             add = lambda old, new: [o + v.astype(F32) for o, v in zip(old, new)]
@@ -892,14 +879,14 @@
         weight_kernel,
         shape((width, 3 * LANES + 2 * mixed_width), BF16),
         [
-            d_in,
-            d_exp,
+            Rows(flat(d_pack)),
+            mixed,
             Rows(flat(x)),
             gate,
             gain1,
             bias1,
-            Rows(flat(d_pack)),
-            mixed,
+            d_in,
+            d_exp,
         ],
         (ffn_grads, *out_moved[1:]),
     )
@@ -941,8 +928,8 @@
         [
             shape((part, size), F32),
             shape((part, size), F32),
-            shape((part, kinds), F32),
-            shape((part, kinds), F32),
+            shape((kinds, part), F32),
+            shape((kinds, part), F32),
             shape((part, mixed_width), F32),
             shape((mixed_width, part), F32),
         ],
@@ -957,8 +944,8 @@
         norms,
         query_grad,
         key_grad,
-        value_sel,
-        output_sel,
+        value_sel.T,
+        output_sel.T,
         value_grad[None],
         output_grad[None],
         router_grad,

time: 287 us -> 273 us (0.951)
  Pallas kernels: 124 us -> 116 us
  waiting for transfers between devices: 81.7 us -> 75.3 us
  local copies, waits for them, and re-layouts: 23.7 us -> 17.3 us
  starting transfers between devices: 37.4 us -> 43.2 us
    pallas_call x22 -> x19, Pallas kernels: 124 us -> 116 us  [call(): pl.pallas_call(kernel, name=name, out_shape=shapes[0] if single else shap...]
    unnamed x99 -> x83, local copies, waits for them, and re-layouts: 19.7 us -> 12.6 us
    ppermute x34 -> x32, waiting for transfers between devices: 70.2 us -> 65.5 us  [to_head(): return lax.ppermute(value, 'head', [(i, i ^ flip) for i in range(n)])]
    ppermute x34 -> x32, starting transfers between devices: 34.7 us -> 37.7 us  [to_head(): return lax.ppermute(value, 'head', [(i, i ^ flip) for i in range(n)])]
  transfers between devices with their start and end apart: 39 -> 37, of which waited for: 21 -> 18; matrix products, arithmetic and copies ran while one was open for 4% -> 4% of each run, Pallas kernels for 31% -> 34%
where the time goes in v1:
time: 273 us; the launch traced here: 272 us
  Pallas kernels  116 us (42%)
  waiting for transfers between devices  75.3 us (28%)
  starting transfers between devices  43.2 us (16%)
  local copies, waits for them, and re-layouts  17.3 us (6%)
  between operations  14.4 us (5%)
  other arithmetic  5.69 us (2%)
    pallas_call x19, Pallas kernels, call(): pl.pallas_call(kernel, name=name, out_shape=shapes[0] if single else shap...  116 us
    ppermute x32, waiting for transfers between devices, to_head(): return lax.ppermute(value, 'head', [(i, i ^ flip) for i in range(n)])  65.5 us
    ppermute x32, starting transfers between devices, to_head(): return lax.ppermute(value, 'head', [(i, i ^ flip) for i in range(n)])  37.7 us
    unnamed x83, local copies, waits for them, and re-layouts  12.6 us
    all_to_all x1, waiting for transfers between devices, shards(): lax.all_to_all(norms, ('head', 'dp'), split_axis=0, concat_axis=0, tiled=...  9.63 us
  transfers between devices with their start and end apart: 37, of which 18 were waited for; matrix products, arithmetic and copies ran while one was open for 4% of the time, Pallas kernels for 34%

profile of v1, /device:TPU:0, one launch (start us, length us, event | category | flops | bytes accessed | tf_op | source)
XLA Modules:
  0.0 272.0 jit_solution(5816863767098841700)
XLA Ops:
  7.2 2.3 pack_weights.1.refs_3_
  12.6 2.0 pack_experts.1
  14.7 3.0 %collective-permute-start.1 = (bf16[256,1024]{1,0:T(8,128)(2,1)S(1)}, bf16[256,1024]{1,0:T(8,128)(2,1)S(1)}, u32[]{:S(2)}, u32[]{:S(2)}) collective-permute-start(bf16[256,1024]{1,0:T(8,128)(2,1)S(1)} %bitcast.64), channel_id=1, source_target_pairs={{0,16},{8,24},{16,0},{24,8},{1,17},{9,25},{17,1},{25,9},{2,18},{10... | collective-permute-start | bytes 1572872 | tf_op jit(solution)/shard_map/ppermute | solution.py:557
  20.0 10.5 %collective-permute-done.1.refs_2_.refs_11_ = bf16[256,1024]{1,0:T(8,128)(2,1)S(1)} collective-permute-done((bf16[256,1024]{1,0:T(8,128)(2,1)S(1)}, bf16[256,1024]{1,0:T(8,128)(2,1)S(1)}, u32[]{:S(2)}, u32[]{:S(2)}) %collective-permute-start.1) | collective-permute-done | bytes 524320 | tf_op jit(solution)/shard_map/ppermute | solution.py:557
  30.5 2.1 collective-permute-start.2
  34.2 8.2 %collective-permute-done.5.refs_12_.refs_11_.refs_5_ = bf16[272,1024]{1,0:T(8,128)(2,1)S(1)} collective-permute-done((bf16[272,1024]{1,0:T(8,128)(2,1)}, bf16[272,1024]{1,0:T(8,128)(2,1)S(1)}, u32[]{:S(2)}, u32[]{:S(2)}) %collective-permute-start.5) | collective-permute-done | bytes 557088 | tf_op jit(solution)/shard_map/ppermute | solution.py:557
  42.5 2.1 collective-permute-start.6
  47.9 2.4 collective-permute-done.2.refs_3_.refs_12_
  50.3 4.1 %collective-permute-done.6.refs_13_.refs_7_.refs_6_ = bf16[128,1024]{1,0:T(8,128)(2,1)} collective-permute-done((bf16[128,1024]{1,0:T(8,128)(2,1)S(1)}, bf16[128,1024]{1,0:T(8,128)(2,1)}, u32[]{:S(2)}, u32[]{:S(2)}) %collective-permute-start.6) | collective-permute-done | bytes 262176 | tf_op jit(solution)/shard_map/ppermute | solution.py:557
  54.5 15.5 %forward.1 = (bf16[256,1024]{1,0:T(8,128)(2,1)}, bf16[256,1024]{1,0:T(8,128)(2,1)}, bf16[256,1024]{1,0:T(8,128)(2,1)}, bf16[256,1024]{1,0:T(8,128)(2,1)}, bf16[1...) custom-call(bf16[256,1024]{1,0:T(8,128)(2,1)} %bitcast.60, ...), custom_call_target="tpu_custom_call" | custom-call | flops 14000000000 | tf_op jit(solution)/shard_map/forward/pallas_call | solution.py:176
  73.6 12.5 %collective-permute-done.8.refs_2_ = bf16[256,1024]{1,0:T(8,128)(2,1)S(1)} collective-permute-done((bf16[256,1024]{1,0:T(8,128)(2,1)}, bf16[256,1024]{1,0:T(8,128)(2,1)S(1)}, u32[]{:S(2)}, u32[]{:S(2)}) %collective-permute-start.8) | collective-permute-done | bytes 524320 | tf_op jit(solution)/shard_map/ppermute | solution.py:557
  86.1 9.4 %collective-permute-done.9.refs_3_ = bf16[256,1024]{1,0:T(8,128)(2,1)S(1)} collective-permute-done((bf16[256,1024]{1,0:T(8,128)(2,1)}, bf16[256,1024]{1,0:T(8,128)(2,1)S(1)}, u32[]{:S(2)}, u32[]{:S(2)}) %collective-permute-start.9) | collective-permute-done | bytes 524320 | tf_op jit(solution)/shard_map/ppermute | solution.py:557
  96.5 3.2 %residual.1 = (f32[256,1024]{1,0:T(8,128)}, bf16[128,1024]{1,0:T(8,128)(2,1)}, bf16[128,1024]{1,0:T(8,128)(2,1)}) custom-call(bf16[256,1024]{1,0:T(8,128)(2,1)} %bitcast.61, bf16[256,1024]{1,0:T(8,128)(2,1)} %get-tuple-element.70.refs_1_, bf16[256,1024]{1,0:T(8,128)(2,1)} %copy-done.25, bf16[256,1024]{1,0:T(8,128)(2,1)} %copy-done.26, ...), custom_call_target="tpu_custom_call" | custom-call | flops 2000000000 | tf_op jit(solution)/shard_map/residual/pallas_call | solution.py:176
  113.0 6.5 %experts_own.1 = (bf16[256,1024]{1,0:T(8,128)(2,1)}, bf16[256,1024]{1,0:T(8,128)(2,1)}, bf16[256,1024]{1,0:T(8,128)(2,1)}, f32[2,1024]{1,0:T(2,128)}, f32[8,1024]{1,0:T(8,128)}) custom-call(bf16[128,1024]{1,0:T(8,128)(2,1)} %get-tuple-element.75.refs_0_.refs_11_, bf16[128,1024]{1,0:T(8,128)(2,1)} %get-tuple-element.76.refs_1_.refs_12_, f32[1,1024]{1,0:T(1,128)} %bitcast.70, ...), custom_call_target="tpu_custom_call" | custom-call | flops 5000000000 | tf_op jit(solution)/shard_map/experts_own/pallas_call | solution.py:176
  120.3 10.5 %experts_near.1 = (bf16[256,1024]{1,0:T(8,128)(2,1)}, bf16[256,1024]{1,0:T(8,128)(2,1)}, bf16[512,1024]{1,0:T(8,128)(2,1)}, bf16[512,1024]{1,0:T(8,128)(2,1)}, f32[2,1024]{1,0:T(2,128)}, /*index=5*/f32[8,1024]{1,0:T(8,128)}) custom-call(bf16[128,1024]{1,0:T(8,128)(2,1)} %copy-done.30, bf16[128,1024]{1,0:T(8,128)(2,1)} %copy-done.29, ...), custom_call_target="tpu_custom_call" | custom-call | flops 8000000000 | tf_op jit(solution)/shard_map/experts_near/pallas_call | solution.py:176
  135.6 6.6 %experts_far.1 = (bf16[256,1024]{1,0:T(8,128)(2,1)}, bf16[256,1024]{1,0:T(8,128)(2,1)}, bf16[256,1024]{1,0:T(8,128)(2,1)}, f32[2,1024]{1,0:T(2,128)}, f32[8,1024]{1,0:T(8,128)}) custom-call(bf16[128,1024]{1,0:T(8,128)(2,1)} %copy-done.34, bf16[128,1024]{1,0:T(8,128)(2,1)} %copy-done.37, f32[1,1024]{1,0:T(1,128)} %bitcast.72, f32[1,1024]{1,0:T(1,128)} %bitcast.75, ...), custom_call_target="tpu_custom_call" | custom-call | flops 5000000000 | tf_op jit(solution)/shard_map/experts_far/pallas_call | solution.py:176
  144.3 10.7 %experts_weights.1.refs_5_ = bf16[8,272,1024]{2,1,0:T(8,128)(2,1)} custom-call(bf16[256,1024]{1,0:T(8,128)(2,1)} %get-tuple-element.77.refs_0_, bf16[512,1024]{1,0:T(8,128)(2,1)} %get-tuple-element.79.refs_1_, bf16[256,1024]{1,0:T(8,128)(2,1)} %get-tuple-element.82.refs_2_, bf16[256,1024]{1,0:T(8,128)(2,1)} %bitcast.39, bf16[272,1024]{1,0:T(8,128)(2,1)} %copy-done.6, ...), custom_call_target="tpu_custom_call" | custom-call | flops 8000000000 | tf_op jit(solution)/shard_map/experts_weights/pallas_call | solution.py:176
  157.4 6.5 %experts_out.1 = (bf16[256,1024]{1,0:T(8,128)(2,1)}, bf16[256,1024]{1,0:T(8,128)(2,1)}, bf16[256,1024]{1,0:T(8,128)(2,1)}, bf16[256,1024]{1,0:T(8,128)(2,1)}) custom-call(bf16[256,1024]{1,0:T(8,128)(2,1)} %get-tuple-element.77.refs_0_, bf16[512,1024]{1,0:T(8,128)(2,1)} %get-tuple-element.79.refs_1_, bf16[256,1024]{1,0:T(8,128)(2,1)} %get-tuple-element.82.refs_2_, ...), custom_call_target="tpu_custom_call" | custom-call | flops 12000000000 | tf_op jit(solution)/shard_map/experts_out/pallas_call | solution.py:176
  163.9 4.1 %collective-permute-done.22.refs_4_ = bf16[256,1024]{1,0:T(8,128)(2,1)S(1)} collective-permute-done((bf16[256,1024]{1,0:T(8,128)(2,1)S(1)}, bf16[256,1024]{1,0:T(8,128)(2,1)S(1)}, u32[]{:S(2)}, u32[]{:S(2)}) %collective-permute-start.22) | collective-permute-done | bytes 524320 | tf_op jit(solution)/shard_map/ppermute | solution.py:557
  168.8 3.3 %residual_back.1 = (f32[256,1024]{1,0:T(8,128)}, bf16[128,1024]{1,0:T(8,128)(2,1)}, bf16[128,1024]{1,0:T(8,128)(2,1)}) custom-call(bf16[256,1024]{1,0:T(8,128)(2,1)} %bitcast.40, bf16[256,1024]{1,0:T(8,128)(2,1)} %get-tuple-element.78.refs_13_.refs_1_, bf16[256,1024]{1,0:T(8,128)(2,1)} %copy-done.3, bf16[256,1024]{1,0:T(8,128)(2,1)} %copy-done.4, ...), custom_call_target="tpu_custom_call" | custom-call | flops 2000000000 | tf_op jit(solution)/shard_map/residual_back/pallas_call | solution.py:176
  177.5 4.1 %collective-permute-done.27.refs_8_.refs_2_ = bf16[128,1024]{1,0:T(8,128)(2,1)S(1)} collective-permute-done((bf16[128,1024]{1,0:T(8,128)(2,1)}, bf16[128,1024]{1,0:T(8,128)(2,1)S(1)}, u32[]{:S(2)}, u32[]{:S(2)}) %collective-permute-start.27) | collective-permute-done | bytes 262176 | tf_op jit(solution)/shard_map/ppermute | solution.py:557
  183.7 3.6 %collective-permute-done.25.refs_9_.refs_3_ = bf16[128,1024]{1,0:T(8,128)(2,1)S(1)} collective-permute-done((bf16[128,1024]{1,0:T(8,128)(2,1)}, bf16[128,1024]{1,0:T(8,128)(2,1)S(1)}, u32[]{:S(2)}, u32[]{:S(2)}) %collective-permute-start.25) | collective-permute-done | bytes 262176 | tf_op jit(solution)/shard_map/ppermute | solution.py:557
  189.2 9.3 %attend_back.1 = (bf16[768,128]{1,0:T(8,128)(2,1)}, f32[1024,128]{1,0:T(8,128)}, f32[1024,128]{1,0:T(8,128)}, f32[1024,128]{1,0:T(8,128)}) custom-call(bf16[1024,128]{1,0:T(8,128)(2,1)} %get-tuple-element.87.refs_0_, bf16[1024,128]{1,0:T(8,128)(2,1)} %get-tuple-element.88.refs_1_, s32[1024,8]{1,0:T(8,128)} %copy.45.refs_7_.refs_2_, s32[1,1024]{1,0:T(1,128)} %bitcast.49, ...), custom_call_target="tpu_custom_call" | custom-call | flops 6000000000 | tf_op jit(solution)/shard_map/attend_back/pallas_call | solution.py:176
  200.9 8.1 %attend_last.1 = (bf16[1024,384]{1,0:T(8,128)(2,1)}, bf16[1024,640]{1,0:T(8,128)(2,1)}) custom-call(bf16[1024,128]{1,0:T(8,128)(2,1)} %get-tuple-element.87.refs_0_, bf16[1024,128]{1,0:T(8,128)(2,1)} %get-tuple-element.88.refs_1_, s32[1024,8]{1,0:T(8,128)} %copy.45.refs_7_.refs_2_, s32[1,1024]{1,0:T(1,128)} %bitcast.50, ...), custom_call_target="tpu_custom_call" | custom-call | flops 5000000000 | tf_op jit(solution)/shard_map/attend_last/pallas_call | solution.py:176
  210.1 9.4 %weights.1.refs_10_ = bf16[1024,1664]{1,0:T(8,128)(2,1)} custom-call(bf16[128,1024]{1,0:T(8,128)(2,1)} %get-tuple-element.97.refs_6_.refs_0_, bf16[128,1024]{1,0:T(8,128)(2,1)} %get-tuple-element.98.refs_7_.refs_1_, bf16[128,1024]{1,0:T(8,128)(2,1)} %copy-done.32, bf16[128,1024]{1,0:T(8,128)(2,1)} %copy-done.35, bf16[128,1024]{1,0:T(8,128)(2,1)} %copy-done.33, ...), custom_call_target="tpu_custom_call" | custom-call | flops 6000000000 | tf_op jit(solution)/shard_map/weights/pallas_call | solution.py:176
  221.3 9.7 %input_back.1 = (bf16[256,1024]{1,0:T(8,128)(2,1)}, bf16[256,1024]{1,0:T(8,128)(2,1)}, bf16[256,1024]{1,0:T(8,128)(2,1)}, bf16[256,1024]{1,0:T(8,128)(2,1)}, f32[2,1024]{1,0:T(2,128)}) custom-call(bf16[256,1024]{1,0:T(8,128)(2,1)} %bitcast.63, bf16[256,1024]{1,0:T(8,128)(2,1)} %copy-done.9, bf16[256,1024]{1,0:T(8,128)(2,1)} %copy-done.8, ...), custom_call_target="tpu_custom_call" | custom-call | flops 6000000000 | tf_op jit(solution)/shard_map/input_back/pallas_call | solution.py:176
  236.1 5.4 %all-to-all-start = ((f32[32,1,128]{2,1,0:T(1,128)}), f32[32,1,128]{2,1,0:T(1,128)S(1)}, u32[]{:S(2)}, u32[]{:S(2)}) async-start(f32[32,1,128]{2,1,0:T(1,128)} %reshape.74), calls=%async_computation.1 | async-start | bytes 32768 | tf_op jit(solution)/shard_map/all_to_all | solution.py:939
  241.5 2.4 finish_experts.1
  243.9 9.6 %all-to-all-done = f32[32,1,128]{2,1,0:T(1,128)S(1)} async-done(((f32[32,1,128]{2,1,0:T(1,128)}), f32[32,1,128]{2,1,0:T(1,128)S(1)}, u32[]{:S(2)}, u32[]{:S(2)}) %all-to-all-start) | async-done | bytes 16416 | tf_op jit(solution)/shard_map/all_to_all | solution.py:939
  256.6 2.8 %output.1 = bf16[256,1024]{1,0:T(8,128)(2,1)} custom-call(f32[256,1024]{1,0:T(8,128)} %get-tuple-element.74.refs_0_, bf16[256,1024]{1,0:T(8,128)(2,1)} %get-tuple-element.83.refs_6_.refs_15_.refs_1_, bf16[256,1024]{1,0:T(8,128)(2,1)} %copy-done.20, bf16[256,1024]{1,0:T(8,128)(2,1)} %copy-done.18, bf16[256,1024]{1,0:T(8,128)(2,1)} %copy-done.19, ...), custom_call_target="tpu_custom_call" | custom-call | flops 2000000000 | tf_op jit(solution)/shard_map/output/pallas_call | solution.py:176
  260.2 2.9 %token_grads.1 = bf16[256,1024]{1,0:T(8,128)(2,1)} custom-call(f32[256,1024]{1,0:T(8,128)} %get-tuple-element.112.refs_0_, bf16[256,1024]{1,0:T(8,128)(2,1)} %get-tuple-element.113.refs_1_, bf16[256,1024]{1,0:T(8,128)(2,1)} %copy-done.23, bf16[256,1024]{1,0:T(8,128)(2,1)} %copy-done.21, bf16[256,1024]{1,0:T(8,128)(2,1)} %copy-done.22), custom_call_target="tpu_custom_call" | custom-call | flops 2000000000 | tf_op jit(solution)/shard_map/token_grads/pallas_call | solution.py:176
  263.1 2.4 finish_weights.1
  (187 shorter events, 62.2 us)
Async XLA Ops:
  7.2 47.2 %all-gather.4.cloned.1.call-start = ((), (), s32[]{:S(2)}) async-start(), calls=%async_computation.3 | async-start | bytes 3833856 | tf_op jit(solution)/shard_map/all_gather | solution.py:695
  9.6 101.9 %all-gather.6.cloned.1.call-start = ((), (), s32[]{:S(2)}) async-start(), calls=%async_computation.6 | async-start | bytes 5013504 | tf_op jit(solution)/shard_map/all_gather | solution.py:732
  14.7 194.5 %reduce-scatter.3.cloned.1.call-start = ((), (), s32[]{:S(2)}) async-start(), calls=%async_computation.4 | async-start | bytes 5013504 | tf_op jit(solution)/shard_map/reduce_scatter | solution.py:833
  14.7 15.8 %collective-permute-start.1 = (bf16[256,1024]{1,0:T(8,128)(2,1)S(1)}, bf16[256,1024]{1,0:T(8,128)(2,1)S(1)}, u32[]{:S(2)}, u32[]{:S(2)}) collective-permute-start(bf16[256,1024]{1,0:T(8,128)(2,1)S(1)} %bitcast.64), channel_id=1, source_target_pairs={{0,16},{8,24},{16,0},{24,8},{1,17},{9,25},{17,1},{25,9},{2,18},{10... | collective-permute-start | bytes 1572872 | tf_op jit(solution)/shard_map/ppermute | solution.py:557
  17.8 14.9 %collective-permute-start = (bf16[256,1024]{1,0:T(8,128)(2,1)S(1)}, bf16[256,1024]{1,0:T(8,128)(2,1)S(1)}, u32[]{:S(2)}, u32[]{:S(2)}) collective-permute-start(bf16[256,1024]{1,0:T(8,128)(2,1)S(1)} %bitcast.65), channel_id=1, source_target_pairs={{0,8},{8,0},{16,24},{24,16},{1,9},{9,1},{17,25},{25,17},{2,10},{10... | collective-permute-start | bytes 1572872 | tf_op jit(solution)/shard_map/ppermute | solution.py:557
  19.3 23.2 %collective-permute-start.5 = (bf16[272,1024]{1,0:T(8,128)(2,1)}, bf16[272,1024]{1,0:T(8,128)(2,1)S(1)}, u32[]{:S(2)}, u32[]{:S(2)}) collective-permute-start(bf16[272,1024]{1,0:T(8,128)(2,1)} %pack_grad.1.refs_4_), channel_id=1, source_target_pairs={{0,16},{8,24},{16,0},{24,8},{1,17},{9,25},{17,1},{25,9},{2,18},{10... | collective-permute-start | bytes 1671176 | tf_op jit(solution)/shard_map/ppermute | solution.py:557
  19.8 24.8 %collective-permute-start.4 = (bf16[272,1024]{1,0:T(8,128)(2,1)}, bf16[272,1024]{1,0:T(8,128)(2,1)S(1)}, u32[]{:S(2)}, u32[]{:S(2)}) collective-permute-start(bf16[272,1024]{1,0:T(8,128)(2,1)} %pack_grad.1.refs_4_), channel_id=1, source_target_pairs={{0,8},{8,0},{16,24},{24,16},{1,9},{9,1},{17,25},{25,17},{2,10},{10... | collective-permute-start | bytes 1671176 | tf_op jit(solution)/shard_map/ppermute | solution.py:557
  30.5 19.7 %collective-permute-start.2 = (bf16[128,1024]{1,0:T(8,128)(2,1)S(1)}, bf16[128,1024]{1,0:T(8,128)(2,1)}, u32[]{:S(2)}, u32[]{:S(2)}) collective-permute-start(bf16[128,1024]{1,0:T(8,128)(2,1)S(1)} %slice.38), channel_id=1, source_target_pairs={{0,8},{8,0},{16,24},{24,16},{1,9},{9,1},{17,25},{25,17},{2,10},{10... | collective-permute-start | bytes 786440 | tf_op jit(solution)/shard_map/ppermute | solution.py:557
  32.7 17.6 %collective-permute-start.3 = (bf16[128,1024]{1,0:T(8,128)(2,1)S(1)}, bf16[128,1024]{1,0:T(8,128)(2,1)}, u32[]{:S(2)}, u32[]{:S(2)}) collective-permute-start(bf16[128,1024]{1,0:T(8,128)(2,1)S(1)} %slice.39), channel_id=1, source_target_pairs={{0,16},{8,24},{16,0},{24,8},{1,17},{9,25},{17,1},{25,9},{2,18},{10... | collective-permute-start | bytes 786440 | tf_op jit(solution)/shard_map/ppermute | solution.py:557
  42.5 11.9 %collective-permute-start.6 = (bf16[128,1024]{1,0:T(8,128)(2,1)S(1)}, bf16[128,1024]{1,0:T(8,128)(2,1)}, u32[]{:S(2)}, u32[]{:S(2)}) collective-permute-start(bf16[128,1024]{1,0:T(8,128)(2,1)S(1)} %slice.40), channel_id=1, source_target_pairs={{0,8},{8,0},{16,24},{24,16},{1,9},{9,1},{17,25},{25,17},{2,10},{10... | collective-permute-start | bytes 786440 | tf_op jit(solution)/shard_map/ppermute | solution.py:557
  70.0 16.1 %collective-permute-start.8 = (bf16[256,1024]{1,0:T(8,128)(2,1)}, bf16[256,1024]{1,0:T(8,128)(2,1)S(1)}, u32[]{:S(2)}, u32[]{:S(2)}) collective-permute-start(bf16[256,1024]{1,0:T(8,128)(2,1)} %get-tuple-element.71), channel_id=1, source_target_pairs={{0,24},{8,16},{16,8},{24,0},{1,25},{9,17},{17,9},{25,1},{2,26},{10... | collective-permute-start | bytes 1572872 | tf_op jit(solution)/shard_map/ppermute | solution.py:557
  72.0 23.5 %collective-permute-start.9 = (bf16[256,1024]{1,0:T(8,128)(2,1)}, bf16[256,1024]{1,0:T(8,128)(2,1)S(1)}, u32[]{:S(2)}, u32[]{:S(2)}) collective-permute-start(bf16[256,1024]{1,0:T(8,128)(2,1)} %get-tuple-element.72), channel_id=1, source_target_pairs={{0,8},{8,0},{16,24},{24,16},{1,9},{9,1},{17,25},{25,17},{2,10},{10... | collective-permute-start | bytes 1572872 | tf_op jit(solution)/shard_map/ppermute | solution.py:557
  72.5 23.0 %collective-permute-start.10 = (bf16[256,1024]{1,0:T(8,128)(2,1)}, bf16[256,1024]{1,0:T(8,128)(2,1)S(1)}, u32[]{:S(2)}, u32[]{:S(2)}) collective-permute-start(bf16[256,1024]{1,0:T(8,128)(2,1)} %get-tuple-element.73), channel_id=1, source_target_pairs={{0,16},{8,24},{16,0},{24,8},{1,17},{9,25},{17,1},{25,9},{2,18},{10... | collective-permute-start | bytes 1572872 | tf_op jit(solution)/shard_map/ppermute | solution.py:557
  105.8 13.7 %collective-permute-start.11 = (bf16[128,1024]{1,0:T(8,128)(2,1)}, bf16[128,1024]{1,0:T(8,128)(2,1)S(1)}, u32[]{:S(2)}, u32[]{:S(2)}) collective-permute-start(bf16[128,1024]{1,0:T(8,128)(2,1)} %get-tuple-element.75.refs_0_.refs_11_), channel_id=1, source_target_pairs={{0,8},{8,0},{16,24},{24,16},{1,9},{9,1},{17,25},{25,17},{2,10},{10... | collective-permute-start | bytes 786440 | tf_op jit(solution)/shard_map/ppermute | solution.py:557
  106.4 13.1 %collective-permute-start.14 = (bf16[128,1024]{1,0:T(8,128)(2,1)}, bf16[128,1024]{1,0:T(8,128)(2,1)S(1)}, u32[]{:S(2)}, u32[]{:S(2)}) collective-permute-start(bf16[128,1024]{1,0:T(8,128)(2,1)} %get-tuple-element.76.refs_1_.refs_12_), channel_id=1, source_target_pairs={{0,16},{8,24},{16,0},{24,8},{1,17},{9,25},{17,1},{25,9},{2,18},{10... | collective-permute-start | bytes 786440 | tf_op jit(solution)/shard_map/ppermute | solution.py:557
  108.1 26.1 %collective-permute-start.15 = (bf16[128,1024]{1,0:T(8,128)(2,1)S(1)}, bf16[128,1024]{1,0:T(8,128)(2,1)S(1)}, u32[]{:S(2)}, u32[]{:S(2)}) collective-permute-start(bf16[128,1024]{1,0:T(8,128)(2,1)S(1)} %collective-permute-done.13.refs_2_.refs_15_), channel_id=1, source_target_pairs={{0,8},{8,0},{16,24},{24,16},{1,9},{9,1},{17,25},{25,17},{2,10},{10... | collective-permute-start | bytes 786440 | tf_op jit(solution)/shard_map/ppermute | solution.py:557
  110.3 23.9 %collective-permute-start.16 = (bf16[128,1024]{1,0:T(8,128)(2,1)S(1)}, bf16[128,1024]{1,0:T(8,128)(2,1)S(1)}, u32[]{:S(2)}, u32[]{:S(2)}) collective-permute-start(bf16[128,1024]{1,0:T(8,128)(2,1)S(1)} %collective-permute-done.12.refs_1_.refs_14_), channel_id=1, source_target_pairs={{0,16},{8,24},{16,0},{24,8},{1,17},{9,25},{17,1},{25,9},{2,18},{10... | collective-permute-start | bytes 786440 | tf_op jit(solution)/shard_map/ppermute | solution.py:557
  130.9 12.4 %collective-permute-start.20 = (bf16[256,1024]{1,0:T(8,128)(2,1)}, bf16[256,1024]{1,0:T(8,128)(2,1)S(1)}, u32[]{:S(2)}, u32[]{:S(2)}) collective-permute-start(bf16[256,1024]{1,0:T(8,128)(2,1)} %get-tuple-element.80.refs_10_), channel_id=1, source_target_pairs={{0,8},{8,0},{16,24},{24,16},{1,9},{9,1},{17,25},{25,17},{2,10},{10... | collective-permute-start | bytes 1572872 | tf_op jit(solution)/shard_map/ppermute | solution.py:557
  132.2 11.3 %collective-permute-start.21 = (bf16[256,1024]{1,0:T(8,128)(2,1)}, bf16[256,1024]{1,0:T(8,128)(2,1)S(1)}, u32[]{:S(2)}, u32[]{:S(2)}) collective-permute-start(bf16[256,1024]{1,0:T(8,128)(2,1)} %get-tuple-element.81.refs_11_), channel_id=1, source_target_pairs={{0,16},{8,24},{16,0},{24,8},{1,17},{9,25},{17,1},{25,9},{2,18},{10... | collective-permute-start | bytes 1572872 | tf_op jit(solution)/shard_map/ppermute | solution.py:557
  155.0 108.0 %reduce-scatter.5.cloned.1.call-start = ((), (), s32[]{:S(2)}) async-start(), calls=%async_computation.5 | async-start | bytes 3833856 | tf_op jit(solution)/shard_map/reduce_scatter | solution.py:923
  156.0 12.0 %collective-permute-start.22 = (bf16[256,1024]{1,0:T(8,128)(2,1)S(1)}, bf16[256,1024]{1,0:T(8,128)(2,1)S(1)}, u32[]{:S(2)}, u32[]{:S(2)}) collective-permute-start(bf16[256,1024]{1,0:T(8,128)(2,1)S(1)} %copy-done.24), channel_id=1, source_target_pairs={{0,24},{8,16},{16,8},{24,0},{1,25},{9,17},{17,9},{25,1},{2,26},{10... | collective-permute-start | bytes 1572872 | tf_op jit(solution)/shard_map/ppermute | solution.py:557
  173.5 13.8 %collective-permute-start.25 = (bf16[128,1024]{1,0:T(8,128)(2,1)}, bf16[128,1024]{1,0:T(8,128)(2,1)S(1)}, u32[]{:S(2)}, u32[]{:S(2)}) collective-permute-start(bf16[128,1024]{1,0:T(8,128)(2,1)} %get-tuple-element.98.refs_7_.refs_1_), channel_id=1, source_target_pairs={{0,8},{8,0},{16,24},{24,16},{1,9},{9,1},{17,25},{25,17},{2,10},{10... | collective-permute-start | bytes 786440 | tf_op jit(solution)/shard_map/ppermute | solution.py:557
  174.5 14.1 %collective-permute-start.28 = (bf16[128,1024]{1,0:T(8,128)(2,1)}, bf16[128,1024]{1,0:T(8,128)(2,1)S(1)}, u32[]{:S(2)}, u32[]{:S(2)}) collective-permute-start(bf16[128,1024]{1,0:T(8,128)(2,1)} %get-tuple-element.98.refs_7_.refs_1_), channel_id=1, source_target_pairs={{0,16},{8,24},{16,0},{24,8},{1,17},{9,25},{17,1},{25,9},{2,18},{10... | collective-permute-start | bytes 786440 | tf_op jit(solution)/shard_map/ppermute | solution.py:557
  176.2 32.8 %collective-permute-start.18 = (bf16[256,1024]{1,0:T(8,128)(2,1)S(1)}, bf16[256,1024]{1,0:T(8,128)(2,1)S(1)}, u32[]{:S(2)}, u32[]{:S(2)}) collective-permute-start(bf16[256,1024]{1,0:T(8,128)(2,1)S(1)} %copy-done.2), channel_id=1, source_target_pairs={{0,8},{8,0},{16,24},{24,16},{1,9},{9,1},{17,25},{25,17},{2,10},{10... | collective-permute-start | bytes 1572872 | tf_op jit(solution)/shard_map/ppermute | solution.py:557
  181.6 27.5 %collective-permute-start.19 = (bf16[256,1024]{1,0:T(8,128)(2,1)S(1)}, bf16[256,1024]{1,0:T(8,128)(2,1)S(1)}, u32[]{:S(2)}, u32[]{:S(2)}) collective-permute-start(bf16[256,1024]{1,0:T(8,128)(2,1)S(1)} %copy-done.1), channel_id=1, source_target_pairs={{0,16},{8,24},{16,0},{24,8},{1,17},{9,25},{17,1},{25,9},{2,18},{10... | collective-permute-start | bytes 1572872 | tf_op jit(solution)/shard_map/ppermute | solution.py:557
  182.9 16.5 %collective-permute-start.24 = (bf16[128,1024]{1,0:T(8,128)(2,1)S(1)}, bf16[128,1024]{1,0:T(8,128)(2,1)S(1)}, u32[]{:S(2)}, u32[]{:S(2)}) collective-permute-start(bf16[128,1024]{1,0:T(8,128)(2,1)S(1)} %collective-permute-done.23.refs_10_.refs_4_), channel_id=1, source_target_pairs={{0,8},{8,0},{16,24},{24,16},{1,9},{9,1},{17,25},{25,17},{2,10},{10... | collective-permute-start | bytes 786440 | tf_op jit(solution)/shard_map/ppermute | solution.py:557
  187.2 13.0 %collective-permute-start.26 = (bf16[128,1024]{1,0:T(8,128)(2,1)S(1)}, bf16[128,1024]{1,0:T(8,128)(2,1)S(1)}, u32[]{:S(2)}, u32[]{:S(2)}) collective-permute-start(bf16[128,1024]{1,0:T(8,128)(2,1)S(1)} %collective-permute-done.25.refs_9_.refs_3_), channel_id=1, source_target_pairs={{0,16},{8,24},{16,0},{24,8},{1,17},{9,25},{17,1},{25,9},{2,18},{10... | collective-permute-start | bytes 786440 | tf_op jit(solution)/shard_map/ppermute | solution.py:557
  220.6 34.8 %collective-permute-start.17 = (bf16[256,1024]{1,0:T(8,128)(2,1)S(1)}, bf16[256,1024]{1,0:T(8,128)(2,1)S(1)}, u32[]{:S(2)}, u32[]{:S(2)}) collective-permute-start(bf16[256,1024]{1,0:T(8,128)(2,1)S(1)} %copy-done), channel_id=1, source_target_pairs={{0,24},{8,16},{16,8},{24,0},{1,25},{9,17},{17,9},{25,1},{2,26},{10... | collective-permute-start | bytes 1572872 | tf_op jit(solution)/shard_map/ppermute | solution.py:557
  231.0 24.4 %collective-permute-start.29 = (bf16[256,1024]{1,0:T(8,128)(2,1)}, bf16[256,1024]{1,0:T(8,128)(2,1)S(1)}, u32[]{:S(2)}, u32[]{:S(2)}) collective-permute-start(bf16[256,1024]{1,0:T(8,128)(2,1)} %get-tuple-element.110), channel_id=1, source_target_pairs={{0,8},{8,0},{16,24},{24,16},{1,9},{9,1},{17,25},{25,17},{2,10},{10... | collective-permute-start | bytes 1572872 | tf_op jit(solution)/shard_map/ppermute | solution.py:557
  232.1 23.3 %collective-permute-start.30 = (bf16[256,1024]{1,0:T(8,128)(2,1)}, bf16[256,1024]{1,0:T(8,128)(2,1)S(1)}, u32[]{:S(2)}, u32[]{:S(2)}) collective-permute-start(bf16[256,1024]{1,0:T(8,128)(2,1)} %get-tuple-element.111), channel_id=1, source_target_pairs={{0,16},{8,24},{16,0},{24,8},{1,17},{9,25},{17,1},{25,9},{2,18},{10... | collective-permute-start | bytes 1572872 | tf_op jit(solution)/shard_map/ppermute | solution.py:557
  233.8 25.6 %collective-permute-start.31 = (bf16[256,1024]{1,0:T(8,128)(2,1)}, bf16[256,1024]{1,0:T(8,128)(2,1)S(1)}, u32[]{:S(2)}, u32[]{:S(2)}) collective-permute-start(bf16[256,1024]{1,0:T(8,128)(2,1)} %get-tuple-element.114), channel_id=1, source_target_pairs={{0,24},{8,16},{16,8},{24,0},{1,25},{9,17},{17,9},{25,1},{2,26},{10... | collective-permute-start | bytes 1572872 | tf_op jit(solution)/shard_map/ppermute | solution.py:557
  236.1 17.4 %all-to-all-start = ((f32[32,1,128]{2,1,0:T(1,128)}), f32[32,1,128]{2,1,0:T(1,128)S(1)}, u32[]{:S(2)}, u32[]{:S(2)}) async-start(f32[32,1,128]{2,1,0:T(1,128)} %reshape.74), calls=%async_computation.1 | async-start | bytes 32768 | tf_op jit(solution)/shard_map/all_to_all | solution.py:939
  (47 other events, 277.0 us)
Sparse Core Ops, SparseCore 0:
  10.2 43.1 all-gather.3
  55.0 48.3 all-gather.5
  155.2 52.1 reduce-scatter.2
  219.7 42.3 reduce-scatter.4

commit v2 on v1

--- a/solution.py
+++ b/solution.py
@@ -622,7 +622,6 @@
             near[4],
             far[4],
         ],
-        moved[:2],
     )
     return back, moved, gated, norm, slabs
 
@@ -838,7 +837,7 @@
 
     dq, dsel, dk, dv = call(
         "attend_back",
-        6,
+        40,
         functools.partial(attend_back_kernel, own, 3, kinds, size),
         [
             shape((3 * own, size), BF16),
@@ -852,7 +851,7 @@
     out_moved = [to_head(out[flip], flip) for flip in (3, 1, 2)]
     d_in, d_exp = call(
         "attend_last",
-        5,
+        40,
         functools.partial(attend_last_kernel, own, kinds, size),
         [shape((length, 3 * LANES), BF16), shape((length, mixed_width), BF16)],
         [

time: 273 us -> 270 us (0.989)
  waiting for transfers between devices: 75.3 us -> 71.6 us
    ppermute x32, waiting for transfers between devices: 65.5 us -> 61.2 us  [to_head(): return lax.ppermute(value, 'head', [(i, i ^ flip) for i in range(n)])]
  transfers between devices with their start and end apart: 37 -> 37, of which waited for: 18 -> 14; matrix products, arithmetic and copies ran while one was open for 4% -> 5% of each run, Pallas kernels for 34% -> 38%
where the time goes in v2:
time: 270 us; the launch traced here: 269 us
  Pallas kernels  116 us (43%)
  waiting for transfers between devices  71.6 us (27%)
  starting transfers between devices  44.2 us (16%)
  local copies, waits for them, and re-layouts  17.1 us (6%)
  between operations  14.4 us (5%)
  other arithmetic  5.69 us (2%)
    pallas_call x19, Pallas kernels, call(): pl.pallas_call(kernel, name=name, out_shape=shapes[0] if single else shap...  116 us
    ppermute x32, waiting for transfers between devices, to_head(): return lax.ppermute(value, 'head', [(i, i ^ flip) for i in range(n)])  61.2 us
    ppermute x32, starting transfers between devices, to_head(): return lax.ppermute(value, 'head', [(i, i ^ flip) for i in range(n)])  39.4 us
    unnamed x83, local copies, waits for them, and re-layouts  11.7 us
    all_to_all x1, waiting for transfers between devices, shards(): lax.all_to_all(norms, ('head', 'dp'), split_axis=0, concat_axis=0, tiled=...  10.3 us
  transfers between devices with their start and end apart: 37, of which 14 were waited for; matrix products, arithmetic and copies ran while one was open for 5% of the time, Pallas kernels for 38%

profile of v2, /device:TPU:0, one launch (start us, length us, event | category | flops | bytes accessed | tf_op | source)
XLA Modules:
  0.0 269.3 jit_solution(17863073176648066583)
XLA Ops:
  7.2 2.3 pack_weights.1.refs_3_
  12.6 2.1 pack_experts.1
  14.7 3.0 %collective-permute-start.1 = (bf16[256,1024]{1,0:T(8,128)(2,1)S(1)}, bf16[256,1024]{1,0:T(8,128)(2,1)S(1)}, u32[]{:S(2)}, u32[]{:S(2)}) collective-permute-start(bf16[256,1024]{1,0:T(8,128)(2,1)S(1)} %bitcast.64), channel_id=1, source_target_pairs={{0,16},{8,24},{16,0},{24,8},{1,17},{9,25},{17,1},{25,9},{2,18},{10... | collective-permute-start | bytes 1572872 | tf_op jit(solution)/shard_map/ppermute | solution.py:557
  20.0 10.5 %collective-permute-done.1.refs_2_.refs_11_ = bf16[256,1024]{1,0:T(8,128)(2,1)S(1)} collective-permute-done((bf16[256,1024]{1,0:T(8,128)(2,1)S(1)}, bf16[256,1024]{1,0:T(8,128)(2,1)S(1)}, u32[]{:S(2)}, u32[]{:S(2)}) %collective-permute-start.1) | collective-permute-done | bytes 524320 | tf_op jit(solution)/shard_map/ppermute | solution.py:557
  30.5 2.1 collective-permute-start.2
  34.3 8.2 %collective-permute-done.5.refs_12_.refs_11_.refs_5_ = bf16[272,1024]{1,0:T(8,128)(2,1)S(1)} collective-permute-done((bf16[272,1024]{1,0:T(8,128)(2,1)}, bf16[272,1024]{1,0:T(8,128)(2,1)S(1)}, u32[]{:S(2)}, u32[]{:S(2)}) %collective-permute-start.5) | collective-permute-done | bytes 557088 | tf_op jit(solution)/shard_map/ppermute | solution.py:557
  42.5 2.1 collective-permute-start.6
  47.9 2.4 collective-permute-done.2.refs_3_.refs_12_
  50.3 4.1 %collective-permute-done.6.refs_13_.refs_7_.refs_6_ = bf16[128,1024]{1,0:T(8,128)(2,1)} collective-permute-done((bf16[128,1024]{1,0:T(8,128)(2,1)S(1)}, bf16[128,1024]{1,0:T(8,128)(2,1)}, u32[]{:S(2)}, u32[]{:S(2)}) %collective-permute-start.6) | collective-permute-done | bytes 262176 | tf_op jit(solution)/shard_map/ppermute | solution.py:557
  54.5 15.6 %forward.1 = (bf16[256,1024]{1,0:T(8,128)(2,1)}, bf16[256,1024]{1,0:T(8,128)(2,1)}, bf16[256,1024]{1,0:T(8,128)(2,1)}, bf16[256,1024]{1,0:T(8,128)(2,1)}, bf16[1...) custom-call(bf16[256,1024]{1,0:T(8,128)(2,1)} %bitcast.60, ...), custom_call_target="tpu_custom_call" | custom-call | flops 14000000000 | tf_op jit(solution)/shard_map/forward/pallas_call | solution.py:176
  75.2 10.9 %collective-permute-done.8.refs_2_ = bf16[256,1024]{1,0:T(8,128)(2,1)S(1)} collective-permute-done((bf16[256,1024]{1,0:T(8,128)(2,1)}, bf16[256,1024]{1,0:T(8,128)(2,1)S(1)}, u32[]{:S(2)}, u32[]{:S(2)}) %collective-permute-start.8) | collective-permute-done | bytes 524320 | tf_op jit(solution)/shard_map/ppermute | solution.py:557
  86.1 9.4 %collective-permute-done.9.refs_3_ = bf16[256,1024]{1,0:T(8,128)(2,1)S(1)} collective-permute-done((bf16[256,1024]{1,0:T(8,128)(2,1)}, bf16[256,1024]{1,0:T(8,128)(2,1)S(1)}, u32[]{:S(2)}, u32[]{:S(2)}) %collective-permute-start.9) | collective-permute-done | bytes 524320 | tf_op jit(solution)/shard_map/ppermute | solution.py:557
  96.5 3.2 %residual.1 = (f32[256,1024]{1,0:T(8,128)}, bf16[128,1024]{1,0:T(8,128)(2,1)}, bf16[128,1024]{1,0:T(8,128)(2,1)}) custom-call(bf16[256,1024]{1,0:T(8,128)(2,1)} %bitcast.61, bf16[256,1024]{1,0:T(8,128)(2,1)} %get-tuple-element.70.refs_1_, bf16[256,1024]{1,0:T(8,128)(2,1)} %copy-done.25, bf16[256,1024]{1,0:T(8,128)(2,1)} %copy-done.26, ...), custom_call_target="tpu_custom_call" | custom-call | flops 2000000000 | tf_op jit(solution)/shard_map/residual/pallas_call | solution.py:176
  113.1 6.5 %experts_own.1 = (bf16[256,1024]{1,0:T(8,128)(2,1)}, bf16[256,1024]{1,0:T(8,128)(2,1)}, bf16[256,1024]{1,0:T(8,128)(2,1)}, f32[2,1024]{1,0:T(2,128)}, f32[8,1024]{1,0:T(8,128)}) custom-call(bf16[128,1024]{1,0:T(8,128)(2,1)} %get-tuple-element.75.refs_0_.refs_11_, bf16[128,1024]{1,0:T(8,128)(2,1)} %get-tuple-element.76.refs_1_.refs_12_, f32[1,1024]{1,0:T(1,128)} %bitcast.70, ...), custom_call_target="tpu_custom_call" | custom-call | flops 5000000000 | tf_op jit(solution)/shard_map/experts_own/pallas_call | solution.py:176
  120.5 10.6 %experts_near.1 = (bf16[256,1024]{1,0:T(8,128)(2,1)}, bf16[256,1024]{1,0:T(8,128)(2,1)}, bf16[512,1024]{1,0:T(8,128)(2,1)}, bf16[512,1024]{1,0:T(8,128)(2,1)}, f32[2,1024]{1,0:T(2,128)}, /*index=5*/f32[8,1024]{1,0:T(8,128)}) custom-call(bf16[128,1024]{1,0:T(8,128)(2,1)} %copy-done.33, bf16[128,1024]{1,0:T(8,128)(2,1)} %copy-done.29, ...), custom_call_target="tpu_custom_call" | custom-call | flops 8000000000 | tf_op jit(solution)/shard_map/experts_near/pallas_call | solution.py:176
  134.9 6.6 %experts_far.1 = (bf16[256,1024]{1,0:T(8,128)(2,1)}, bf16[256,1024]{1,0:T(8,128)(2,1)}, bf16[256,1024]{1,0:T(8,128)(2,1)}, f32[2,1024]{1,0:T(2,128)}, f32[8,1024]{1,0:T(8,128)}) custom-call(bf16[128,1024]{1,0:T(8,128)(2,1)} %copy-done.36, bf16[128,1024]{1,0:T(8,128)(2,1)} %copy-done.37, f32[1,1024]{1,0:T(1,128)} %bitcast.72, f32[1,1024]{1,0:T(1,128)} %bitcast.75, ...), custom_call_target="tpu_custom_call" | custom-call | flops 5000000000 | tf_op jit(solution)/shard_map/experts_far/pallas_call | solution.py:176
  141.5 10.5 %experts_weights.1.refs_5_ = bf16[8,272,1024]{2,1,0:T(8,128)(2,1)} custom-call(bf16[256,1024]{1,0:T(8,128)(2,1)} %get-tuple-element.77.refs_0_, bf16[512,1024]{1,0:T(8,128)(2,1)} %get-tuple-element.79.refs_1_, bf16[256,1024]{1,0:T(8,128)(2,1)} %get-tuple-element.82.refs_2_, bf16[256,1024]{1,0:T(8,128)(2,1)} %bitcast.39, bf16[272,1024]{1,0:T(8,128)(2,1)} %copy-done.6, ...), custom_call_target="tpu_custom_call" | custom-call | flops 8000000000 | tf_op jit(solution)/shard_map/experts_weights/pallas_call | solution.py:176
  154.3 6.6 %experts_out.1 = (bf16[256,1024]{1,0:T(8,128)(2,1)}, bf16[256,1024]{1,0:T(8,128)(2,1)}, bf16[256,1024]{1,0:T(8,128)(2,1)}, bf16[256,1024]{1,0:T(8,128)(2,1)}) custom-call(bf16[256,1024]{1,0:T(8,128)(2,1)} %get-tuple-element.77.refs_0_, bf16[512,1024]{1,0:T(8,128)(2,1)} %get-tuple-element.79.refs_1_, bf16[256,1024]{1,0:T(8,128)(2,1)} %get-tuple-element.82.refs_2_, ...), custom_call_target="tpu_custom_call" | custom-call | flops 12000000000 | tf_op jit(solution)/shard_map/experts_out/pallas_call | solution.py:176
  160.9 3.8 %collective-permute-done.22.refs_4_ = bf16[256,1024]{1,0:T(8,128)(2,1)S(1)} collective-permute-done((bf16[256,1024]{1,0:T(8,128)(2,1)S(1)}, bf16[256,1024]{1,0:T(8,128)(2,1)S(1)}, u32[]{:S(2)}, u32[]{:S(2)}) %collective-permute-start.22) | collective-permute-done | bytes 524320 | tf_op jit(solution)/shard_map/ppermute | solution.py:557
  165.5 3.3 %residual_back.1 = (f32[256,1024]{1,0:T(8,128)}, bf16[128,1024]{1,0:T(8,128)(2,1)}, bf16[128,1024]{1,0:T(8,128)(2,1)}) custom-call(bf16[256,1024]{1,0:T(8,128)(2,1)} %bitcast.40, bf16[256,1024]{1,0:T(8,128)(2,1)} %get-tuple-element.78.refs_13_.refs_1_, bf16[256,1024]{1,0:T(8,128)(2,1)} %copy-done.3, bf16[256,1024]{1,0:T(8,128)(2,1)} %copy-done.4, ...), custom_call_target="tpu_custom_call" | custom-call | flops 2000000000 | tf_op jit(solution)/shard_map/residual_back/pallas_call | solution.py:176
  173.6 4.7 %collective-permute-done.27.refs_8_.refs_2_ = bf16[128,1024]{1,0:T(8,128)(2,1)S(1)} collective-permute-done((bf16[128,1024]{1,0:T(8,128)(2,1)}, bf16[128,1024]{1,0:T(8,128)(2,1)S(1)}, u32[]{:S(2)}, u32[]{:S(2)}) %collective-permute-start.27) | collective-permute-done | bytes 262176 | tf_op jit(solution)/shard_map/ppermute | solution.py:557
  180.7 3.3 %collective-permute-done.25.refs_9_.refs_3_ = bf16[128,1024]{1,0:T(8,128)(2,1)S(1)} collective-permute-done((bf16[128,1024]{1,0:T(8,128)(2,1)}, bf16[128,1024]{1,0:T(8,128)(2,1)S(1)}, u32[]{:S(2)}, u32[]{:S(2)}) %collective-permute-start.25) | collective-permute-done | bytes 262176 | tf_op jit(solution)/shard_map/ppermute | solution.py:557
  185.5 9.4 %attend_back.1 = (bf16[768,128]{1,0:T(8,128)(2,1)}, f32[1024,128]{1,0:T(8,128)}, f32[1024,128]{1,0:T(8,128)}, f32[1024,128]{1,0:T(8,128)}) custom-call(bf16[1024,128]{1,0:T(8,128)(2,1)} %get-tuple-element.87.refs_0_, bf16[1024,128]{1,0:T(8,128)(2,1)} %get-tuple-element.88.refs_1_, s32[1024,8]{1,0:T(8,128)} %copy.45.refs_7_.refs_2_, s32[1,1024]{1,0:T(1,128)} %bitcast.49, ...), custom_call_target="tpu_custom_call" | custom-call | flops 40000000000 | tf_op jit(solution)/shard_map/attend_back/pallas_call | solution.py:176
  197.5 8.1 %attend_last.1 = (bf16[1024,384]{1,0:T(8,128)(2,1)}, bf16[1024,640]{1,0:T(8,128)(2,1)}) custom-call(bf16[1024,128]{1,0:T(8,128)(2,1)} %get-tuple-element.87.refs_0_, bf16[1024,128]{1,0:T(8,128)(2,1)} %get-tuple-element.88.refs_1_, s32[1024,8]{1,0:T(8,128)} %copy.45.refs_7_.refs_2_, s32[1,1024]{1,0:T(1,128)} %bitcast.50, ...), custom_call_target="tpu_custom_call" | custom-call | flops 40000000000 | tf_op jit(solution)/shard_map/attend_last/pallas_call | solution.py:176
  206.6 9.5 %weights.1.refs_10_ = bf16[1024,1664]{1,0:T(8,128)(2,1)} custom-call(bf16[128,1024]{1,0:T(8,128)(2,1)} %get-tuple-element.97.refs_6_.refs_0_, bf16[128,1024]{1,0:T(8,128)(2,1)} %get-tuple-element.98.refs_7_.refs_1_, bf16[128,1024]{1,0:T(8,128)(2,1)} %copy-done.30, bf16[128,1024]{1,0:T(8,128)(2,1)} %copy-done.32, bf16[128,1024]{1,0:T(8,128)(2,1)} %copy-done.31, ...), custom_call_target="tpu_custom_call" | custom-call | flops 6000000000 | tf_op jit(solution)/shard_map/weights/pallas_call | solution.py:176
  218.6 9.6 %input_back.1 = (bf16[256,1024]{1,0:T(8,128)(2,1)}, bf16[256,1024]{1,0:T(8,128)(2,1)}, bf16[256,1024]{1,0:T(8,128)(2,1)}, bf16[256,1024]{1,0:T(8,128)(2,1)}, f32[2,1024]{1,0:T(2,128)}) custom-call(bf16[256,1024]{1,0:T(8,128)(2,1)} %bitcast.63, bf16[256,1024]{1,0:T(8,128)(2,1)} %copy-done.9, bf16[256,1024]{1,0:T(8,128)(2,1)} %copy-done.8, ...), custom_call_target="tpu_custom_call" | custom-call | flops 6000000000 | tf_op jit(solution)/shard_map/input_back/pallas_call | solution.py:176
  233.4 4.7 %all-to-all-start = ((f32[32,1,128]{2,1,0:T(1,128)}), f32[32,1,128]{2,1,0:T(1,128)S(1)}, u32[]{:S(2)}, u32[]{:S(2)}) async-start(f32[32,1,128]{2,1,0:T(1,128)} %reshape.74), calls=%async_computation.1 | async-start | bytes 32768 | tf_op jit(solution)/shard_map/all_to_all | solution.py:938
  238.1 2.4 finish_experts.1
  240.5 10.3 %all-to-all-done = f32[32,1,128]{2,1,0:T(1,128)S(1)} async-done(((f32[32,1,128]{2,1,0:T(1,128)}), f32[32,1,128]{2,1,0:T(1,128)S(1)}, u32[]{:S(2)}, u32[]{:S(2)}) %all-to-all-start) | async-done | bytes 16416 | tf_op jit(solution)/shard_map/all_to_all | solution.py:938
  253.9 2.8 %output.1 = bf16[256,1024]{1,0:T(8,128)(2,1)} custom-call(f32[256,1024]{1,0:T(8,128)} %get-tuple-element.74.refs_0_, bf16[256,1024]{1,0:T(8,128)(2,1)} %get-tuple-element.83.refs_6_.refs_15_.refs_1_, bf16[256,1024]{1,0:T(8,128)(2,1)} %copy-done.20, bf16[256,1024]{1,0:T(8,128)(2,1)} %copy-done.18, bf16[256,1024]{1,0:T(8,128)(2,1)} %copy-done.19, ...), custom_call_target="tpu_custom_call" | custom-call | flops 2000000000 | tf_op jit(solution)/shard_map/output/pallas_call | solution.py:176
  257.5 2.9 %token_grads.1 = bf16[256,1024]{1,0:T(8,128)(2,1)} custom-call(f32[256,1024]{1,0:T(8,128)} %get-tuple-element.112.refs_0_, bf16[256,1024]{1,0:T(8,128)(2,1)} %get-tuple-element.113.refs_1_, bf16[256,1024]{1,0:T(8,128)(2,1)} %copy-done.23, bf16[256,1024]{1,0:T(8,128)(2,1)} %copy-done.21, bf16[256,1024]{1,0:T(8,128)(2,1)} %copy-done.22), custom_call_target="tpu_custom_call" | custom-call | flops 2000000000 | tf_op jit(solution)/shard_map/token_grads/pallas_call | solution.py:176
  260.4 2.4 finish_weights.1
  (186 shorter events, 61.1 us)
Async XLA Ops:
  7.2 47.2 %all-gather.4.cloned.1.call-start = ((), (), s32[]{:S(2)}) async-start(), calls=%async_computation.3 | async-start | bytes 3833856 | tf_op jit(solution)/shard_map/all_gather | solution.py:694
  9.6 102.0 %all-gather.6.cloned.1.call-start = ((), (), s32[]{:S(2)}) async-start(), calls=%async_computation.6 | async-start | bytes 5013504 | tf_op jit(solution)/shard_map/all_gather | solution.py:731
  14.7 191.0 %reduce-scatter.3.cloned.1.call-start = ((), (), s32[]{:S(2)}) async-start(), calls=%async_computation.4 | async-start | bytes 5013504 | tf_op jit(solution)/shard_map/reduce_scatter | solution.py:832
  14.7 15.8 %collective-permute-start.1 = (bf16[256,1024]{1,0:T(8,128)(2,1)S(1)}, bf16[256,1024]{1,0:T(8,128)(2,1)S(1)}, u32[]{:S(2)}, u32[]{:S(2)}) collective-permute-start(bf16[256,1024]{1,0:T(8,128)(2,1)S(1)} %bitcast.64), channel_id=1, source_target_pairs={{0,16},{8,24},{16,0},{24,8},{1,17},{9,25},{17,1},{25,9},{2,18},{10... | collective-permute-start | bytes 1572872 | tf_op jit(solution)/shard_map/ppermute | solution.py:557
  17.8 14.9 %collective-permute-start = (bf16[256,1024]{1,0:T(8,128)(2,1)S(1)}, bf16[256,1024]{1,0:T(8,128)(2,1)S(1)}, u32[]{:S(2)}, u32[]{:S(2)}) collective-permute-start(bf16[256,1024]{1,0:T(8,128)(2,1)S(1)} %bitcast.65), channel_id=1, source_target_pairs={{0,8},{8,0},{16,24},{24,16},{1,9},{9,1},{17,25},{25,17},{2,10},{10... | collective-permute-start | bytes 1572872 | tf_op jit(solution)/shard_map/ppermute | solution.py:557
  19.3 23.2 %collective-permute-start.5 = (bf16[272,1024]{1,0:T(8,128)(2,1)}, bf16[272,1024]{1,0:T(8,128)(2,1)S(1)}, u32[]{:S(2)}, u32[]{:S(2)}) collective-permute-start(bf16[272,1024]{1,0:T(8,128)(2,1)} %pack_grad.1.refs_4_), channel_id=1, source_target_pairs={{0,16},{8,24},{16,0},{24,8},{1,17},{9,25},{17,1},{25,9},{2,18},{10... | collective-permute-start | bytes 1671176 | tf_op jit(solution)/shard_map/ppermute | solution.py:557
  19.8 24.8 %collective-permute-start.4 = (bf16[272,1024]{1,0:T(8,128)(2,1)}, bf16[272,1024]{1,0:T(8,128)(2,1)S(1)}, u32[]{:S(2)}, u32[]{:S(2)}) collective-permute-start(bf16[272,1024]{1,0:T(8,128)(2,1)} %pack_grad.1.refs_4_), channel_id=1, source_target_pairs={{0,8},{8,0},{16,24},{24,16},{1,9},{9,1},{17,25},{25,17},{2,10},{10... | collective-permute-start | bytes 1671176 | tf_op jit(solution)/shard_map/ppermute | solution.py:557
  30.5 19.7 %collective-permute-start.2 = (bf16[128,1024]{1,0:T(8,128)(2,1)S(1)}, bf16[128,1024]{1,0:T(8,128)(2,1)}, u32[]{:S(2)}, u32[]{:S(2)}) collective-permute-start(bf16[128,1024]{1,0:T(8,128)(2,1)S(1)} %slice.38), channel_id=1, source_target_pairs={{0,8},{8,0},{16,24},{24,16},{1,9},{9,1},{17,25},{25,17},{2,10},{10... | collective-permute-start | bytes 786440 | tf_op jit(solution)/shard_map/ppermute | solution.py:557
  32.7 17.6 %collective-permute-start.3 = (bf16[128,1024]{1,0:T(8,128)(2,1)S(1)}, bf16[128,1024]{1,0:T(8,128)(2,1)}, u32[]{:S(2)}, u32[]{:S(2)}) collective-permute-start(bf16[128,1024]{1,0:T(8,128)(2,1)S(1)} %slice.39), channel_id=1, source_target_pairs={{0,16},{8,24},{16,0},{24,8},{1,17},{9,25},{17,1},{25,9},{2,18},{10... | collective-permute-start | bytes 786440 | tf_op jit(solution)/shard_map/ppermute | solution.py:557
  42.5 11.9 %collective-permute-start.6 = (bf16[128,1024]{1,0:T(8,128)(2,1)S(1)}, bf16[128,1024]{1,0:T(8,128)(2,1)}, u32[]{:S(2)}, u32[]{:S(2)}) collective-permute-start(bf16[128,1024]{1,0:T(8,128)(2,1)S(1)} %slice.40), channel_id=1, source_target_pairs={{0,8},{8,0},{16,24},{24,16},{1,9},{9,1},{17,25},{25,17},{2,10},{10... | collective-permute-start | bytes 786440 | tf_op jit(solution)/shard_map/ppermute | solution.py:557
  70.0 16.1 %collective-permute-start.8 = (bf16[256,1024]{1,0:T(8,128)(2,1)}, bf16[256,1024]{1,0:T(8,128)(2,1)S(1)}, u32[]{:S(2)}, u32[]{:S(2)}) collective-permute-start(bf16[256,1024]{1,0:T(8,128)(2,1)} %get-tuple-element.71), channel_id=1, source_target_pairs={{0,24},{8,16},{16,8},{24,0},{1,25},{9,17},{17,9},{25,1},{2,26},{10... | collective-permute-start | bytes 1572872 | tf_op jit(solution)/shard_map/ppermute | solution.py:557
  72.0 23.5 %collective-permute-start.9 = (bf16[256,1024]{1,0:T(8,128)(2,1)}, bf16[256,1024]{1,0:T(8,128)(2,1)S(1)}, u32[]{:S(2)}, u32[]{:S(2)}) collective-permute-start(bf16[256,1024]{1,0:T(8,128)(2,1)} %get-tuple-element.72), channel_id=1, source_target_pairs={{0,8},{8,0},{16,24},{24,16},{1,9},{9,1},{17,25},{25,17},{2,10},{10... | collective-permute-start | bytes 1572872 | tf_op jit(solution)/shard_map/ppermute | solution.py:557
  72.5 23.0 %collective-permute-start.10 = (bf16[256,1024]{1,0:T(8,128)(2,1)}, bf16[256,1024]{1,0:T(8,128)(2,1)S(1)}, u32[]{:S(2)}, u32[]{:S(2)}) collective-permute-start(bf16[256,1024]{1,0:T(8,128)(2,1)} %get-tuple-element.73), channel_id=1, source_target_pairs={{0,16},{8,24},{16,0},{24,8},{1,17},{9,25},{17,1},{25,9},{2,18},{10... | collective-permute-start | bytes 1572872 | tf_op jit(solution)/shard_map/ppermute | solution.py:557
  105.7 14.0 %collective-permute-start.11 = (bf16[128,1024]{1,0:T(8,128)(2,1)}, bf16[128,1024]{1,0:T(8,128)(2,1)S(1)}, u32[]{:S(2)}, u32[]{:S(2)}) collective-permute-start(bf16[128,1024]{1,0:T(8,128)(2,1)} %get-tuple-element.75.refs_0_.refs_11_), channel_id=1, source_target_pairs={{0,8},{8,0},{16,24},{24,16},{1,9},{9,1},{17,25},{25,17},{2,10},{10... | collective-permute-start | bytes 786440 | tf_op jit(solution)/shard_map/ppermute | solution.py:557
  106.2 13.4 %collective-permute-start.14 = (bf16[128,1024]{1,0:T(8,128)(2,1)}, bf16[128,1024]{1,0:T(8,128)(2,1)S(1)}, u32[]{:S(2)}, u32[]{:S(2)}) collective-permute-start(bf16[128,1024]{1,0:T(8,128)(2,1)} %get-tuple-element.76.refs_1_.refs_12_), channel_id=1, source_target_pairs={{0,16},{8,24},{16,0},{24,8},{1,17},{9,25},{17,1},{25,9},{2,18},{10... | collective-permute-start | bytes 786440 | tf_op jit(solution)/shard_map/ppermute | solution.py:557
  108.0 25.4 %collective-permute-start.15 = (bf16[128,1024]{1,0:T(8,128)(2,1)S(1)}, bf16[128,1024]{1,0:T(8,128)(2,1)S(1)}, u32[]{:S(2)}, u32[]{:S(2)}) collective-permute-start(bf16[128,1024]{1,0:T(8,128)(2,1)S(1)} %collective-permute-done.13.refs_2_.refs_15_), channel_id=1, source_target_pairs={{0,8},{8,0},{16,24},{24,16},{1,9},{9,1},{17,25},{25,17},{2,10},{10... | collective-permute-start | bytes 786440 | tf_op jit(solution)/shard_map/ppermute | solution.py:557
  110.4 23.0 %collective-permute-start.16 = (bf16[128,1024]{1,0:T(8,128)(2,1)S(1)}, bf16[128,1024]{1,0:T(8,128)(2,1)S(1)}, u32[]{:S(2)}, u32[]{:S(2)}) collective-permute-start(bf16[128,1024]{1,0:T(8,128)(2,1)S(1)} %collective-permute-done.12.refs_1_.refs_14_), channel_id=1, source_target_pairs={{0,16},{8,24},{16,0},{24,8},{1,17},{9,25},{17,1},{25,9},{2,18},{10... | collective-permute-start | bytes 786440 | tf_op jit(solution)/shard_map/ppermute | solution.py:557
  131.0 29.8 %collective-permute-start.20 = (bf16[256,1024]{1,0:T(8,128)(2,1)}, bf16[256,1024]{1,0:T(8,128)(2,1)S(1)}, u32[]{:S(2)}, u32[]{:S(2)}) collective-permute-start(bf16[256,1024]{1,0:T(8,128)(2,1)} %get-tuple-element.80.refs_10_), channel_id=1, source_target_pairs={{0,8},{8,0},{16,24},{24,16},{1,9},{9,1},{17,25},{25,17},{2,10},{10... | collective-permute-start | bytes 1572872 | tf_op jit(solution)/shard_map/ppermute | solution.py:557
  132.2 28.7 %collective-permute-start.21 = (bf16[256,1024]{1,0:T(8,128)(2,1)}, bf16[256,1024]{1,0:T(8,128)(2,1)S(1)}, u32[]{:S(2)}, u32[]{:S(2)}) collective-permute-start(bf16[256,1024]{1,0:T(8,128)(2,1)} %get-tuple-element.81.refs_11_), channel_id=1, source_target_pairs={{0,16},{8,24},{16,0},{24,8},{1,17},{9,25},{17,1},{25,9},{2,18},{10... | collective-permute-start | bytes 1572872 | tf_op jit(solution)/shard_map/ppermute | solution.py:557
  152.1 108.3 %reduce-scatter.5.cloned.1.call-start = ((), (), s32[]{:S(2)}) async-start(), calls=%async_computation.5 | async-start | bytes 3833856 | tf_op jit(solution)/shard_map/reduce_scatter | solution.py:922
  153.1 11.6 %collective-permute-start.22 = (bf16[256,1024]{1,0:T(8,128)(2,1)S(1)}, bf16[256,1024]{1,0:T(8,128)(2,1)S(1)}, u32[]{:S(2)}, u32[]{:S(2)}) collective-permute-start(bf16[256,1024]{1,0:T(8,128)(2,1)S(1)} %copy-done.24), channel_id=1, source_target_pairs={{0,24},{8,16},{16,8},{24,0},{1,25},{9,17},{17,9},{25,1},{2,26},{10... | collective-permute-start | bytes 1572872 | tf_op jit(solution)/shard_map/ppermute | solution.py:557
  171.2 12.8 %collective-permute-start.25 = (bf16[128,1024]{1,0:T(8,128)(2,1)}, bf16[128,1024]{1,0:T(8,128)(2,1)S(1)}, u32[]{:S(2)}, u32[]{:S(2)}) collective-permute-start(bf16[128,1024]{1,0:T(8,128)(2,1)} %get-tuple-element.98.refs_7_.refs_1_), channel_id=1, source_target_pairs={{0,8},{8,0},{16,24},{24,16},{1,9},{9,1},{17,25},{25,17},{2,10},{10... | collective-permute-start | bytes 786440 | tf_op jit(solution)/shard_map/ppermute | solution.py:557
  171.8 13.1 %collective-permute-start.28 = (bf16[128,1024]{1,0:T(8,128)(2,1)}, bf16[128,1024]{1,0:T(8,128)(2,1)S(1)}, u32[]{:S(2)}, u32[]{:S(2)}) collective-permute-start(bf16[128,1024]{1,0:T(8,128)(2,1)} %get-tuple-element.98.refs_7_.refs_1_), channel_id=1, source_target_pairs={{0,16},{8,24},{16,0},{24,8},{1,17},{9,25},{17,1},{25,9},{2,18},{10... | collective-permute-start | bytes 786440 | tf_op jit(solution)/shard_map/ppermute | solution.py:557
  173.0 32.7 %collective-permute-start.18 = (bf16[256,1024]{1,0:T(8,128)(2,1)S(1)}, bf16[256,1024]{1,0:T(8,128)(2,1)S(1)}, u32[]{:S(2)}, u32[]{:S(2)}) collective-permute-start(bf16[256,1024]{1,0:T(8,128)(2,1)S(1)} %copy-done.2), channel_id=1, source_target_pairs={{0,8},{8,0},{16,24},{24,16},{1,9},{9,1},{17,25},{25,17},{2,10},{10... | collective-permute-start | bytes 1572872 | tf_op jit(solution)/shard_map/ppermute | solution.py:557
  178.4 27.3 %collective-permute-start.19 = (bf16[256,1024]{1,0:T(8,128)(2,1)S(1)}, bf16[256,1024]{1,0:T(8,128)(2,1)S(1)}, u32[]{:S(2)}, u32[]{:S(2)}) collective-permute-start(bf16[256,1024]{1,0:T(8,128)(2,1)S(1)} %copy-done.1), channel_id=1, source_target_pairs={{0,16},{8,24},{16,0},{24,8},{1,17},{9,25},{17,1},{25,9},{2,18},{10... | collective-permute-start | bytes 1572872 | tf_op jit(solution)/shard_map/ppermute | solution.py:557
  179.2 16.5 %collective-permute-start.24 = (bf16[128,1024]{1,0:T(8,128)(2,1)S(1)}, bf16[128,1024]{1,0:T(8,128)(2,1)S(1)}, u32[]{:S(2)}, u32[]{:S(2)}) collective-permute-start(bf16[128,1024]{1,0:T(8,128)(2,1)S(1)} %collective-permute-done.23.refs_10_.refs_4_), channel_id=1, source_target_pairs={{0,8},{8,0},{16,24},{24,16},{1,9},{9,1},{17,25},{25,17},{2,10},{10... | collective-permute-start | bytes 786440 | tf_op jit(solution)/shard_map/ppermute | solution.py:557
  184.0 12.8 %collective-permute-start.26 = (bf16[128,1024]{1,0:T(8,128)(2,1)S(1)}, bf16[128,1024]{1,0:T(8,128)(2,1)S(1)}, u32[]{:S(2)}, u32[]{:S(2)}) collective-permute-start(bf16[128,1024]{1,0:T(8,128)(2,1)S(1)} %collective-permute-done.25.refs_9_.refs_3_), channel_id=1, source_target_pairs={{0,16},{8,24},{16,0},{24,8},{1,17},{9,25},{17,1},{25,9},{2,18},{10... | collective-permute-start | bytes 786440 | tf_op jit(solution)/shard_map/ppermute | solution.py:557
  217.2 35.6 %collective-permute-start.17 = (bf16[256,1024]{1,0:T(8,128)(2,1)S(1)}, bf16[256,1024]{1,0:T(8,128)(2,1)S(1)}, u32[]{:S(2)}, u32[]{:S(2)}) collective-permute-start(bf16[256,1024]{1,0:T(8,128)(2,1)S(1)} %copy-done), channel_id=1, source_target_pairs={{0,24},{8,16},{16,8},{24,0},{1,25},{9,17},{17,9},{25,1},{2,26},{10... | collective-permute-start | bytes 1572872 | tf_op jit(solution)/shard_map/ppermute | solution.py:557
  228.3 24.5 %collective-permute-start.29 = (bf16[256,1024]{1,0:T(8,128)(2,1)}, bf16[256,1024]{1,0:T(8,128)(2,1)S(1)}, u32[]{:S(2)}, u32[]{:S(2)}) collective-permute-start(bf16[256,1024]{1,0:T(8,128)(2,1)} %get-tuple-element.110), channel_id=1, source_target_pairs={{0,8},{8,0},{16,24},{24,16},{1,9},{9,1},{17,25},{25,17},{2,10},{10... | collective-permute-start | bytes 1572872 | tf_op jit(solution)/shard_map/ppermute | solution.py:557
  230.1 22.7 %collective-permute-start.30 = (bf16[256,1024]{1,0:T(8,128)(2,1)}, bf16[256,1024]{1,0:T(8,128)(2,1)S(1)}, u32[]{:S(2)}, u32[]{:S(2)}) collective-permute-start(bf16[256,1024]{1,0:T(8,128)(2,1)} %get-tuple-element.111), channel_id=1, source_target_pairs={{0,16},{8,24},{16,0},{24,8},{1,17},{9,25},{17,1},{25,9},{2,18},{10... | collective-permute-start | bytes 1572872 | tf_op jit(solution)/shard_map/ppermute | solution.py:557
  230.3 26.4 %collective-permute-start.31 = (bf16[256,1024]{1,0:T(8,128)(2,1)}, bf16[256,1024]{1,0:T(8,128)(2,1)S(1)}, u32[]{:S(2)}, u32[]{:S(2)}) collective-permute-start(bf16[256,1024]{1,0:T(8,128)(2,1)} %get-tuple-element.114), channel_id=1, source_target_pairs={{0,24},{8,16},{16,8},{24,0},{1,25},{9,17},{17,9},{25,1},{2,26},{10... | collective-permute-start | bytes 1572872 | tf_op jit(solution)/shard_map/ppermute | solution.py:557
  233.4 17.4 %all-to-all-start = ((f32[32,1,128]{2,1,0:T(1,128)}), f32[32,1,128]{2,1,0:T(1,128)S(1)}, u32[]{:S(2)}, u32[]{:S(2)}) async-start(f32[32,1,128]{2,1,0:T(1,128)} %reshape.74), calls=%async_computation.1 | async-start | bytes 32768 | tf_op jit(solution)/shard_map/all_to_all | solution.py:938
  (46 other events, 278.2 us)
Sparse Core Ops, SparseCore 0:
  10.2 43.1 all-gather.3
  55.0 48.3 all-gather.5
  152.2 51.5 reduce-scatter.2
  216.3 42.9 reduce-scatter.4

commit v3 on v2

--- a/solution.py
+++ b/solution.py
@@ -837,7 +837,7 @@
 
     dq, dsel, dk, dv = call(
         "attend_back",
-        40,
+        46,
         functools.partial(attend_back_kernel, own, 3, kinds, size),
         [
             shape((3 * own, size), BF16),
@@ -851,7 +851,7 @@
     out_moved = [to_head(out[flip], flip) for flip in (3, 1, 2)]
     d_in, d_exp = call(
         "attend_last",
-        40,
+        46,
         functools.partial(attend_last_kernel, own, kinds, size),
         [shape((length, 3 * LANES), BF16), shape((length, mixed_width), BF16)],
         [

time: 270 us -> 278 us (1.030)
  waiting for transfers between devices: 71.6 us -> 82.9 us
    reduce_scatter x1, waiting for transfers between devices: 0.02 us -> 11.3 us  [shards(): ffn_grads = lax.psum_scatter(slabs, 'dp', scatter_dimension=0, tiled=True)]
    unnamed x83 -> x81, local copies, waits for them, and re-layouts: 11.7 us -> 10.7 us
  transfers between devices with their start and end apart: 37 -> 37, of which waited for: 14 -> 17; matrix products, arithmetic and copies ran while one was open for 5% -> 4% of each run, Pallas kernels for 38% -> 37%
where the time goes in v3:
time: 278 us; the launch traced here: 277 us
  Pallas kernels  116 us (42%)
  waiting for transfers between devices  82.9 us (30%)
  starting transfers between devices  42.7 us (15%)
  local copies, waits for them, and re-layouts  15.4 us (6%)
  between operations  14.4 us (5%)
  other arithmetic  5.69 us (2%)
    pallas_call x19, Pallas kernels, call(): pl.pallas_call(kernel, name=name, out_shape=shapes[0] if single else shap...  116 us
    ppermute x32, waiting for transfers between devices, to_head(): return lax.ppermute(value, 'head', [(i, i ^ flip) for i in range(n)])  58.6 us
    ppermute x32, starting transfers between devices, to_head(): return lax.ppermute(value, 'head', [(i, i ^ flip) for i in range(n)])  40 us
    all_to_all x1, waiting for transfers between devices, shards(): lax.all_to_all(norms, ('head', 'dp'), split_axis=0, concat_axis=0, tiled=...  12.9 us
    reduce_scatter x1, waiting for transfers between devices, shards(): ffn_grads = lax.psum_scatter(slabs, 'dp', scatter_dimension=0, tiled=True)  11.3 us
    unnamed x81, local copies, waits for them, and re-layouts  10.7 us
  transfers between devices with their start and end apart: 37, of which 17 were waited for; matrix products, arithmetic and copies ran while one was open for 4% of the time, Pallas kernels for 37%

profile of v3, /device:TPU:0, one launch (start us, length us, event | category | flops | bytes accessed | tf_op | source)
XLA Modules:
  0.0 277.5 jit_solution(4982129125498403210)
XLA Ops:
  7.2 2.3 pack_weights.1.refs_3_
  14.7 3.0 %collective-permute-start.1 = (bf16[256,1024]{1,0:T(8,128)(2,1)}, bf16[256,1024]{1,0:T(8,128)(2,1)S(1)}, u32[]{:S(2)}, u32[]{:S(2)}) collective-permute-start(bf16[256,1024]{1,0:T(8,128)(2,1)} %bitcast.refs_0_.refs_9_), channel_id=1, source_target_pairs={{0,16},{8,24},{16,0},{24,8},{1,17},{9,25},{17,1},{25,9},{2,18},{10... | collective-permute-start | bytes 1572872 | tf_op jit(solution)/shard_map/ppermute | solution.py:557
  20.0 10.7 %collective-permute-done.1.refs_2_.refs_11_ = bf16[256,1024]{1,0:T(8,128)(2,1)S(1)} collective-permute-done((bf16[256,1024]{1,0:T(8,128)(2,1)}, bf16[256,1024]{1,0:T(8,128)(2,1)S(1)}, u32[]{:S(2)}, u32[]{:S(2)}) %collective-permute-start.1) | collective-permute-done | bytes 524320 | tf_op jit(solution)/shard_map/ppermute | solution.py:557
  34.4 8.2 %collective-permute-done.5.refs_12_.refs_11_.refs_5_ = bf16[272,1024]{1,0:T(8,128)(2,1)S(1)} collective-permute-done((bf16[272,1024]{1,0:T(8,128)(2,1)}, bf16[272,1024]{1,0:T(8,128)(2,1)S(1)}, u32[]{:S(2)}, u32[]{:S(2)}) %collective-permute-start.5) | collective-permute-done | bytes 557088 | tf_op jit(solution)/shard_map/ppermute | solution.py:557
  48.0 2.4 collective-permute-done.2.refs_3_.refs_12_
  50.4 4.1 %collective-permute-done.6.refs_13_.refs_7_.refs_6_ = bf16[128,1024]{1,0:T(8,128)(2,1)} collective-permute-done((bf16[128,1024]{1,0:T(8,128)(2,1)S(1)}, bf16[128,1024]{1,0:T(8,128)(2,1)}, u32[]{:S(2)}, u32[]{:S(2)}) %collective-permute-start.6) | collective-permute-done | bytes 262176 | tf_op jit(solution)/shard_map/ppermute | solution.py:557
  55.3 15.5 %forward.1 = (bf16[256,1024]{1,0:T(8,128)(2,1)}, bf16[256,1024]{1,0:T(8,128)(2,1)}, bf16[256,1024]{1,0:T(8,128)(2,1)}, bf16[256,1024]{1,0:T(8,128)(2,1)}, bf16[1...) custom-call(bf16[256,1024]{1,0:T(8,128)(2,1)} %bitcast.refs_0_.refs_, ...), custom_call_target="tpu_custom_call" | custom-call | flops 14000000000 | tf_op jit(solution)/shard_map/forward/pallas_call | solution.py:176
  76.0 10.9 %collective-permute-done.8.refs_2_ = bf16[256,1024]{1,0:T(8,128)(2,1)S(1)} collective-permute-done((bf16[256,1024]{1,0:T(8,128)(2,1)}, bf16[256,1024]{1,0:T(8,128)(2,1)S(1)}, u32[]{:S(2)}, u32[]{:S(2)}) %collective-permute-start.8) | collective-permute-done | bytes 524320 | tf_op jit(solution)/shard_map/ppermute | solution.py:557
  86.9 8.7 %collective-permute-done.9.refs_3_ = bf16[256,1024]{1,0:T(8,128)(2,1)S(1)} collective-permute-done((bf16[256,1024]{1,0:T(8,128)(2,1)}, bf16[256,1024]{1,0:T(8,128)(2,1)S(1)}, u32[]{:S(2)}, u32[]{:S(2)}) %collective-permute-start.9) | collective-permute-done | bytes 524320 | tf_op jit(solution)/shard_map/ppermute | solution.py:557
  96.6 3.2 %residual.1 = (f32[256,1024]{1,0:T(8,128)}, bf16[128,1024]{1,0:T(8,128)(2,1)}, bf16[128,1024]{1,0:T(8,128)(2,1)}) custom-call(bf16[256,1024]{1,0:T(8,128)(2,1)} %bitcast.refs_0_.refs_9_, bf16[256,1024]{1,0:T(8,128)(2,1)} %get-tuple-element.70.refs_1_, bf16[256,1024]{1,0:T(8,128)(2,1)} %copy-done.24, bf16[256,1024]{1,0:T(8,128)(2,1)} %copy-done.25, ...), custom_call_target="tpu_custom_call" | custom-call | flops 2000000000 | tf_op jit(solution)/shard_map/residual/pallas_call | solution.py:176
  106.4 2.5 collective-permute-done.13.refs_2_.refs_15_
  113.5 6.5 %experts_own.1 = (bf16[256,1024]{1,0:T(8,128)(2,1)}, bf16[256,1024]{1,0:T(8,128)(2,1)}, bf16[256,1024]{1,0:T(8,128)(2,1)}, f32[2,1024]{1,0:T(2,128)}, f32[8,1024]{1,0:T(8,128)}) custom-call(bf16[128,1024]{1,0:T(8,128)(2,1)} %get-tuple-element.75.refs_0_.refs_11_, bf16[128,1024]{1,0:T(8,128)(2,1)} %get-tuple-element.76.refs_1_.refs_12_, f32[1,1024]{1,0:T(1,128)} %bitcast.64, ...), custom_call_target="tpu_custom_call" | custom-call | flops 5000000000 | tf_op jit(solution)/shard_map/experts_own/pallas_call | solution.py:176
  120.8 10.5 %experts_near.1 = (bf16[256,1024]{1,0:T(8,128)(2,1)}, bf16[256,1024]{1,0:T(8,128)(2,1)}, bf16[512,1024]{1,0:T(8,128)(2,1)}, bf16[512,1024]{1,0:T(8,128)(2,1)}, f32[2,1024]{1,0:T(2,128)}, /*index=5*/f32[8,1024]{1,0:T(8,128)}) custom-call(bf16[128,1024]{1,0:T(8,128)(2,1)} %copy-done.29, bf16[128,1024]{1,0:T(8,128)(2,1)} %copy-done.28, ...), custom_call_target="tpu_custom_call" | custom-call | flops 8000000000 | tf_op jit(solution)/shard_map/experts_near/pallas_call | solution.py:176
  134.9 6.6 %experts_far.1 = (bf16[256,1024]{1,0:T(8,128)(2,1)}, bf16[256,1024]{1,0:T(8,128)(2,1)}, bf16[256,1024]{1,0:T(8,128)(2,1)}, f32[2,1024]{1,0:T(2,128)}, f32[8,1024]{1,0:T(8,128)}) custom-call(bf16[128,1024]{1,0:T(8,128)(2,1)} %copy-done.33, bf16[128,1024]{1,0:T(8,128)(2,1)} %copy-done.36, f32[1,1024]{1,0:T(1,128)} %bitcast.66, f32[1,1024]{1,0:T(1,128)} %bitcast.69, ...), custom_call_target="tpu_custom_call" | custom-call | flops 5000000000 | tf_op jit(solution)/shard_map/experts_far/pallas_call | solution.py:176
  143.0 6.5 %experts_out.1 = (bf16[256,1024]{1,0:T(8,128)(2,1)}, bf16[256,1024]{1,0:T(8,128)(2,1)}, bf16[256,1024]{1,0:T(8,128)(2,1)}, bf16[256,1024]{1,0:T(8,128)(2,1)}) custom-call(bf16[256,1024]{1,0:T(8,128)(2,1)} %get-tuple-element.77.refs_0_, bf16[512,1024]{1,0:T(8,128)(2,1)} %get-tuple-element.79.refs_1_, bf16[256,1024]{1,0:T(8,128)(2,1)} %get-tuple-element.82.refs_2_, ...), custom_call_target="tpu_custom_call" | custom-call | flops 12000000000 | tf_op jit(solution)/shard_map/experts_out/pallas_call | solution.py:176
  149.5 10.6 %experts_weights.1.refs_5_ = bf16[8,272,1024]{2,1,0:T(8,128)(2,1)} custom-call(bf16[256,1024]{1,0:T(8,128)(2,1)} %get-tuple-element.77.refs_0_, bf16[512,1024]{1,0:T(8,128)(2,1)} %get-tuple-element.79.refs_1_, bf16[256,1024]{1,0:T(8,128)(2,1)} %get-tuple-element.82.refs_2_, bf16[256,1024]{1,0:T(8,128)(2,1)} %bitcast.39, bf16[272,1024]{1,0:T(8,128)(2,1)} %copy-done.6, ...), custom_call_target="tpu_custom_call" | custom-call | flops 8000000000 | tf_op jit(solution)/shard_map/experts_weights/pallas_call | solution.py:176
  161.4 3.2 %residual_back.1 = (f32[256,1024]{1,0:T(8,128)}, bf16[128,1024]{1,0:T(8,128)(2,1)}, bf16[128,1024]{1,0:T(8,128)(2,1)}) custom-call(bf16[256,1024]{1,0:T(8,128)(2,1)} %bitcast.40, bf16[256,1024]{1,0:T(8,128)(2,1)} %get-tuple-element.78.refs_13_.refs_1_, bf16[256,1024]{1,0:T(8,128)(2,1)} %copy-done.3, bf16[256,1024]{1,0:T(8,128)(2,1)} %copy-done.4, ...), custom_call_target="tpu_custom_call" | custom-call | flops 2000000000 | tf_op jit(solution)/shard_map/residual_back/pallas_call | solution.py:176
  169.6 4.5 %collective-permute-done.27.refs_8_.refs_2_ = bf16[128,1024]{1,0:T(8,128)(2,1)S(1)} collective-permute-done((bf16[128,1024]{1,0:T(8,128)(2,1)}, bf16[128,1024]{1,0:T(8,128)(2,1)S(1)}, u32[]{:S(2)}, u32[]{:S(2)}) %collective-permute-start.27) | collective-permute-done | bytes 262176 | tf_op jit(solution)/shard_map/ppermute | solution.py:557
  176.2 3.5 %collective-permute-done.25.refs_9_.refs_3_ = bf16[128,1024]{1,0:T(8,128)(2,1)S(1)} collective-permute-done((bf16[128,1024]{1,0:T(8,128)(2,1)}, bf16[128,1024]{1,0:T(8,128)(2,1)S(1)}, u32[]{:S(2)}, u32[]{:S(2)}) %collective-permute-start.25) | collective-permute-done | bytes 262176 | tf_op jit(solution)/shard_map/ppermute | solution.py:557
  181.3 9.3 %attend_back.1 = (bf16[768,128]{1,0:T(8,128)(2,1)}, f32[1024,128]{1,0:T(8,128)}, f32[1024,128]{1,0:T(8,128)}, f32[1024,128]{1,0:T(8,128)}) custom-call(bf16[1024,128]{1,0:T(8,128)(2,1)} %get-tuple-element.87.refs_0_, bf16[1024,128]{1,0:T(8,128)(2,1)} %get-tuple-element.88.refs_1_, s32[1024,8]{1,0:T(8,128)} %copy.45.refs_7_.refs_2_, s32[1,1024]{1,0:T(1,128)} %bitcast.49, ...), custom_call_target="tpu_custom_call" | custom-call | flops 46000001024 | tf_op jit(solution)/shard_map/attend_back/pallas_call | solution.py:176
  193.5 8.2 %attend_last.1 = (bf16[1024,384]{1,0:T(8,128)(2,1)}, bf16[1024,640]{1,0:T(8,128)(2,1)}) custom-call(bf16[1024,128]{1,0:T(8,128)(2,1)} %get-tuple-element.87.refs_0_, bf16[1024,128]{1,0:T(8,128)(2,1)} %get-tuple-element.88.refs_1_, s32[1024,8]{1,0:T(8,128)} %copy.45.refs_7_.refs_2_, s32[1,1024]{1,0:T(1,128)} %bitcast.50, ...), custom_call_target="tpu_custom_call" | custom-call | flops 46000001024 | tf_op jit(solution)/shard_map/attend_last/pallas_call | solution.py:176
  201.8 11.3 %reduce-scatter.3.cloned.1.call-done.refs_19_ = bf16[1,272,1024]{2,1,0:T(8,128)(2,1)} async-done(((bf16[8,272,1024]{2,1,0:T(8,128)(2,1)}), bf16[1,272,1024]{2,1,0:T(8,128)(2,1)}) %reduce-scatter.3.cloned.1.call-update) | async-done | bytes 557072 | tf_op jit(solution)/shard_map/reduce_scatter | solution.py:832
  213.1 9.5 %weights.1.refs_10_ = bf16[1024,1664]{1,0:T(8,128)(2,1)} custom-call(bf16[128,1024]{1,0:T(8,128)(2,1)} %get-tuple-element.97.refs_6_.refs_0_, bf16[128,1024]{1,0:T(8,128)(2,1)} %get-tuple-element.98.refs_7_.refs_1_, bf16[128,1024]{1,0:T(8,128)(2,1)} %copy-done.31, bf16[128,1024]{1,0:T(8,128)(2,1)} %copy-done.34, bf16[128,1024]{1,0:T(8,128)(2,1)} %copy-done.32, ...), custom_call_target="tpu_custom_call" | custom-call | flops 6000000000 | tf_op jit(solution)/shard_map/weights/pallas_call | solution.py:176
  223.6 2.4 collective-permute-start.17
  226.0 9.9 %input_back.1 = (bf16[256,1024]{1,0:T(8,128)(2,1)}, bf16[256,1024]{1,0:T(8,128)(2,1)}, bf16[256,1024]{1,0:T(8,128)(2,1)}, bf16[256,1024]{1,0:T(8,128)(2,1)}, f32[2,1024]{1,0:T(2,128)}) custom-call(bf16[256,1024]{1,0:T(8,128)(2,1)} %bitcast.refs_0_.refs_9_, bf16[256,1024]{1,0:T(8,128)(2,1)} %copy-done.9, bf16[256,1024]{1,0:T(8,128)(2,1)} %copy-done.8, ...), custom_call_target="tpu_custom_call" | custom-call | flops 6000000000 | tf_op jit(solution)/shard_map/input_back/pallas_call | solution.py:176
  236.8 2.7 collective-permute-start.31
  241.1 2.5 all-to-all-start
  243.6 2.4 finish_experts.1
  246.0 12.9 %all-to-all-done = f32[32,1,128]{2,1,0:T(1,128)S(1)} async-done(((f32[32,1,128]{2,1,0:T(1,128)}), f32[32,1,128]{2,1,0:T(1,128)S(1)}, u32[]{:S(2)}, u32[]{:S(2)}) %all-to-all-start) | async-done | bytes 16416 | tf_op jit(solution)/shard_map/all_to_all | solution.py:938
  262.0 2.9 %output.1 = bf16[256,1024]{1,0:T(8,128)(2,1)} custom-call(f32[256,1024]{1,0:T(8,128)} %get-tuple-element.74.refs_0_, bf16[256,1024]{1,0:T(8,128)(2,1)} %get-tuple-element.83.refs_6_.refs_15_.refs_1_, bf16[256,1024]{1,0:T(8,128)(2,1)} %copy-done.20, bf16[256,1024]{1,0:T(8,128)(2,1)} %copy-done.18, bf16[256,1024]{1,0:T(8,128)(2,1)} %copy-done.19, ...), custom_call_target="tpu_custom_call" | custom-call | flops 2000000000 | tf_op jit(solution)/shard_map/output/pallas_call | solution.py:176
  265.7 2.8 %token_grads.1 = bf16[256,1024]{1,0:T(8,128)(2,1)} custom-call(f32[256,1024]{1,0:T(8,128)} %get-tuple-element.112.refs_0_, bf16[256,1024]{1,0:T(8,128)(2,1)} %get-tuple-element.113.refs_1_, bf16[256,1024]{1,0:T(8,128)(2,1)} %copy-done.23, bf16[256,1024]{1,0:T(8,128)(2,1)} %copy-done.21, bf16[256,1024]{1,0:T(8,128)(2,1)} %copy-done.22), custom_call_target="tpu_custom_call" | custom-call | flops 2000000000 | tf_op jit(solution)/shard_map/token_grads/pallas_call | solution.py:176
  268.5 2.4 finish_weights.1
  (185 shorter events, 60.2 us)
Async XLA Ops:
  7.2 47.4 %all-gather.4.cloned.1.call-start = ((), (), s32[]{:S(2)}) async-start(), calls=%async_computation.3 | async-start | bytes 3833856 | tf_op jit(solution)/shard_map/all_gather | solution.py:694
  9.6 102.4 %all-gather.6.cloned.1.call-start = ((), (), s32[]{:S(2)}) async-start(), calls=%async_computation.6 | async-start | bytes 5013504 | tf_op jit(solution)/shard_map/all_gather | solution.py:731
  14.6 198.4 %reduce-scatter.3.cloned.1.call-start = ((), (), s32[]{:S(2)}) async-start(), calls=%async_computation.4 | async-start | bytes 5013504 | tf_op jit(solution)/shard_map/reduce_scatter | solution.py:832
  14.7 16.0 %collective-permute-start.1 = (bf16[256,1024]{1,0:T(8,128)(2,1)}, bf16[256,1024]{1,0:T(8,128)(2,1)S(1)}, u32[]{:S(2)}, u32[]{:S(2)}) collective-permute-start(bf16[256,1024]{1,0:T(8,128)(2,1)} %bitcast.refs_0_.refs_9_), channel_id=1, source_target_pairs={{0,16},{8,24},{16,0},{24,8},{1,17},{9,25},{17,1},{25,9},{2,18},{10... | collective-permute-start | bytes 1572872 | tf_op jit(solution)/shard_map/ppermute | solution.py:557
  17.7 15.1 %collective-permute-start = (bf16[256,1024]{1,0:T(8,128)(2,1)}, bf16[256,1024]{1,0:T(8,128)(2,1)S(1)}, u32[]{:S(2)}, u32[]{:S(2)}) collective-permute-start(bf16[256,1024]{1,0:T(8,128)(2,1)} %bitcast.refs_0_.refs_9_), channel_id=1, source_target_pairs={{0,8},{8,0},{16,24},{24,16},{1,9},{9,1},{17,25},{25,17},{2,10},{10... | collective-permute-start | bytes 1572872 | tf_op jit(solution)/shard_map/ppermute | solution.py:557
  19.2 23.4 %collective-permute-start.5 = (bf16[272,1024]{1,0:T(8,128)(2,1)}, bf16[272,1024]{1,0:T(8,128)(2,1)S(1)}, u32[]{:S(2)}, u32[]{:S(2)}) collective-permute-start(bf16[272,1024]{1,0:T(8,128)(2,1)} %pack_grad.1.refs_4_), channel_id=1, source_target_pairs={{0,16},{8,24},{16,0},{24,8},{1,17},{9,25},{17,1},{25,9},{2,18},{10... | collective-permute-start | bytes 1671176 | tf_op jit(solution)/shard_map/ppermute | solution.py:557
  19.7 25.0 %collective-permute-start.4 = (bf16[272,1024]{1,0:T(8,128)(2,1)}, bf16[272,1024]{1,0:T(8,128)(2,1)S(1)}, u32[]{:S(2)}, u32[]{:S(2)}) collective-permute-start(bf16[272,1024]{1,0:T(8,128)(2,1)} %pack_grad.1.refs_4_), channel_id=1, source_target_pairs={{0,8},{8,0},{16,24},{24,16},{1,9},{9,1},{17,25},{25,17},{2,10},{10... | collective-permute-start | bytes 1671176 | tf_op jit(solution)/shard_map/ppermute | solution.py:557
  30.7 19.7 %collective-permute-start.2 = (bf16[128,1024]{1,0:T(8,128)(2,1)S(1)}, bf16[128,1024]{1,0:T(8,128)(2,1)}, u32[]{:S(2)}, u32[]{:S(2)}) collective-permute-start(bf16[128,1024]{1,0:T(8,128)(2,1)S(1)} %slice.38), channel_id=1, source_target_pairs={{0,8},{8,0},{16,24},{24,16},{1,9},{9,1},{17,25},{25,17},{2,10},{10... | collective-permute-start | bytes 786440 | tf_op jit(solution)/shard_map/ppermute | solution.py:557
  32.8 17.6 %collective-permute-start.3 = (bf16[128,1024]{1,0:T(8,128)(2,1)S(1)}, bf16[128,1024]{1,0:T(8,128)(2,1)}, u32[]{:S(2)}, u32[]{:S(2)}) collective-permute-start(bf16[128,1024]{1,0:T(8,128)(2,1)S(1)} %slice.39), channel_id=1, source_target_pairs={{0,16},{8,24},{16,0},{24,8},{1,17},{9,25},{17,1},{25,9},{2,18},{10... | collective-permute-start | bytes 786440 | tf_op jit(solution)/shard_map/ppermute | solution.py:557
  42.6 11.9 %collective-permute-start.6 = (bf16[128,1024]{1,0:T(8,128)(2,1)S(1)}, bf16[128,1024]{1,0:T(8,128)(2,1)}, u32[]{:S(2)}, u32[]{:S(2)}) collective-permute-start(bf16[128,1024]{1,0:T(8,128)(2,1)S(1)} %slice.40), channel_id=1, source_target_pairs={{0,8},{8,0},{16,24},{24,16},{1,9},{9,1},{17,25},{25,17},{2,10},{10... | collective-permute-start | bytes 786440 | tf_op jit(solution)/shard_map/ppermute | solution.py:557
  70.8 16.1 %collective-permute-start.8 = (bf16[256,1024]{1,0:T(8,128)(2,1)}, bf16[256,1024]{1,0:T(8,128)(2,1)S(1)}, u32[]{:S(2)}, u32[]{:S(2)}) collective-permute-start(bf16[256,1024]{1,0:T(8,128)(2,1)} %get-tuple-element.71), channel_id=1, source_target_pairs={{0,24},{8,16},{16,8},{24,0},{1,25},{9,17},{17,9},{25,1},{2,26},{10... | collective-permute-start | bytes 1572872 | tf_op jit(solution)/shard_map/ppermute | solution.py:557
  72.7 22.9 %collective-permute-start.9 = (bf16[256,1024]{1,0:T(8,128)(2,1)}, bf16[256,1024]{1,0:T(8,128)(2,1)S(1)}, u32[]{:S(2)}, u32[]{:S(2)}) collective-permute-start(bf16[256,1024]{1,0:T(8,128)(2,1)} %get-tuple-element.72), channel_id=1, source_target_pairs={{0,8},{8,0},{16,24},{24,16},{1,9},{9,1},{17,25},{25,17},{2,10},{10... | collective-permute-start | bytes 1572872 | tf_op jit(solution)/shard_map/ppermute | solution.py:557
  73.2 22.5 %collective-permute-start.10 = (bf16[256,1024]{1,0:T(8,128)(2,1)}, bf16[256,1024]{1,0:T(8,128)(2,1)S(1)}, u32[]{:S(2)}, u32[]{:S(2)}) collective-permute-start(bf16[256,1024]{1,0:T(8,128)(2,1)} %get-tuple-element.73), channel_id=1, source_target_pairs={{0,16},{8,24},{16,0},{24,8},{1,17},{9,25},{17,1},{25,9},{2,18},{10... | collective-permute-start | bytes 1572872 | tf_op jit(solution)/shard_map/ppermute | solution.py:557
  105.1 15.0 %collective-permute-start.11 = (bf16[128,1024]{1,0:T(8,128)(2,1)}, bf16[128,1024]{1,0:T(8,128)(2,1)S(1)}, u32[]{:S(2)}, u32[]{:S(2)}) collective-permute-start(bf16[128,1024]{1,0:T(8,128)(2,1)} %get-tuple-element.75.refs_0_.refs_11_), channel_id=1, source_target_pairs={{0,8},{8,0},{16,24},{24,16},{1,9},{9,1},{17,25},{25,17},{2,10},{10... | collective-permute-start | bytes 786440 | tf_op jit(solution)/shard_map/ppermute | solution.py:557
  105.6 14.4 %collective-permute-start.14 = (bf16[128,1024]{1,0:T(8,128)(2,1)}, bf16[128,1024]{1,0:T(8,128)(2,1)S(1)}, u32[]{:S(2)}, u32[]{:S(2)}) collective-permute-start(bf16[128,1024]{1,0:T(8,128)(2,1)} %get-tuple-element.76.refs_1_.refs_12_), channel_id=1, source_target_pairs={{0,16},{8,24},{16,0},{24,8},{1,17},{9,25},{17,1},{25,9},{2,18},{10... | collective-permute-start | bytes 786440 | tf_op jit(solution)/shard_map/ppermute | solution.py:557
  108.9 24.6 %collective-permute-start.15 = (bf16[128,1024]{1,0:T(8,128)(2,1)S(1)}, bf16[128,1024]{1,0:T(8,128)(2,1)S(1)}, u32[]{:S(2)}, u32[]{:S(2)}) collective-permute-start(bf16[128,1024]{1,0:T(8,128)(2,1)S(1)} %collective-permute-done.13.refs_2_.refs_15_), channel_id=1, source_target_pairs={{0,8},{8,0},{16,24},{24,16},{1,9},{9,1},{17,25},{25,17},{2,10},{10... | collective-permute-start | bytes 786440 | tf_op jit(solution)/shard_map/ppermute | solution.py:557
  110.5 23.0 %collective-permute-start.16 = (bf16[128,1024]{1,0:T(8,128)(2,1)S(1)}, bf16[128,1024]{1,0:T(8,128)(2,1)S(1)}, u32[]{:S(2)}, u32[]{:S(2)}) collective-permute-start(bf16[128,1024]{1,0:T(8,128)(2,1)S(1)} %collective-permute-done.12.refs_1_.refs_14_), channel_id=1, source_target_pairs={{0,16},{8,24},{16,0},{24,8},{1,17},{9,25},{17,1},{25,9},{2,18},{10... | collective-permute-start | bytes 786440 | tf_op jit(solution)/shard_map/ppermute | solution.py:557
  131.4 28.8 %collective-permute-start.20 = (bf16[256,1024]{1,0:T(8,128)(2,1)}, bf16[256,1024]{1,0:T(8,128)(2,1)S(1)}, u32[]{:S(2)}, u32[]{:S(2)}) collective-permute-start(bf16[256,1024]{1,0:T(8,128)(2,1)} %get-tuple-element.80.refs_10_), channel_id=1, source_target_pairs={{0,8},{8,0},{16,24},{24,16},{1,9},{9,1},{17,25},{25,17},{2,10},{10... | collective-permute-start | bytes 1572872 | tf_op jit(solution)/shard_map/ppermute | solution.py:557
  132.3 27.9 %collective-permute-start.21 = (bf16[256,1024]{1,0:T(8,128)(2,1)}, bf16[256,1024]{1,0:T(8,128)(2,1)S(1)}, u32[]{:S(2)}, u32[]{:S(2)}) collective-permute-start(bf16[256,1024]{1,0:T(8,128)(2,1)} %get-tuple-element.81.refs_11_), channel_id=1, source_target_pairs={{0,16},{8,24},{16,0},{24,8},{1,17},{9,25},{17,1},{25,9},{2,18},{10... | collective-permute-start | bytes 1572872 | tf_op jit(solution)/shard_map/ppermute | solution.py:557
  141.5 18.8 %collective-permute-start.22 = (bf16[256,1024]{1,0:T(8,128)(2,1)}, bf16[256,1024]{1,0:T(8,128)(2,1)S(1)}, u32[]{:S(2)}, u32[]{:S(2)}) collective-permute-start(bf16[256,1024]{1,0:T(8,128)(2,1)} %get-tuple-element.90), channel_id=1, source_target_pairs={{0,24},{8,16},{16,8},{24,0},{1,25},{9,17},{17,9},{25,1},{2,26},{10... | collective-permute-start | bytes 1572872 | tf_op jit(solution)/shard_map/ppermute | solution.py:557
  160.1 108.4 %reduce-scatter.5.cloned.1.call-start = ((), (), s32[]{:S(2)}) async-start(), calls=%async_computation.5 | async-start | bytes 3833856 | tf_op jit(solution)/shard_map/reduce_scatter | solution.py:922
  166.7 13.0 %collective-permute-start.25 = (bf16[128,1024]{1,0:T(8,128)(2,1)}, bf16[128,1024]{1,0:T(8,128)(2,1)S(1)}, u32[]{:S(2)}, u32[]{:S(2)}) collective-permute-start(bf16[128,1024]{1,0:T(8,128)(2,1)} %get-tuple-element.98.refs_7_.refs_1_), channel_id=1, source_target_pairs={{0,8},{8,0},{16,24},{24,16},{1,9},{9,1},{17,25},{25,17},{2,10},{10... | collective-permute-start | bytes 786440 | tf_op jit(solution)/shard_map/ppermute | solution.py:557
  167.2 13.3 %collective-permute-start.28 = (bf16[128,1024]{1,0:T(8,128)(2,1)}, bf16[128,1024]{1,0:T(8,128)(2,1)S(1)}, u32[]{:S(2)}, u32[]{:S(2)}) collective-permute-start(bf16[128,1024]{1,0:T(8,128)(2,1)} %get-tuple-element.98.refs_7_.refs_1_), channel_id=1, source_target_pairs={{0,16},{8,24},{16,0},{24,8},{1,17},{9,25},{17,1},{25,9},{2,18},{10... | collective-permute-start | bytes 786440 | tf_op jit(solution)/shard_map/ppermute | solution.py:557
  168.7 33.0 %collective-permute-start.18 = (bf16[256,1024]{1,0:T(8,128)(2,1)S(1)}, bf16[256,1024]{1,0:T(8,128)(2,1)S(1)}, u32[]{:S(2)}, u32[]{:S(2)}) collective-permute-start(bf16[256,1024]{1,0:T(8,128)(2,1)S(1)} %copy-done.2), channel_id=1, source_target_pairs={{0,8},{8,0},{16,24},{24,16},{1,9},{9,1},{17,25},{25,17},{2,10},{10... | collective-permute-start | bytes 1572872 | tf_op jit(solution)/shard_map/ppermute | solution.py:557
  174.1 27.6 %collective-permute-start.19 = (bf16[256,1024]{1,0:T(8,128)(2,1)S(1)}, bf16[256,1024]{1,0:T(8,128)(2,1)S(1)}, u32[]{:S(2)}, u32[]{:S(2)}) collective-permute-start(bf16[256,1024]{1,0:T(8,128)(2,1)S(1)} %copy-done.1), channel_id=1, source_target_pairs={{0,16},{8,24},{16,0},{24,8},{1,17},{9,25},{17,1},{25,9},{2,18},{10... | collective-permute-start | bytes 1572872 | tf_op jit(solution)/shard_map/ppermute | solution.py:557
  175.0 17.5 %collective-permute-start.24 = (bf16[128,1024]{1,0:T(8,128)(2,1)S(1)}, bf16[128,1024]{1,0:T(8,128)(2,1)S(1)}, u32[]{:S(2)}, u32[]{:S(2)}) collective-permute-start(bf16[128,1024]{1,0:T(8,128)(2,1)S(1)} %collective-permute-done.23.refs_10_.refs_4_), channel_id=1, source_target_pairs={{0,8},{8,0},{16,24},{24,16},{1,9},{9,1},{17,25},{25,17},{2,10},{10... | collective-permute-start | bytes 786440 | tf_op jit(solution)/shard_map/ppermute | solution.py:557
  179.7 13.0 %collective-permute-start.26 = (bf16[128,1024]{1,0:T(8,128)(2,1)S(1)}, bf16[128,1024]{1,0:T(8,128)(2,1)S(1)}, u32[]{:S(2)}, u32[]{:S(2)}) collective-permute-start(bf16[128,1024]{1,0:T(8,128)(2,1)S(1)} %collective-permute-done.25.refs_9_.refs_3_), channel_id=1, source_target_pairs={{0,16},{8,24},{16,0},{24,8},{1,17},{9,25},{17,1},{25,9},{2,18},{10... | collective-permute-start | bytes 786440 | tf_op jit(solution)/shard_map/ppermute | solution.py:557
  223.6 37.2 %collective-permute-start.17 = (bf16[256,1024]{1,0:T(8,128)(2,1)S(1)}, bf16[256,1024]{1,0:T(8,128)(2,1)S(1)}, u32[]{:S(2)}, u32[]{:S(2)}) collective-permute-start(bf16[256,1024]{1,0:T(8,128)(2,1)S(1)} %copy-done), channel_id=1, source_target_pairs={{0,24},{8,16},{16,8},{24,0},{1,25},{9,17},{17,9},{25,1},{2,26},{10... | collective-permute-start | bytes 1572872 | tf_op jit(solution)/shard_map/ppermute | solution.py:557
  235.9 24.9 %collective-permute-start.29 = (bf16[256,1024]{1,0:T(8,128)(2,1)}, bf16[256,1024]{1,0:T(8,128)(2,1)S(1)}, u32[]{:S(2)}, u32[]{:S(2)}) collective-permute-start(bf16[256,1024]{1,0:T(8,128)(2,1)} %get-tuple-element.110), channel_id=1, source_target_pairs={{0,8},{8,0},{16,24},{24,16},{1,9},{9,1},{17,25},{25,17},{2,10},{10... | collective-permute-start | bytes 1572872 | tf_op jit(solution)/shard_map/ppermute | solution.py:557
  236.6 24.3 %collective-permute-start.30 = (bf16[256,1024]{1,0:T(8,128)(2,1)}, bf16[256,1024]{1,0:T(8,128)(2,1)S(1)}, u32[]{:S(2)}, u32[]{:S(2)}) collective-permute-start(bf16[256,1024]{1,0:T(8,128)(2,1)} %get-tuple-element.111), channel_id=1, source_target_pairs={{0,16},{8,24},{16,0},{24,8},{1,17},{9,25},{17,1},{25,9},{2,18},{10... | collective-permute-start | bytes 1572872 | tf_op jit(solution)/shard_map/ppermute | solution.py:557
  236.8 28.0 %collective-permute-start.31 = (bf16[256,1024]{1,0:T(8,128)(2,1)}, bf16[256,1024]{1,0:T(8,128)(2,1)S(1)}, u32[]{:S(2)}, u32[]{:S(2)}) collective-permute-start(bf16[256,1024]{1,0:T(8,128)(2,1)} %get-tuple-element.114), channel_id=1, source_target_pairs={{0,24},{8,16},{16,8},{24,0},{1,25},{9,17},{17,9},{25,1},{2,26},{10... | collective-permute-start | bytes 1572872 | tf_op jit(solution)/shard_map/ppermute | solution.py:557
  241.1 17.8 %all-to-all-start = ((f32[32,1,128]{2,1,0:T(1,128)}), f32[32,1,128]{2,1,0:T(1,128)S(1)}, u32[]{:S(2)}, u32[]{:S(2)}) async-start(f32[32,1,128]{2,1,0:T(1,128)} %reshape.74), calls=%async_computation.1 | async-start | bytes 32768 | tf_op jit(solution)/shard_map/all_to_all | solution.py:938
  (46 other events, 281.2 us)
Sparse Core Ops, SparseCore 0:
  10.2 43.1 all-gather.3
  55.0 48.3 all-gather.5
  160.3 52.7 reduce-scatter.2
  222.7 40.9 reduce-scatter.4
